TPU v7x, 256 devices: a whole 4x4x8 slice. The times are simulated.
256 devices in a mesh: loop: 64 (over x_lo, z, y), team: 4 (over x_hi, core).
Axes of the slice: x: 4 (x_hi: 2, x_lo: 2; x = x_hi * 2 + x_lo), y: 4, z: 8, core: 2. Of those that a mesh axis runs over, the one named last changes fastest.
Arguments:
- samples: bfloat16 [4096, 11776], P(('loop', 'team')), may hold values from -6 to 6
- input_gains: float32 [2, 4096, 4, 128], P(None, 'loop', None, 'team'), may hold values from -5 to 5
Outputs:
- visibility: float32 [64, 4, 2, 256, 4096], P('loop', 'team')
All inputs are finite; a program needn't handle non-finite values.
Results may differ from a plain program's by a relative error of at most 0.0038.
Values may be sent and summed in bfloat16 or wider, within the bound.
No kernel may reach another device: no remote copies, remote signals or barrier semaphores. Data moves between devices by JAX's collectives and lax.ppermute only.
A program may use at most 64 MiB of HBM per device.

v0:
```python
import math

import jax
import jax.numpy as jnp
from jax import lax
from jax.sharding import PartitionSpec as P

FCH = 512
TAPS = 8
AVG = 32
SPEC = 16


def shifted(array, axis, by):
    count = lax.axis_size(axis)
    pairs = [(i, i + by) for i in range(count) if 0 <= i + by < count]
    return lax.ppermute(array, axis, pairs)


def from_behind(block, axis, distance):
    devices = range(lax.axis_size(axis))
    route = [((i - distance) % len(devices), i) for i in devices]
    return lax.ppermute(block, axis, route)


def pfb_window():
    sample_pos = jnp.arange(TAPS * FCH, dtype=jnp.float32) + 0.5
    taper = jnp.sin(jnp.pi * sample_pos / (TAPS * FCH)) ** 2
    taps_table = jnp.sinc(sample_pos / FCH - TAPS / 2) * taper
    return taps_table.reshape(TAPS, FCH)


def filter_bank(raw_rows, channel_index):
    rows_here = raw_rows.shape[0]
    frames = raw_rows.astype(jnp.float32).reshape(rows_here, SPEC + TAPS - 1, FCH)
    window = pfb_window()
    filtered = window[0] * frames[:, 0:SPEC, :]
    for tap_index in range(1, TAPS):
        filtered = filtered + window[tap_index] * frames[:, tap_index : tap_index + SPEC, :]
    channel_flat = channel_index.reshape(channel_index.shape[0], -1)
    positions = jnp.arange(FCH, dtype=jnp.int32)
    angles_table = (positions[:, None, None] * channel_flat[None] % FCH).astype(jnp.float32) * (
        2.0 * math.pi / FCH
    )
    dft_table = jnp.concatenate(
        [jnp.cos(angles_table), -jnp.sin(angles_table)], axis=2
    ) / math.sqrt(FCH)
    return jnp.einsum(
        "itp,pmc->imtc",
        filtered,
        dft_table,
        precision=lax.Precision.HIGHEST,
        preferred_element_type=jnp.float32,
    )


def apply_gains(spectra, gain_rows):
    rows_here = spectra.shape[0]
    bin_groups = gain_rows.shape[2]
    shaped = spectra.reshape(rows_here, SPEC, 2, bin_groups, AVG)
    real_part = shaped[:, :, 0]
    imag_part = shaped[:, :, 1]
    gain_re = gain_rows[0][:, None]
    gain_im = gain_rows[1][:, None]
    volt_re = (gain_re * real_part - gain_im * imag_part).astype(jnp.bfloat16)
    volt_im = (gain_re * imag_part + gain_im * real_part).astype(jnp.bfloat16)
    stacked = jnp.stack([volt_re, volt_im], axis=1)
    return stacked.transpose(3, 0, 1, 2, 4).reshape(bin_groups, rows_here, 2 * SPEC * AVG)


def local(samples, input_gains):
    member = lax.axis_index("team")
    team_size = lax.axis_size("team")
    loop_size = lax.axis_size("loop")
    loop_place = lax.axis_index("loop")
    team_rows = input_gains.shape[1]
    bin_groups = input_gains.shape[2]
    group_count = loop_size // bin_groups
    bin_slot = loop_place % bin_groups
    row_group = loop_place // bin_groups
    bin_range = jnp.arange(bin_groups, dtype=jnp.int32)
    avg_range = jnp.arange(AVG, dtype=jnp.int32)
    own_channels = (bin_range[:, None] * team_size + member) * AVG + avg_range[None, :]
    spectra = filter_bank(lax.all_gather(samples, "team", axis=0, tiled=True), own_channels[None])[
        :, 0
    ]
    packed_all = apply_gains(spectra, input_gains)
    width_k = packed_all.shape[2]
    own_part = lax.dynamic_index_in_dim(packed_all, bin_slot, 0, keepdims=False)
    gathered = jnp.zeros((bin_groups, team_rows, width_k), jnp.bfloat16)
    gathered = lax.dynamic_update_index_in_dim(gathered, own_part, bin_slot, 0)
    offsets = [value for value in range(1 - bin_groups, bin_groups) if value != 0]
    for row_offset in offsets:
        send_slot = jnp.clip(bin_slot + row_offset, 0, bin_groups - 1)
        outgoing = lax.dynamic_index_in_dim(packed_all, send_slot, 0, keepdims=False)
        incoming = shifted(outgoing, "loop", row_offset)
        anchor_slot = bin_slot - row_offset
        from_group = (anchor_slot >= 0) & (anchor_slot < bin_groups)
        store_slot = jnp.clip(anchor_slot, 0, bin_groups - 1)
        kept_rows = lax.dynamic_index_in_dim(gathered, store_slot, 0, keepdims=False)
        gathered = lax.dynamic_update_index_in_dim(
            gathered, jnp.where(from_group, incoming, kept_rows), store_slot, 0
        )
    rows_block = gathered.reshape(bin_groups * team_rows, width_k)
    width_rows = rows_block.shape[0]
    half_width = width_k // 2
    rotated = jnp.concatenate([rows_block[:, half_width:], -rows_block[:, :half_width]], axis=1)
    local_pair = jnp.stack([rows_block, rotated])
    norm_scale = 1.0 / (AVG * SPEC)
    nought = jnp.zeros((), jnp.int32)

    def place_tile(tile_state, partner, source_group):
        tile_values = (
            jnp.einsum("crk,pk->crp", local_pair, partner, preferred_element_type=jnp.float32)
            * norm_scale
        )
        start_col = source_group * width_rows
        return lax.dynamic_update_slice(tile_state, tile_values, (nought, nought, start_col))

    visibility = jnp.zeros((2, width_rows, width_rows * group_count), jnp.float32)
    visibility = place_tile(visibility, rows_block, row_group)

    def visit(visit_index, carry):
        partner, tile_state = carry
        partner = from_behind(partner, "loop", bin_groups)
        return (partner, place_tile(tile_state, partner, (row_group - visit_index) % group_count))

    partner, visibility = lax.fori_loop(1, group_count, visit, (rows_block, visibility))
    return visibility[None, None]


def solution(mesh):
    placed = (P(("loop", "team"), None), P(None, "loop", None, "team"))
    return jax.shard_map(
        local,
        mesh=mesh,
        in_specs=placed,
        out_specs=P("loop", "team", None, None, None),
        check_vma=False,
    )
```

profile of v0, /device:TPU:6, one launch (start us, length us, event | category | flops | bytes accessed | tf_op | source)
XLA Modules:
  0.0 314.2 jit_solution(12989422514897380619)
XLA Ops:
  10.9 25.6 %all-gather.2.cloned.1.call-done = bf16[64,11776]{1,0:T(8,128)(2,1)} async-done(((bf16[16,11776]{1,0:T(8,128)(2,1)}), bf16[64,11776]{1,0:T(8,128)(2,1)}) %all-gather.2.cloned.1.call-update) | async-done | bytes 1507344 | tf_op jit(solution)/shard_map/all_gather | solution.py:84
  39.2 2.8 fusion.2
  47.0 5.5 %collective-permute-start.1 = (bf16[64,1024]{1,0:T(8,128)(2,1)S(1)}, bf16[64,1024]{1,0:T(8,128)(2,1)S(1)}, u32[]{:S(2)}, u32[]{:S(2)}) collective-permute-start(bf16[64,1024]{1,0:T(8,128)(2,1)S(1)} %bitcast.99), channel_id=1, source_target_pairs={{12,0},{16,4},{20,8},{24,12},{28,16},{32,20},{36,24},{40,28},{44,3... | collective-permute-start | bytes 393224 | tf_op jit(solution)/shard_map/ppermute | solution.py:17
  52.5 5.4 %collective-permute-start.2 = (bf16[64,1024]{1,0:T(8,128)(2,1)S(1)}, bf16[64,1024]{1,0:T(8,128)(2,1)S(1)}, u32[]{:S(2)}, u32[]{:S(2)}) collective-permute-start(bf16[64,1024]{1,0:T(8,128)(2,1)S(1)} %bitcast.98), channel_id=1, source_target_pairs={{8,0},{12,4},{16,8},{20,12},{24,16},{28,20},{32,24},{36,28},{40,32... | collective-permute-start | bytes 393224 | tf_op jit(solution)/shard_map/ppermute | solution.py:17
  58.0 3.3 %collective-permute-start.3 = (bf16[64,1024]{1,0:T(8,128)(2,1)S(1)}, bf16[64,1024]{1,0:T(8,128)(2,1)S(1)}, u32[]{:S(2)}, u32[]{:S(2)}) collective-permute-start(bf16[64,1024]{1,0:T(8,128)(2,1)S(1)} %bitcast.97), channel_id=1, source_target_pairs={{4,0},{8,4},{12,8},{16,12},{20,16},{24,20},{28,24},{32,28},{36,32}... | collective-permute-start | bytes 393224 | tf_op jit(solution)/shard_map/ppermute | solution.py:17
  66.0 4.6 %collective-permute-start.6 = (bf16[64,1024]{1,0:T(8,128)(2,1)S(1)}, bf16[64,1024]{1,0:T(8,128)(2,1)S(1)}, u32[]{:S(2)}, u32[]{:S(2)}) collective-permute-start(bf16[64,1024]{1,0:T(8,128)(2,1)S(1)} %bitcast.94), channel_id=1, source_target_pairs={{0,12},{4,16},{8,20},{12,24},{16,28},{20,32},{24,36},{28,40},{32,4... | collective-permute-start | bytes 393224 | tf_op jit(solution)/shard_map/ppermute | solution.py:17
  70.8 3.2 %collective-permute-done.4 = bf16[64,1024]{1,0:T(8,128)(2,1)S(1)} collective-permute-done((bf16[64,1024]{1,0:T(8,128)(2,1)S(1)}, bf16[64,1024]{1,0:T(8,128)(2,1)S(1)}, u32[]{:S(2)}, u32[]{:S(2)}) %collective-permute-start.4) | collective-permute-done | bytes 131104 | tf_op jit(solution)/shard_map/ppermute | solution.py:17
  79.1 3.4 %copy-done = f32[2,256,4096]{2,1,0:T(8,128)} copy-done((f32[2,256,4096]{2,1,0:T(8,128)}, f32[2,256,4096]{2,1,0:T(8,128)S(1)}, u32[]{:S(2)}) %copy-start) | copy-done | bytes 8388632
  82.5 224.9 %while.17 = (s32[]{:T(128)}, bf16[256,1024]{1,0:T(8,128)(2,1)S(1)}, f32[2,256,4096]{2,1,0:T(8,128)}, bf16[2,256,1024]{2,1,0:T(8,128)(2,1)S(1)}, s32[]{:T(128)}, ...) while((s32[]{:T(128)}, bf16[256,1024]{1,0:T(8,128)(2,1)S(1)}, ...), condition=%wide.region_1.2_spmd, body=%wide.region_0.1_spmd.sunk | while | flops 268566560 | bytes 5243200 | solution.py:128
  82.5 14.1 %collective-permute-done = bf16[256,1024]{1,0:T(8,128)(2,1)S(1)} collective-permute-done((bf16[256,1024]{1,0:T(8,128)(2,1)S(1)}, bf16[256,1024]{1,0:T(8,128)(2,1)S(1)}, u32[]{:S(2)}, u32[]{:S(2)}) %collective-permute-start) | collective-permute-done | bytes 524320 | tf_op jit(solution)/shard_map/while/body/eval_jaxpr/ppermute | solution.py:23
  97.9 13.1 %collective-permute-done = bf16[256,1024]{1,0:T(8,128)(2,1)S(1)} collective-permute-done((bf16[256,1024]{1,0:T(8,128)(2,1)S(1)}, bf16[256,1024]{1,0:T(8,128)(2,1)S(1)}, u32[]{:S(2)}, u32[]{:S(2)}) %collective-permute-start) | collective-permute-done | bytes 524320 | tf_op jit(solution)/shard_map/while/body/eval_jaxpr/ppermute | solution.py:23
  112.3 12.2 %collective-permute-done = bf16[256,1024]{1,0:T(8,128)(2,1)S(1)} collective-permute-done((bf16[256,1024]{1,0:T(8,128)(2,1)S(1)}, bf16[256,1024]{1,0:T(8,128)(2,1)S(1)}, u32[]{:S(2)}, u32[]{:S(2)}) %collective-permute-start) | collective-permute-done | bytes 524320 | tf_op jit(solution)/shard_map/while/body/eval_jaxpr/ppermute | solution.py:23
  125.9 11.3 %collective-permute-done = bf16[256,1024]{1,0:T(8,128)(2,1)S(1)} collective-permute-done((bf16[256,1024]{1,0:T(8,128)(2,1)S(1)}, bf16[256,1024]{1,0:T(8,128)(2,1)S(1)}, u32[]{:S(2)}, u32[]{:S(2)}) %collective-permute-start) | collective-permute-done | bytes 524320 | tf_op jit(solution)/shard_map/while/body/eval_jaxpr/ppermute | solution.py:23
  138.5 12.1 %collective-permute-done = bf16[256,1024]{1,0:T(8,128)(2,1)S(1)} collective-permute-done((bf16[256,1024]{1,0:T(8,128)(2,1)S(1)}, bf16[256,1024]{1,0:T(8,128)(2,1)S(1)}, u32[]{:S(2)}, u32[]{:S(2)}) %collective-permute-start) | collective-permute-done | bytes 524320 | tf_op jit(solution)/shard_map/while/body/eval_jaxpr/ppermute | solution.py:23
  152.0 13.2 %collective-permute-done = bf16[256,1024]{1,0:T(8,128)(2,1)S(1)} collective-permute-done((bf16[256,1024]{1,0:T(8,128)(2,1)S(1)}, bf16[256,1024]{1,0:T(8,128)(2,1)S(1)}, u32[]{:S(2)}, u32[]{:S(2)}) %collective-permute-start) | collective-permute-done | bytes 524320 | tf_op jit(solution)/shard_map/while/body/eval_jaxpr/ppermute | solution.py:23
  166.5 14.3 %collective-permute-done = bf16[256,1024]{1,0:T(8,128)(2,1)S(1)} collective-permute-done((bf16[256,1024]{1,0:T(8,128)(2,1)S(1)}, bf16[256,1024]{1,0:T(8,128)(2,1)S(1)}, u32[]{:S(2)}, u32[]{:S(2)}) %collective-permute-start) | collective-permute-done | bytes 524320 | tf_op jit(solution)/shard_map/while/body/eval_jaxpr/ppermute | solution.py:23
  182.1 15.4 %collective-permute-done = bf16[256,1024]{1,0:T(8,128)(2,1)S(1)} collective-permute-done((bf16[256,1024]{1,0:T(8,128)(2,1)S(1)}, bf16[256,1024]{1,0:T(8,128)(2,1)S(1)}, u32[]{:S(2)}, u32[]{:S(2)}) %collective-permute-start) | collective-permute-done | bytes 524320 | tf_op jit(solution)/shard_map/while/body/eval_jaxpr/ppermute | solution.py:23
  198.8 16.6 %collective-permute-done = bf16[256,1024]{1,0:T(8,128)(2,1)S(1)} collective-permute-done((bf16[256,1024]{1,0:T(8,128)(2,1)S(1)}, bf16[256,1024]{1,0:T(8,128)(2,1)S(1)}, u32[]{:S(2)}, u32[]{:S(2)}) %collective-permute-start) | collective-permute-done | bytes 524320 | tf_op jit(solution)/shard_map/while/body/eval_jaxpr/ppermute | solution.py:23
  216.8 16.1 %collective-permute-done = bf16[256,1024]{1,0:T(8,128)(2,1)S(1)} collective-permute-done((bf16[256,1024]{1,0:T(8,128)(2,1)S(1)}, bf16[256,1024]{1,0:T(8,128)(2,1)S(1)}, u32[]{:S(2)}, u32[]{:S(2)}) %collective-permute-start) | collective-permute-done | bytes 524320 | tf_op jit(solution)/shard_map/while/body/eval_jaxpr/ppermute | solution.py:23
  234.1 15.2 %collective-permute-done = bf16[256,1024]{1,0:T(8,128)(2,1)S(1)} collective-permute-done((bf16[256,1024]{1,0:T(8,128)(2,1)S(1)}, bf16[256,1024]{1,0:T(8,128)(2,1)S(1)}, u32[]{:S(2)}, u32[]{:S(2)}) %collective-permute-start) | collective-permute-done | bytes 524320 | tf_op jit(solution)/shard_map/while/body/eval_jaxpr/ppermute | solution.py:23
  250.7 14.3 %collective-permute-done = bf16[256,1024]{1,0:T(8,128)(2,1)S(1)} collective-permute-done((bf16[256,1024]{1,0:T(8,128)(2,1)S(1)}, bf16[256,1024]{1,0:T(8,128)(2,1)S(1)}, u32[]{:S(2)}, u32[]{:S(2)}) %collective-permute-start) | collective-permute-done | bytes 524320 | tf_op jit(solution)/shard_map/while/body/eval_jaxpr/ppermute | solution.py:23
  266.3 13.4 %collective-permute-done = bf16[256,1024]{1,0:T(8,128)(2,1)S(1)} collective-permute-done((bf16[256,1024]{1,0:T(8,128)(2,1)S(1)}, bf16[256,1024]{1,0:T(8,128)(2,1)S(1)}, u32[]{:S(2)}, u32[]{:S(2)}) %collective-permute-start) | collective-permute-done | bytes 524320 | tf_op jit(solution)/shard_map/while/body/eval_jaxpr/ppermute | solution.py:23
  281.0 12.4 %collective-permute-done = bf16[256,1024]{1,0:T(8,128)(2,1)S(1)} collective-permute-done((bf16[256,1024]{1,0:T(8,128)(2,1)S(1)}, bf16[256,1024]{1,0:T(8,128)(2,1)S(1)}, u32[]{:S(2)}, u32[]{:S(2)}) %collective-permute-start) | collective-permute-done | bytes 524320 | tf_op jit(solution)/shard_map/while/body/eval_jaxpr/ppermute | solution.py:23
  294.7 11.3 %collective-permute-done = bf16[256,1024]{1,0:T(8,128)(2,1)S(1)} collective-permute-done((bf16[256,1024]{1,0:T(8,128)(2,1)S(1)}, bf16[256,1024]{1,0:T(8,128)(2,1)S(1)}, u32[]{:S(2)}, u32[]{:S(2)}) %collective-permute-start) | collective-permute-done | bytes 524320 | tf_op jit(solution)/shard_map/while/body/eval_jaxpr/ppermute | solution.py:23
  (97 shorter events, 41.4 us)
Async XLA Ops:
  6.5 29.9 %all-gather.2.cloned.1.call-start = ((), (), s32[]{:S(2)}) async-start(), calls=%async_computation | async-start | bytes 1884160 | tf_op jit(solution)/shard_map/all_gather | solution.py:84
  39.1 2.8 copy-start.1
  47.0 19.0 %collective-permute-start.1 = (bf16[64,1024]{1,0:T(8,128)(2,1)S(1)}, bf16[64,1024]{1,0:T(8,128)(2,1)S(1)}, u32[]{:S(2)}, u32[]{:S(2)}) collective-permute-start(bf16[64,1024]{1,0:T(8,128)(2,1)S(1)} %bitcast.99), channel_id=1, source_target_pairs={{12,0},{16,4},{20,8},{24,12},{28,16},{32,20},{36,24},{40,28},{44,3... | collective-permute-start | bytes 393224 | tf_op jit(solution)/shard_map/ppermute | solution.py:17
  52.5 18.1 %collective-permute-start.2 = (bf16[64,1024]{1,0:T(8,128)(2,1)S(1)}, bf16[64,1024]{1,0:T(8,128)(2,1)S(1)}, u32[]{:S(2)}, u32[]{:S(2)}) collective-permute-start(bf16[64,1024]{1,0:T(8,128)(2,1)S(1)} %bitcast.98), channel_id=1, source_target_pairs={{8,0},{12,4},{16,8},{20,12},{24,16},{28,20},{32,24},{36,28},{40,32... | collective-permute-start | bytes 393224 | tf_op jit(solution)/shard_map/ppermute | solution.py:17
  58.0 12.7 %collective-permute-start.3 = (bf16[64,1024]{1,0:T(8,128)(2,1)S(1)}, bf16[64,1024]{1,0:T(8,128)(2,1)S(1)}, u32[]{:S(2)}, u32[]{:S(2)}) collective-permute-start(bf16[64,1024]{1,0:T(8,128)(2,1)S(1)} %bitcast.97), channel_id=1, source_target_pairs={{4,0},{8,4},{12,8},{16,12},{20,16},{24,20},{28,24},{32,28},{36,32}... | collective-permute-start | bytes 393224 | tf_op jit(solution)/shard_map/ppermute | solution.py:17
  61.3 12.7 %collective-permute-start.4 = (bf16[64,1024]{1,0:T(8,128)(2,1)S(1)}, bf16[64,1024]{1,0:T(8,128)(2,1)S(1)}, u32[]{:S(2)}, u32[]{:S(2)}) collective-permute-start(bf16[64,1024]{1,0:T(8,128)(2,1)S(1)} %bitcast.96), channel_id=1, source_target_pairs={{0,4},{4,8},{8,12},{12,16},{16,20},{20,24},{24,28},{28,32},{32,36}... | collective-permute-start | bytes 393224 | tf_op jit(solution)/shard_map/ppermute | solution.py:17
  64.0 11.6 %collective-permute-start.5 = (bf16[64,1024]{1,0:T(8,128)(2,1)S(1)}, bf16[64,1024]{1,0:T(8,128)(2,1)S(1)}, u32[]{:S(2)}, u32[]{:S(2)}) collective-permute-start(bf16[64,1024]{1,0:T(8,128)(2,1)S(1)} %bitcast.95), channel_id=1, source_target_pairs={{0,8},{4,12},{8,16},{12,20},{16,24},{20,28},{24,32},{28,36},{32,40... | collective-permute-start | bytes 393224 | tf_op jit(solution)/shard_map/ppermute | solution.py:17
  66.0 11.3 %collective-permute-start.6 = (bf16[64,1024]{1,0:T(8,128)(2,1)S(1)}, bf16[64,1024]{1,0:T(8,128)(2,1)S(1)}, u32[]{:S(2)}, u32[]{:S(2)}) collective-permute-start(bf16[64,1024]{1,0:T(8,128)(2,1)S(1)} %bitcast.94), channel_id=1, source_target_pairs={{0,12},{4,16},{8,20},{12,24},{16,28},{20,32},{24,36},{28,40},{32,4... | collective-permute-start | bytes 393224 | tf_op jit(solution)/shard_map/ppermute | solution.py:17
  79.1 3.4 %copy-start = (f32[2,256,4096]{2,1,0:T(8,128)}, f32[2,256,4096]{2,1,0:T(8,128)S(1)}, u32[]{:S(2)}) copy-start(f32[2,256,4096]{2,1,0:T(8,128)S(1)} %fusion.14) | copy-start | bytes 25165828
  82.5 14.1 %collective-permute-start = (bf16[256,1024]{1,0:T(8,128)(2,1)S(1)}, bf16[256,1024]{1,0:T(8,128)(2,1)S(1)}, u32[]{:S(2)}, u32[]{:S(2)}) collective-permute-start(bf16[256,1024]{1,0:T(8,128)(2,1)S(1)} %get-tuple-element.215), channel_id=1, source_target_pairs={{240,0},{244,4},{248,8},{252,12},{0,16},{4,20},{8,24},{12,28},{16,... | collective-permute-start | bytes 1572872 | tf_op jit(solution)/shard_map/while/body/eval_jaxpr/ppermute | solution.py:23
  97.9 13.1 %collective-permute-start = (bf16[256,1024]{1,0:T(8,128)(2,1)S(1)}, bf16[256,1024]{1,0:T(8,128)(2,1)S(1)}, u32[]{:S(2)}, u32[]{:S(2)}) collective-permute-start(bf16[256,1024]{1,0:T(8,128)(2,1)S(1)} %get-tuple-element.215), channel_id=1, source_target_pairs={{240,0},{244,4},{248,8},{252,12},{0,16},{4,20},{8,24},{12,28},{16,... | collective-permute-start | bytes 1572872 | tf_op jit(solution)/shard_map/while/body/eval_jaxpr/ppermute | solution.py:23
  112.3 12.2 %collective-permute-start = (bf16[256,1024]{1,0:T(8,128)(2,1)S(1)}, bf16[256,1024]{1,0:T(8,128)(2,1)S(1)}, u32[]{:S(2)}, u32[]{:S(2)}) collective-permute-start(bf16[256,1024]{1,0:T(8,128)(2,1)S(1)} %get-tuple-element.215), channel_id=1, source_target_pairs={{240,0},{244,4},{248,8},{252,12},{0,16},{4,20},{8,24},{12,28},{16,... | collective-permute-start | bytes 1572872 | tf_op jit(solution)/shard_map/while/body/eval_jaxpr/ppermute | solution.py:23
  125.9 11.3 %collective-permute-start = (bf16[256,1024]{1,0:T(8,128)(2,1)S(1)}, bf16[256,1024]{1,0:T(8,128)(2,1)S(1)}, u32[]{:S(2)}, u32[]{:S(2)}) collective-permute-start(bf16[256,1024]{1,0:T(8,128)(2,1)S(1)} %get-tuple-element.215), channel_id=1, source_target_pairs={{240,0},{244,4},{248,8},{252,12},{0,16},{4,20},{8,24},{12,28},{16,... | collective-permute-start | bytes 1572872 | tf_op jit(solution)/shard_map/while/body/eval_jaxpr/ppermute | solution.py:23
  138.5 12.1 %collective-permute-start = (bf16[256,1024]{1,0:T(8,128)(2,1)S(1)}, bf16[256,1024]{1,0:T(8,128)(2,1)S(1)}, u32[]{:S(2)}, u32[]{:S(2)}) collective-permute-start(bf16[256,1024]{1,0:T(8,128)(2,1)S(1)} %get-tuple-element.215), channel_id=1, source_target_pairs={{240,0},{244,4},{248,8},{252,12},{0,16},{4,20},{8,24},{12,28},{16,... | collective-permute-start | bytes 1572872 | tf_op jit(solution)/shard_map/while/body/eval_jaxpr/ppermute | solution.py:23
  151.9 13.2 %collective-permute-start = (bf16[256,1024]{1,0:T(8,128)(2,1)S(1)}, bf16[256,1024]{1,0:T(8,128)(2,1)S(1)}, u32[]{:S(2)}, u32[]{:S(2)}) collective-permute-start(bf16[256,1024]{1,0:T(8,128)(2,1)S(1)} %get-tuple-element.215), channel_id=1, source_target_pairs={{240,0},{244,4},{248,8},{252,12},{0,16},{4,20},{8,24},{12,28},{16,... | collective-permute-start | bytes 1572872 | tf_op jit(solution)/shard_map/while/body/eval_jaxpr/ppermute | solution.py:23
  166.5 14.3 %collective-permute-start = (bf16[256,1024]{1,0:T(8,128)(2,1)S(1)}, bf16[256,1024]{1,0:T(8,128)(2,1)S(1)}, u32[]{:S(2)}, u32[]{:S(2)}) collective-permute-start(bf16[256,1024]{1,0:T(8,128)(2,1)S(1)} %get-tuple-element.215), channel_id=1, source_target_pairs={{240,0},{244,4},{248,8},{252,12},{0,16},{4,20},{8,24},{12,28},{16,... | collective-permute-start | bytes 1572872 | tf_op jit(solution)/shard_map/while/body/eval_jaxpr/ppermute | solution.py:23
  182.1 15.4 %collective-permute-start = (bf16[256,1024]{1,0:T(8,128)(2,1)S(1)}, bf16[256,1024]{1,0:T(8,128)(2,1)S(1)}, u32[]{:S(2)}, u32[]{:S(2)}) collective-permute-start(bf16[256,1024]{1,0:T(8,128)(2,1)S(1)} %get-tuple-element.215), channel_id=1, source_target_pairs={{240,0},{244,4},{248,8},{252,12},{0,16},{4,20},{8,24},{12,28},{16,... | collective-permute-start | bytes 1572872 | tf_op jit(solution)/shard_map/while/body/eval_jaxpr/ppermute | solution.py:23
  198.8 16.6 %collective-permute-start = (bf16[256,1024]{1,0:T(8,128)(2,1)S(1)}, bf16[256,1024]{1,0:T(8,128)(2,1)S(1)}, u32[]{:S(2)}, u32[]{:S(2)}) collective-permute-start(bf16[256,1024]{1,0:T(8,128)(2,1)S(1)} %get-tuple-element.215), channel_id=1, source_target_pairs={{240,0},{244,4},{248,8},{252,12},{0,16},{4,20},{8,24},{12,28},{16,... | collective-permute-start | bytes 1572872 | tf_op jit(solution)/shard_map/while/body/eval_jaxpr/ppermute | solution.py:23
  216.8 16.1 %collective-permute-start = (bf16[256,1024]{1,0:T(8,128)(2,1)S(1)}, bf16[256,1024]{1,0:T(8,128)(2,1)S(1)}, u32[]{:S(2)}, u32[]{:S(2)}) collective-permute-start(bf16[256,1024]{1,0:T(8,128)(2,1)S(1)} %get-tuple-element.215), channel_id=1, source_target_pairs={{240,0},{244,4},{248,8},{252,12},{0,16},{4,20},{8,24},{12,28},{16,... | collective-permute-start | bytes 1572872 | tf_op jit(solution)/shard_map/while/body/eval_jaxpr/ppermute | solution.py:23
  234.1 15.2 %collective-permute-start = (bf16[256,1024]{1,0:T(8,128)(2,1)S(1)}, bf16[256,1024]{1,0:T(8,128)(2,1)S(1)}, u32[]{:S(2)}, u32[]{:S(2)}) collective-permute-start(bf16[256,1024]{1,0:T(8,128)(2,1)S(1)} %get-tuple-element.215), channel_id=1, source_target_pairs={{240,0},{244,4},{248,8},{252,12},{0,16},{4,20},{8,24},{12,28},{16,... | collective-permute-start | bytes 1572872 | tf_op jit(solution)/shard_map/while/body/eval_jaxpr/ppermute | solution.py:23
  250.7 14.3 %collective-permute-start = (bf16[256,1024]{1,0:T(8,128)(2,1)S(1)}, bf16[256,1024]{1,0:T(8,128)(2,1)S(1)}, u32[]{:S(2)}, u32[]{:S(2)}) collective-permute-start(bf16[256,1024]{1,0:T(8,128)(2,1)S(1)} %get-tuple-element.215), channel_id=1, source_target_pairs={{240,0},{244,4},{248,8},{252,12},{0,16},{4,20},{8,24},{12,28},{16,... | collective-permute-start | bytes 1572872 | tf_op jit(solution)/shard_map/while/body/eval_jaxpr/ppermute | solution.py:23
  266.3 13.4 %collective-permute-start = (bf16[256,1024]{1,0:T(8,128)(2,1)S(1)}, bf16[256,1024]{1,0:T(8,128)(2,1)S(1)}, u32[]{:S(2)}, u32[]{:S(2)}) collective-permute-start(bf16[256,1024]{1,0:T(8,128)(2,1)S(1)} %get-tuple-element.215), channel_id=1, source_target_pairs={{240,0},{244,4},{248,8},{252,12},{0,16},{4,20},{8,24},{12,28},{16,... | collective-permute-start | bytes 1572872 | tf_op jit(solution)/shard_map/while/body/eval_jaxpr/ppermute | solution.py:23
  281.0 12.4 %collective-permute-start = (bf16[256,1024]{1,0:T(8,128)(2,1)S(1)}, bf16[256,1024]{1,0:T(8,128)(2,1)S(1)}, u32[]{:S(2)}, u32[]{:S(2)}) collective-permute-start(bf16[256,1024]{1,0:T(8,128)(2,1)S(1)} %get-tuple-element.215), channel_id=1, source_target_pairs={{240,0},{244,4},{248,8},{252,12},{0,16},{4,20},{8,24},{12,28},{16,... | collective-permute-start | bytes 1572872 | tf_op jit(solution)/shard_map/while/body/eval_jaxpr/ppermute | solution.py:23
  294.7 11.3 %collective-permute-start = (bf16[256,1024]{1,0:T(8,128)(2,1)S(1)}, bf16[256,1024]{1,0:T(8,128)(2,1)S(1)}, u32[]{:S(2)}, u32[]{:S(2)}) collective-permute-start(bf16[256,1024]{1,0:T(8,128)(2,1)S(1)} %get-tuple-element.215), channel_id=1, source_target_pairs={{240,0},{244,4},{248,8},{252,12},{0,16},{4,20},{8,24},{12,28},{16,... | collective-permute-start | bytes 1572872 | tf_op jit(solution)/shard_map/while/body/eval_jaxpr/ppermute | solution.py:23
Sparse Core Ops, SparseCore 0:
  9.2 27.2 all-gather.1
where the time goes:
time: 319 us; the launch traced here: 314 us
  waiting for transfers between devices  238 us (75%)
  starting transfers between devices  23.4 us (7%)
  matrix products  22.4 us (7%)
  between operations  13.8 us (4%)
  local copies, waits for them, and re-layouts  11.1 us (3%)
  other arithmetic  5.64 us (2%)
    ppermute x15, waiting for transfers between devices, from_behind(): return lax.ppermute(block, axis, route)  205 us
    all_gather x1, waiting for transfers between devices, local(): lax.all_gather(samples, 'team', axis=0, tiled=True)  25.6 us
    ppermute x6, starting transfers between devices, shifted(): return lax.ppermute(array, axis, pairs)  23.4 us
    dot_general x16, matrix products, place_tile(): jnp.einsum('crk,pk->crp', local_pair, partner, preferred_element_type=jnp...  19.7 us
    ppermute x6, waiting for transfers between devices, shifted(): return lax.ppermute(array, axis, pairs)  6.38 us
  transfers between devices with their start and end apart: 22, of which 19 were waited for; matrix products, arithmetic and copies ran while one was open for 1% of the time, Pallas kernels for 0%

commit v1 on v0

v1 whole, which is shorter than its diff:
```python
import math

import jax
import jax.numpy as jnp
import numpy as np
from jax import lax
from jax.sharding import Mesh
from jax.sharding import PartitionSpec as P

FCH = 512
TAPS = 8
AVG = 32
SPEC = 16
SCALE = 1.0 / (AVG * SPEC)


def ring_pairs(count, by):
    return [(i, (i + by) % count) for i in range(count)]


def xor_pairs(count, by):
    return [(i, i ^ by) for i in range(count)]


def pfb_window():
    sample_pos = jnp.arange(TAPS * FCH, dtype=jnp.float32) + 0.5
    taper = jnp.sin(jnp.pi * sample_pos / (TAPS * FCH)) ** 2
    taps_table = jnp.sinc(sample_pos / FCH - TAPS / 2) * taper
    return taps_table.reshape(TAPS, FCH)


def dft_table():
    position = np.arange(FCH)
    angle = (position[:, None] * position[None, :] % FCH) * (2.0 * math.pi / FCH)
    table = np.concatenate([np.cos(angle), -np.sin(angle)], axis=1) / math.sqrt(FCH)
    return jnp.asarray(table.astype(np.float32))


def pick(stacked, slot):
    return lax.dynamic_index_in_dim(stacked, slot, 0, keepdims=False)


def exchange(pieces, axis, place):
    count = pieces.shape[0]
    received = [pick(pieces, place)]
    for by in range(1, count):
        received.append(lax.ppermute(pick(pieces, place ^ by), axis, xor_pairs(count, by)))
    stacked = jnp.stack(received)
    return jnp.stack([pick(stacked, place ^ i) for i in range(count)])


def spectra(samples):
    rows = samples.shape[0]
    frames = samples.astype(jnp.float32).reshape(rows, SPEC + TAPS - 1, FCH)
    window = pfb_window()
    filtered = window[0] * frames[:, 0:SPEC, :]
    for tap in range(1, TAPS):
        filtered = filtered + window[tap] * frames[:, tap : tap + SPEC, :]
    return jnp.einsum(
        "itp,pc->itc",
        filtered,
        dft_table(),
        precision=lax.Precision.HIGH,
        preferred_element_type=jnp.float32,
    )


def turned(block):
    half = block.shape[1] // 2
    return jnp.concatenate([block[:, half:], -block[:, :half]], axis=1)


def local(samples, input_gains):
    team = ("xh", "c")
    member = lax.axis_index(team)
    y_place = lax.axis_index("y")
    z_place = lax.axis_index("z")
    x_place = lax.axis_index("xl")
    members = lax.axis_size(team)
    bins = input_gains.shape[2]
    z_size = lax.axis_size("z")
    rows = samples.shape[0]

    gain_parts = input_gains.reshape(2, members, rows, bins * AVG).transpose(1, 0, 2, 3)
    gains = exchange(gain_parts, team, member)
    gains = gains.reshape(members, 2, rows, bins, AVG).transpose(1, 2, 3, 0, 4)

    shaped = spectra(samples).reshape(rows, SPEC, 2, bins, members, AVG)
    real, imag = shaped[:, :, 0], shaped[:, :, 1]
    gain_re, gain_im = gains[0][:, None], gains[1][:, None]
    volt_re = (gain_re * real - gain_im * imag).astype(jnp.bfloat16)
    volt_im = (gain_re * imag + gain_im * real).astype(jnp.bfloat16)
    packed = jnp.stack([volt_re, volt_im], axis=1)
    packed = packed.transpose(4, 3, 0, 1, 2, 5)
    packed = packed.reshape(members, bins, rows, 2 * SPEC * AVG)

    by_member = exchange(packed, team, member)
    by_bin = by_member.transpose(1, 0, 2, 3).reshape(bins, members * rows, -1)
    block = exchange(by_bin, "y", y_place)
    block = block.reshape(bins * members * rows, -1)
    height = block.shape[0]

    other = lax.ppermute(block, "xl", ring_pairs(2, 1))
    own_left = jnp.concatenate([block, turned(block)], axis=0)
    other_left = jnp.concatenate([other, turned(other)], axis=0)

    visibility = jnp.zeros((2, height, height * z_size * 2), jnp.float32)

    def product(lhs, columns):
        return (
            jnp.einsum("rk,pk->rp", lhs, columns, preferred_element_type=jnp.float32) * SCALE
        )

    def place(state, values, group):
        values = values.astype(jnp.float32).reshape(2, height, -1)
        nought = jnp.zeros((), jnp.int32)
        return lax.dynamic_update_slice(state, values, (nought, nought, group * height))

    visibility = place(visibility, product(own_left, block), x_place * z_size + z_place)
    visibility = place(visibility, product(own_left, other), (1 - x_place) * z_size + z_place)

    ahead, behind = block, block
    for step in range(1, z_size // 2 + 1):
        if step < z_size // 2:
            ahead = lax.ppermute(ahead, "z", ring_pairs(z_size, 1))
            behind = lax.ppermute(behind, "z", ring_pairs(z_size, -1))
            arrived = [(ahead, (z_place - step) % z_size), (behind, (z_place + step) % z_size)]
        else:
            half = height // 2
            upper = lax.ppermute(ahead[:half], "z", ring_pairs(z_size, 1))
            lower = lax.ppermute(behind[half:], "z", ring_pairs(z_size, -1))
            arrived = [(jnp.concatenate([upper, lower], axis=0), (z_place + step) % z_size)]
        made = [product(other_left, columns).astype(jnp.bfloat16) for columns, _ in arrived]
        given = lax.ppermute(jnp.stack(made), "xl", ring_pairs(2, 1))
        for index, (columns, group) in enumerate(arrived):
            visibility = place(visibility, product(own_left, columns), x_place * z_size + group)
            visibility = place(visibility, given[index], (1 - x_place) * z_size + group)
    return visibility[None, None]


def solution(mesh):
    fine = Mesh(
        mesh.devices.reshape(2, 8, 4, 2, 2), ("xl", "z", "y", "xh", "c")
    )
    everything = ("xl", "z", "y", "xh", "c")
    return jax.shard_map(
        local,
        mesh=fine,
        in_specs=(P(everything, None), P(None, ("xl", "z", "y"), None, ("xh", "c"))),
        out_specs=P(("xl", "z", "y"), ("xh", "c"), None, None, None),
        check_vma=False,
    )
```

time: 319 us -> 113 us (0.35)
  waiting for transfers between devices: 238 us -> 46 us
  between operations: 13.8 us -> 0.57 us
  matrix products: 22.4 us -> 10.7 us
  starting transfers between devices: 23.4 us -> 33.1 us
  local copies, waits for them, and re-layouts: 11.1 us -> 15.1 us
    ppermute x21 -> x22, waiting for transfers between devices: 211 us -> 46 us  [the longest x3 16.9 us: local(): behind = lax.ppermute(behind, 'z', ring_pairs(z_size, -1))]
    all_gather x1 -> x0, waiting for transfers between devices: 25.6 us -> none  [local(): lax.all_gather(samples, 'team', axis=0, tiled=True)]
    dot_general x17, matrix products: 22.4 us -> 10.7 us  [the longest x16 7.63 us: product(): jnp.einsum('rk,pk->rp', lhs, columns, preferred_element_type=jnp.float32)]
    ppermute x21 -> x22, starting transfers between devices: 23.4 us -> 33.1 us  [the longest x9 11.2 us: exchange(): lax.ppermute(pick(pieces, place ^ by), axis, xor_pairs(count, by))]
    reshape x1 -> x5, local copies, waits for them, and re-layouts: 2.68 us -> 7.31 us  [the longest x1 3.52 us: local(): shaped = spectra(samples).reshape(rows, SPEC, 2, bins, members, AVG)]
    slice x1 -> x7, local copies, waits for them, and re-layouts: 0.62 us -> 4.76 us  [the longest x1 4.61 us: local(): real, imag = (shaped[:, :, 0], shaped[:, :, 1])]
  transfers between devices with their start and end apart: 22 -> 22, of which waited for: 19 -> 13; matrix products, arithmetic and copies ran while one was open for 1% -> 20% of each run, Pallas kernels for 0% -> 0%
where the time goes in v1:
time: 113 us; the launch traced here: 111 us
  waiting for transfers between devices  46 us (41%)
  starting transfers between devices  33.1 us (29%)
  local copies, waits for them, and re-layouts  15.1 us (13%)
  matrix products  10.7 us (9%)
  other arithmetic  5.37 us (5%)
    ppermute x3, waiting for transfers between devices, local(): behind = lax.ppermute(behind, 'z', ring_pairs(z_size, -1))  16.9 us
    ppermute x9, waiting for transfers between devices, exchange(): lax.ppermute(pick(pieces, place ^ by), axis, xor_pairs(count, by))  13.4 us
    ppermute x9, starting transfers between devices, exchange(): lax.ppermute(pick(pieces, place ^ by), axis, xor_pairs(count, by))  11.2 us
    ppermute x3, starting transfers between devices, local(): behind = lax.ppermute(behind, 'z', ring_pairs(z_size, -1))  10.7 us
    dot_general x16, matrix products, product(): jnp.einsum('rk,pk->rp', lhs, columns, preferred_element_type=jnp.float32)  7.63 us
    ppermute x4, waiting for transfers between devices, local(): given = lax.ppermute(jnp.stack(made), 'xl', ring_pairs(2, 1))  5.06 us
    slice x1, local copies, waits for them, and re-layouts, local(): real, imag = (shaped[:, :, 0], shaped[:, :, 1])  4.61 us
    ppermute x4, starting transfers between devices, local(): given = lax.ppermute(jnp.stack(made), 'xl', ring_pairs(2, 1))  4.4 us
  transfers between devices with their start and end apart: 22, of which 13 were waited for; matrix products, arithmetic and copies ran while one was open for 20% of the time, Pallas kernels for 0%

profile of v1, /device:TPU:6, one launch (start us, length us, event | category | flops | bytes accessed | tf_op | source)
XLA Modules:
  0.0 110.8 jit_solution(17767197692073585982)
XLA Ops:
  2.2 2.1 %collective-permute-start.1 = (f32[2,16,128]{2,1,0:T(8,128)S(1)}, f32[2,16,128]{2,1,0:T(8,128)S(1)}, u32[]{:S(2)}, u32[]{:S(2)}) collective-permute-start(f32[2,16,128]{2,1,0:T(8,128)S(1)} %get-tuple-element.43), channel_id=1, source_target_pairs={{0,2},{1,3},{2,0},{3,1},{4,6},{5,7},{6,4},{7,5},{8,10},{9,11},{10,... | collective-permute-start | bytes 49160 | tf_op jit(solution)/shard_map/ppermute | solution.py:47
  6.1 3.1 %fusion.15 = f32[16,16,1024]{2,1,0:T(8,128)S(1)} fusion(f32[512,1024,1]{1,0,2:T(8,128)} %constant.203, f32[16,23,512]{2,1,0:T(8,128)S(1)} %reshape.249, f32[512]{0:T(512)S(1)} %get-tuple-element.46, f32[512]{0:T(512)S(1)} %get-tuple-element.47, f32[512]{0:T(512)S(1)} %get-tuple-element.48, f32[512]{0:T(512)S(1)} %get-tuple-element.49, ...), kind=kOutput, calls=%fused_computation.39 | convolution fusion | flops 807272448 | bytes 7356416 | tf_op jit(solution)/shard_map/itp,pc->itc/dot_general | solution.py:59
  9.2 3.5 %reshape.244 = f32[16,16,2,4,4,32]{5,4,3,2,1,0:T(4,128)} reshape(f32[16,16,1024]{2,1,0:T(8,128)S(1)} %fusion.15) | data formatting | bytes 2097152 | tf_op jit(solution)/shard_map/reshape | solution.py:88
  12.7 4.6 %fusion.50 = (f32[16,16,1,4,4,32]{5,4,3,2,1,0:T(4,128)S(1)}, f32[16,16,1,4,4,32]{5,4,3,2,1,0:T(4,128)}) fusion(f32[16,16,2,4,4,32]{5,4,3,2,1,0:T(4,128)} %reshape.244), kind=kLoop, calls=%fused_computation.140 | loop fusion | bytes 2097152 | tf_op jit(solution)/shard_map/slice | solution.py:89
  17.6 3.2 %subtract_convert_fusion = (bf16[16,1,16,4,4,32]{5,2,1,0,3,4:T(8,128)(2,1)S(1)}, bf16[16,1,16,4,4,32]{5,2,1,0,3,4:T(8,128)(2,1)S(1)}) fusion(f32[16,16,1,4,4,32]{5,4,3,2,1,0:T(4,128)} %get-tuple-element.8, f32[16,16,1,4,4,32]{5,4,3,2,1,0:T(4,128)S(1)} %get-tuple-element.7, f32[16,4,4,32]{3,0,1,2:T(8,128)S(1)} %copy.8, f32[16,4,4,32]{3,0,1,2:T(8,128)S(1)} %copy.6), kind=kLoop, calls=%fused_computation.4 | loop fusion | flops 1048576 | bytes 1638400 | tf_op jit(solution)/shard_map/convert_element_type | solution.py:91
  21.2 2.2 %reshape.245 = bf16[4,4,16,1024]{3,2,1,0:T(8,128)(2,1)S(1)} reshape(bf16[4,4,16,2,16,32]{5,4,3,2,1,0:T(8,128)(2,1)S(1)} %maximum_bitcast_fusion) | data formatting | bytes 1048576 | tf_op jit(solution)/shard_map/reshape | solution.py:95
  24.7 2.1 %collective-permute-start.4 = (bf16[4,16,1024]{2,1,0:T(8,128)(2,1)S(1)}, bf16[4,16,1024]{2,1,0:T(8,128)(2,1)S(1)}, u32[]{:S(2)}, u32[]{:S(2)}) collective-permute-start(bf16[4,16,1024]{2,1,0:T(8,128)(2,1)S(1)} %get-tuple-element.33), channel_id=1, source_target_pairs={{0,2},{1,3},{2,0},{3,1},{4,6},{5,7},{6,4},{7,5},{8,10},{9,11},{10,... | collective-permute-start | bytes 393224 | tf_op jit(solution)/shard_map/ppermute | solution.py:47
  27.0 3.6 %collective-permute-done.5 = bf16[4,16,1024]{2,1,0:T(8,128)(2,1)S(1)} collective-permute-done((bf16[4,16,1024]{2,1,0:T(8,128)(2,1)S(1)}, bf16[4,16,1024]{2,1,0:T(8,128)(2,1)S(1)}, u32[]{:S(2)}, u32[]{:S(2)}) %collective-permute-start.5) | collective-permute-done | bytes 131104 | tf_op jit(solution)/shard_map/ppermute | solution.py:47
  30.6 3.1 %collective-permute-done.4 = bf16[4,16,1024]{2,1,0:T(8,128)(2,1)S(1)} collective-permute-done((bf16[4,16,1024]{2,1,0:T(8,128)(2,1)S(1)}, bf16[4,16,1024]{2,1,0:T(8,128)(2,1)S(1)}, u32[]{:S(2)}, u32[]{:S(2)}) %collective-permute-start.4) | collective-permute-done | bytes 131104 | tf_op jit(solution)/shard_map/ppermute | solution.py:47
  34.0 3.1 %collective-permute-start.8 = (bf16[64,1024]{1,0:T(8,128)(2,1)S(1)}, bf16[64,1024]{1,0:T(8,128)(2,1)S(1)}, u32[]{:S(2)}, u32[]{:S(2)}) collective-permute-start(bf16[64,1024]{1,0:T(8,128)(2,1)S(1)} %get-tuple-element.24), channel_id=1, source_target_pairs={{0,12},{4,8},{8,4},{12,0},{1,13},{5,9},{9,5},{13,1},{2,14},{6,10},... | collective-permute-start | bytes 393224 | tf_op jit(solution)/shard_map/ppermute | solution.py:47
  38.3 4.4 %collective-permute-done.8 = bf16[64,1024]{1,0:T(8,128)(2,1)S(1)} collective-permute-done((bf16[64,1024]{1,0:T(8,128)(2,1)S(1)}, bf16[64,1024]{1,0:T(8,128)(2,1)S(1)}, u32[]{:S(2)}, u32[]{:S(2)}) %collective-permute-start.8) | collective-permute-done | bytes 131104 | tf_op jit(solution)/shard_map/ppermute | solution.py:47
  42.7 2.3 %collective-permute-done.7 = bf16[64,1024]{1,0:T(8,128)(2,1)S(1)} collective-permute-done((bf16[64,1024]{1,0:T(8,128)(2,1)S(1)}, bf16[64,1024]{1,0:T(8,128)(2,1)S(1)}, u32[]{:S(2)}, u32[]{:S(2)}) %collective-permute-start.7) | collective-permute-done | bytes 131104 | tf_op jit(solution)/shard_map/ppermute | solution.py:47
  46.1 1.9 %collective-permute-start.10 = (bf16[256,1024]{1,0:T(8,128)(2,1)S(1)}, bf16[256,1024]{1,0:T(8,128)(2,1)S(1)}, u32[]{:S(2)}, u32[]{:S(2)}) collective-permute-start(bf16[256,1024]{1,0:T(8,128)(2,1)S(1)} %bitcast.112), channel_id=1, source_target_pairs={{0,16},{16,32},{32,48},{48,64},{64,80},{80,96},{96,112},{112,0},{1... | collective-permute-start | bytes 1572872 | tf_op jit(solution)/shard_map/ppermute | solution.py:125
  48.0 3.9 %collective-permute-start.11 = (bf16[256,1024]{1,0:T(8,128)(2,1)S(1)}, bf16[256,1024]{1,0:T(8,128)(2,1)S(1)}, u32[]{:S(2)}, u32[]{:S(2)}) collective-permute-start(bf16[256,1024]{1,0:T(8,128)(2,1)S(1)} %bitcast.113), channel_id=1, source_target_pairs={{0,112},{16,0},{32,16},{48,32},{64,48},{80,64},{96,80},{112,96},{1... | collective-permute-start | bytes 1572872 | tf_op jit(solution)/shard_map/ppermute | solution.py:126
  53.6 3.9 %collective-permute-done.9 = bf16[256,1024]{1,0:T(8,128)(2,1)S(1)} collective-permute-done((bf16[256,1024]{1,0:T(8,128)(2,1)S(1)}, bf16[256,1024]{1,0:T(8,128)(2,1)S(1)}, u32[]{:S(2)}, u32[]{:S(2)}) %collective-permute-start.9) | collective-permute-done | bytes 524320 | tf_op jit(solution)/shard_map/ppermute | solution.py:103
  57.5 3.9 %collective-permute-done.11 = bf16[256,1024]{1,0:T(8,128)(2,1)S(1)} collective-permute-done((bf16[256,1024]{1,0:T(8,128)(2,1)S(1)}, bf16[256,1024]{1,0:T(8,128)(2,1)S(1)}, u32[]{:S(2)}, u32[]{:S(2)}) %collective-permute-start.11) | collective-permute-done | bytes 524320 | tf_op jit(solution)/shard_map/ppermute | solution.py:126
  64.4 3.5 %collective-permute-start.14 = (bf16[256,1024]{1,0:T(8,128)(2,1)S(1)}, bf16[256,1024]{1,0:T(8,128)(2,1)S(1)}, u32[]{:S(2)}, u32[]{:S(2)}) collective-permute-start(bf16[256,1024]{1,0:T(8,128)(2,1)S(1)} %collective-permute-done.11), channel_id=1, source_target_pairs={{0,112},{16,0},{32,16},{48,32},{64,48},{80,64},{96,80},{112,96},{1... | collective-permute-start | bytes 1572872 | tf_op jit(solution)/shard_map/ppermute | solution.py:126
  69.1 7.0 %collective-permute-done.14 = bf16[256,1024]{1,0:T(8,128)(2,1)S(1)} collective-permute-done((bf16[256,1024]{1,0:T(8,128)(2,1)S(1)}, bf16[256,1024]{1,0:T(8,128)(2,1)S(1)}, u32[]{:S(2)}, u32[]{:S(2)}) %collective-permute-start.14) | collective-permute-done | bytes 524320 | tf_op jit(solution)/shard_map/ppermute | solution.py:126
  76.6 3.5 %collective-permute-done.13 = bf16[256,1024]{1,0:T(8,128)(2,1)S(1)} collective-permute-done((bf16[256,1024]{1,0:T(8,128)(2,1)S(1)}, bf16[256,1024]{1,0:T(8,128)(2,1)S(1)}, u32[]{:S(2)}, u32[]{:S(2)}) %collective-permute-start.13) | collective-permute-done | bytes 524320 | tf_op jit(solution)/shard_map/ppermute | solution.py:125
  82.3 3.2 %collective-permute-start.17 = (bf16[256,1024]{1,0:T(8,128)(2,1)S(1)}, bf16[256,1024]{1,0:T(8,128)(2,1)S(1)}, u32[]{:S(2)}, u32[]{:S(2)}) collective-permute-start(bf16[256,1024]{1,0:T(8,128)(2,1)S(1)} %collective-permute-done.14), channel_id=1, source_target_pairs={{0,112},{16,0},{32,16},{48,32},{64,48},{80,64},{96,80},{112,96},{1... | collective-permute-start | bytes 1572872 | tf_op jit(solution)/shard_map/ppermute | solution.py:126
  86.1 6.1 %collective-permute-done.17 = bf16[256,1024]{1,0:T(8,128)(2,1)S(1)} collective-permute-done((bf16[256,1024]{1,0:T(8,128)(2,1)S(1)}, bf16[256,1024]{1,0:T(8,128)(2,1)S(1)}, u32[]{:S(2)}, u32[]{:S(2)}) %collective-permute-start.17) | collective-permute-done | bytes 524320 | tf_op jit(solution)/shard_map/ppermute | solution.py:126
  95.0 3.8 %collective-permute-start.20 = (bf16[128,1024]{1,0:T(8,128)(2,1)S(1)}, bf16[128,1024]{1,0:T(8,128)(2,1)S(1)}, u32[]{:S(2)}, u32[]{:S(2)}) collective-permute-start(bf16[128,1024]{1,0:T(8,128)(2,1)S(1)} %slice.167), channel_id=1, source_target_pairs={{0,112},{16,0},{32,16},{48,32},{64,48},{80,64},{96,80},{112,96},{1... | collective-permute-start | bytes 786440 | tf_op jit(solution)/shard_map/ppermute | solution.py:131
  100.1 2.9 %collective-permute-done.19 = bf16[128,1024]{1,0:T(8,128)(2,1)S(1)} collective-permute-done((bf16[128,1024]{1,0:T(8,128)(2,1)S(1)}, bf16[128,1024]{1,0:T(8,128)(2,1)S(1)}, u32[]{:S(2)}, u32[]{:S(2)}) %collective-permute-start.19) | collective-permute-done | bytes 262176 | tf_op jit(solution)/shard_map/ppermute | solution.py:130
  105.7 4.3 %collective-permute-done.21 = bf16[1,512,256]{2,1,0:T(8,128)(2,1)S(1)} collective-permute-done((bf16[1,512,256]{2,1,0:T(8,128)(2,1)S(1)}, bf16[1,512,256]{2,1,0:T(8,128)(2,1)S(1)}, u32[]{:S(2)}, u32[]{:S(2)}) %collective-permute-start.21) | collective-permute-done | bytes 262176 | tf_op jit(solution)/shard_map/ppermute | solution.py:134
  (95 shorter events, 24.9 us)
Async XLA Ops:
  1.3 16.0 %collective-permute-start.2 = (f32[2,16,128]{2,1,0:T(8,128)S(1)}, f32[2,16,128]{2,1,0:T(8,128)S(1)}, u32[]{:S(2)}, u32[]{:S(2)}) collective-permute-start(f32[2,16,128]{2,1,0:T(8,128)S(1)} %get-tuple-element.42), channel_id=1, source_target_pairs={{0,3},{1,2},{2,1},{3,0},{4,7},{5,6},{6,5},{7,4},{8,11},{9,10},{10,... | collective-permute-start | bytes 49160 | tf_op jit(solution)/shard_map/ppermute | solution.py:47
  2.2 15.1 %collective-permute-start.1 = (f32[2,16,128]{2,1,0:T(8,128)S(1)}, f32[2,16,128]{2,1,0:T(8,128)S(1)}, u32[]{:S(2)}, u32[]{:S(2)}) collective-permute-start(f32[2,16,128]{2,1,0:T(8,128)S(1)} %get-tuple-element.43), channel_id=1, source_target_pairs={{0,2},{1,3},{2,0},{3,1},{4,6},{5,7},{6,4},{7,5},{8,10},{9,11},{10,... | collective-permute-start | bytes 49160 | tf_op jit(solution)/shard_map/ppermute | solution.py:47
  4.3 13.0 %collective-permute-start = (f32[2,16,128]{2,1,0:T(8,128)S(1)}, f32[2,16,128]{2,1,0:T(8,128)S(1)}, u32[]{:S(2)}, u32[]{:S(2)}) collective-permute-start(f32[2,16,128]{2,1,0:T(8,128)S(1)} %get-tuple-element.44), channel_id=1, source_target_pairs={{0,1},{1,0},{2,3},{3,2},{4,5},{5,4},{6,7},{7,6},{8,9},{9,8},{10,11... | collective-permute-start | bytes 49160 | tf_op jit(solution)/shard_map/ppermute | solution.py:47
  23.5 7.1 %collective-permute-start.5 = (bf16[4,16,1024]{2,1,0:T(8,128)(2,1)S(1)}, bf16[4,16,1024]{2,1,0:T(8,128)(2,1)S(1)}, u32[]{:S(2)}, u32[]{:S(2)}) collective-permute-start(bf16[4,16,1024]{2,1,0:T(8,128)(2,1)S(1)} %get-tuple-element.32), channel_id=1, source_target_pairs={{0,3},{1,2},{2,1},{3,0},{4,7},{5,6},{6,5},{7,4},{8,11},{9,10},{10,... | collective-permute-start | bytes 393224 | tf_op jit(solution)/shard_map/ppermute | solution.py:47
  24.7 9.0 %collective-permute-start.4 = (bf16[4,16,1024]{2,1,0:T(8,128)(2,1)S(1)}, bf16[4,16,1024]{2,1,0:T(8,128)(2,1)S(1)}, u32[]{:S(2)}, u32[]{:S(2)}) collective-permute-start(bf16[4,16,1024]{2,1,0:T(8,128)(2,1)S(1)} %get-tuple-element.33), channel_id=1, source_target_pairs={{0,2},{1,3},{2,0},{3,1},{4,6},{5,7},{6,4},{7,5},{8,10},{9,11},{10,... | collective-permute-start | bytes 393224 | tf_op jit(solution)/shard_map/ppermute | solution.py:47
  26.8 6.9 %collective-permute-start.3 = (bf16[4,16,1024]{2,1,0:T(8,128)(2,1)S(1)}, bf16[4,16,1024]{2,1,0:T(8,128)(2,1)S(1)}, u32[]{:S(2)}, u32[]{:S(2)}) collective-permute-start(bf16[4,16,1024]{2,1,0:T(8,128)(2,1)S(1)} %get-tuple-element.34), channel_id=1, source_target_pairs={{0,1},{1,0},{2,3},{3,2},{4,5},{5,4},{6,7},{7,6},{8,9},{9,8},{10,11... | collective-permute-start | bytes 393224 | tf_op jit(solution)/shard_map/ppermute | solution.py:47
  34.0 8.7 %collective-permute-start.8 = (bf16[64,1024]{1,0:T(8,128)(2,1)S(1)}, bf16[64,1024]{1,0:T(8,128)(2,1)S(1)}, u32[]{:S(2)}, u32[]{:S(2)}) collective-permute-start(bf16[64,1024]{1,0:T(8,128)(2,1)S(1)} %get-tuple-element.24), channel_id=1, source_target_pairs={{0,12},{4,8},{8,4},{12,0},{1,13},{5,9},{9,5},{13,1},{2,14},{6,10},... | collective-permute-start | bytes 393224 | tf_op jit(solution)/shard_map/ppermute | solution.py:47
  37.1 7.9 %collective-permute-start.7 = (bf16[64,1024]{1,0:T(8,128)(2,1)S(1)}, bf16[64,1024]{1,0:T(8,128)(2,1)S(1)}, u32[]{:S(2)}, u32[]{:S(2)}) collective-permute-start(bf16[64,1024]{1,0:T(8,128)(2,1)S(1)} %get-tuple-element.25), channel_id=1, source_target_pairs={{0,8},{4,12},{8,0},{12,4},{1,9},{5,13},{9,1},{13,5},{2,10},{6,14},... | collective-permute-start | bytes 393224 | tf_op jit(solution)/shard_map/ppermute | solution.py:47
  37.8 7.2 %collective-permute-start.6 = (bf16[64,1024]{1,0:T(8,128)(2,1)S(1)}, bf16[64,1024]{1,0:T(8,128)(2,1)S(1)}, u32[]{:S(2)}, u32[]{:S(2)}) collective-permute-start(bf16[64,1024]{1,0:T(8,128)(2,1)S(1)} %get-tuple-element.26), channel_id=1, source_target_pairs={{0,4},{4,0},{8,12},{12,8},{1,5},{5,1},{9,13},{13,9},{2,6},{6,2},{1... | collective-permute-start | bytes 393224 | tf_op jit(solution)/shard_map/ppermute | solution.py:47
  45.2 12.2 %collective-permute-start.9 = (bf16[256,1024]{1,0:T(8,128)(2,1)S(1)}, bf16[256,1024]{1,0:T(8,128)(2,1)S(1)}, u32[]{:S(2)}, u32[]{:S(2)}) collective-permute-start(bf16[256,1024]{1,0:T(8,128)(2,1)S(1)} %bitcast.111), channel_id=1, source_target_pairs={{0,128},{128,0},{1,129},{129,1},{2,130},{130,2},{3,131},{131,3},{4... | collective-permute-start | bytes 1572872 | tf_op jit(solution)/shard_map/ppermute | solution.py:103
  46.1 16.0 %collective-permute-start.10 = (bf16[256,1024]{1,0:T(8,128)(2,1)S(1)}, bf16[256,1024]{1,0:T(8,128)(2,1)S(1)}, u32[]{:S(2)}, u32[]{:S(2)}) collective-permute-start(bf16[256,1024]{1,0:T(8,128)(2,1)S(1)} %bitcast.112), channel_id=1, source_target_pairs={{0,16},{16,32},{32,48},{48,64},{64,80},{80,96},{96,112},{112,0},{1... | collective-permute-start | bytes 1572872 | tf_op jit(solution)/shard_map/ppermute | solution.py:125
  48.0 13.3 %collective-permute-start.11 = (bf16[256,1024]{1,0:T(8,128)(2,1)S(1)}, bf16[256,1024]{1,0:T(8,128)(2,1)S(1)}, u32[]{:S(2)}, u32[]{:S(2)}) collective-permute-start(bf16[256,1024]{1,0:T(8,128)(2,1)S(1)} %bitcast.113), channel_id=1, source_target_pairs={{0,112},{16,0},{32,16},{48,32},{64,48},{80,64},{96,80},{112,96},{1... | collective-permute-start | bytes 1572872 | tf_op jit(solution)/shard_map/ppermute | solution.py:126
  62.6 18.9 %collective-permute-start.12 = (bf16[2,512,256]{2,1,0:T(8,128)(2,1)S(1)}, bf16[2,512,256]{2,1,0:T(8,128)(2,1)S(1)}, u32[]{:S(2)}, u32[]{:S(2)}) collective-permute-start(bf16[2,512,256]{2,1,0:T(8,128)(2,1)S(1)} %pad_maximum_fusion.3), channel_id=1, source_target_pairs={{0,128},{128,0},{1,129},{129,1},{2,130},{130,2},{3,131},{131,3},{4... | collective-permute-start | bytes 1572872 | tf_op jit(solution)/shard_map/ppermute | solution.py:134
  64.4 11.7 %collective-permute-start.14 = (bf16[256,1024]{1,0:T(8,128)(2,1)S(1)}, bf16[256,1024]{1,0:T(8,128)(2,1)S(1)}, u32[]{:S(2)}, u32[]{:S(2)}) collective-permute-start(bf16[256,1024]{1,0:T(8,128)(2,1)S(1)} %collective-permute-done.11), channel_id=1, source_target_pairs={{0,112},{16,0},{32,16},{48,32},{64,48},{80,64},{96,80},{112,96},{1... | collective-permute-start | bytes 1572872 | tf_op jit(solution)/shard_map/ppermute | solution.py:126
  68.4 11.7 %collective-permute-start.13 = (bf16[256,1024]{1,0:T(8,128)(2,1)S(1)}, bf16[256,1024]{1,0:T(8,128)(2,1)S(1)}, u32[]{:S(2)}, u32[]{:S(2)}) collective-permute-start(bf16[256,1024]{1,0:T(8,128)(2,1)S(1)} %collective-permute-done.10), channel_id=1, source_target_pairs={{0,16},{16,32},{32,48},{48,64},{64,80},{80,96},{96,112},{112,0},{1... | collective-permute-start | bytes 1572872 | tf_op jit(solution)/shard_map/ppermute | solution.py:125
  80.6 18.1 %collective-permute-start.15 = (bf16[2,512,256]{2,1,0:T(8,128)(2,1)S(1)}, bf16[2,512,256]{2,1,0:T(8,128)(2,1)S(1)}, u32[]{:S(2)}, u32[]{:S(2)}) collective-permute-start(bf16[2,512,256]{2,1,0:T(8,128)(2,1)S(1)} %pad_maximum_fusion.4), channel_id=1, source_target_pairs={{0,128},{128,0},{1,129},{129,1},{2,130},{130,2},{3,131},{131,3},{4... | collective-permute-start | bytes 1572872 | tf_op jit(solution)/shard_map/ppermute | solution.py:134
  82.2 10.5 %collective-permute-start.16 = (bf16[256,1024]{1,0:T(8,128)(2,1)S(1)}, bf16[256,1024]{1,0:T(8,128)(2,1)S(1)}, u32[]{:S(2)}, u32[]{:S(2)}) collective-permute-start(bf16[256,1024]{1,0:T(8,128)(2,1)S(1)} %collective-permute-done.13), channel_id=1, source_target_pairs={{0,16},{16,32},{32,48},{48,64},{64,80},{80,96},{96,112},{112,0},{1... | collective-permute-start | bytes 1572872 | tf_op jit(solution)/shard_map/ppermute | solution.py:125
  82.3 9.9 %collective-permute-start.17 = (bf16[256,1024]{1,0:T(8,128)(2,1)S(1)}, bf16[256,1024]{1,0:T(8,128)(2,1)S(1)}, u32[]{:S(2)}, u32[]{:S(2)}) collective-permute-start(bf16[256,1024]{1,0:T(8,128)(2,1)S(1)} %collective-permute-done.14), channel_id=1, source_target_pairs={{0,112},{16,0},{32,16},{48,32},{64,48},{80,64},{96,80},{112,96},{1... | collective-permute-start | bytes 1572872 | tf_op jit(solution)/shard_map/ppermute | solution.py:126
  93.3 12.1 %collective-permute-start.18 = (bf16[2,512,256]{2,1,0:T(8,128)(2,1)S(1)}, bf16[2,512,256]{2,1,0:T(8,128)(2,1)S(1)}, u32[]{:S(2)}, u32[]{:S(2)}) collective-permute-start(bf16[2,512,256]{2,1,0:T(8,128)(2,1)S(1)} %pad_maximum_fusion.5), channel_id=1, source_target_pairs={{0,128},{128,0},{1,129},{129,1},{2,130},{130,2},{3,131},{131,3},{4... | collective-permute-start | bytes 1572872 | tf_op jit(solution)/shard_map/ppermute | solution.py:134
  94.9 8.1 %collective-permute-start.19 = (bf16[128,1024]{1,0:T(8,128)(2,1)S(1)}, bf16[128,1024]{1,0:T(8,128)(2,1)S(1)}, u32[]{:S(2)}, u32[]{:S(2)}) collective-permute-start(bf16[128,1024]{1,0:T(8,128)(2,1)S(1)} %slice.166), channel_id=1, source_target_pairs={{0,16},{16,32},{32,48},{48,64},{64,80},{80,96},{96,112},{112,0},{1... | collective-permute-start | bytes 786440 | tf_op jit(solution)/shard_map/ppermute | solution.py:130
  95.0 8.0 %collective-permute-start.20 = (bf16[128,1024]{1,0:T(8,128)(2,1)S(1)}, bf16[128,1024]{1,0:T(8,128)(2,1)S(1)}, u32[]{:S(2)}, u32[]{:S(2)}) collective-permute-start(bf16[128,1024]{1,0:T(8,128)(2,1)S(1)} %slice.167), channel_id=1, source_target_pairs={{0,112},{16,0},{32,16},{48,32},{64,48},{80,64},{96,80},{112,96},{1... | collective-permute-start | bytes 786440 | tf_op jit(solution)/shard_map/ppermute | solution.py:131
  103.5 6.5 %collective-permute-start.21 = (bf16[1,512,256]{2,1,0:T(8,128)(2,1)S(1)}, bf16[1,512,256]{2,1,0:T(8,128)(2,1)S(1)}, u32[]{:S(2)}, u32[]{:S(2)}) collective-permute-start(bf16[1,512,256]{2,1,0:T(8,128)(2,1)S(1)} %fusion.7), channel_id=1, source_target_pairs={{0,128},{128,0},{1,129},{129,1},{2,130},{130,2},{3,131},{131,3},{4... | collective-permute-start | bytes 786440 | tf_op jit(solution)/shard_map/ppermute | solution.py:134
  105.7 4.4 %copy-start = (f32[1,1,2,256,4096]{4,3,2,1,0:T(8,128)}, f32[1,1,2,256,4096]{4,3,2,1,0:T(8,128)S(1)}, u32[]{:S(2)}) copy-start(f32[1,1,2,256,4096]{4,3,2,1,0:T(8,128)S(1)} %constant_dynamic-update-slice_fusion) | copy-start | bytes 25165828

commit v2 on v1

--- a/solution.py
+++ b/solution.py
@@ -2,8 +2,11 @@
 
 import jax
 import jax.numpy as jnp
+import ml_dtypes
 import numpy as np
 from jax import lax
+from jax.experimental import pallas as pl
+from jax.experimental.pallas import tpu as pltpu
 from jax.sharding import Mesh
 from jax.sharding import PartitionSpec as P
 
@@ -23,46 +26,125 @@
 
 
 def pfb_window():
-    sample_pos = jnp.arange(TAPS * FCH, dtype=jnp.float32) + 0.5
-    taper = jnp.sin(jnp.pi * sample_pos / (TAPS * FCH)) ** 2
-    taps_table = jnp.sinc(sample_pos / FCH - TAPS / 2) * taper
-    return taps_table.reshape(TAPS, FCH)
+    position = np.arange(TAPS * FCH) + 0.5
+    taper = np.sin(np.pi * position / (TAPS * FCH)) ** 2
+    table = np.sinc(position / FCH - TAPS / 2) * taper
+    return table.reshape(TAPS, FCH).astype(np.float32)
 
 
 def dft_table():
     position = np.arange(FCH)
     angle = (position[:, None] * position[None, :] % FCH) * (2.0 * math.pi / FCH)
     table = np.concatenate([np.cos(angle), -np.sin(angle)], axis=1) / math.sqrt(FCH)
-    return jnp.asarray(table.astype(np.float32))
+    upper = table.astype(ml_dtypes.bfloat16)
+    lower = (table - upper.astype(np.float64)).astype(ml_dtypes.bfloat16)
+    return np.concatenate([upper, lower, upper], axis=0)
 
 
 def pick(stacked, slot):
     return lax.dynamic_index_in_dim(stacked, slot, 0, keepdims=False)
 
 
-def exchange(pieces, axis, place):
-    count = pieces.shape[0]
-    received = [pick(pieces, place)]
-    for by in range(1, count):
-        received.append(lax.ppermute(pick(pieces, place ^ by), axis, xor_pairs(count, by)))
+def exchange(pieces, axis):
+    count = len(pieces)
+    return [pieces[0]] + [
+        lax.ppermute(pieces[by], axis, xor_pairs(count, by)) for by in range(1, count)
+    ]
+
+
+def in_order(received, place):
     stacked = jnp.stack(received)
-    return jnp.stack([pick(stacked, place ^ i) for i in range(count)])
+    return jnp.stack([pick(stacked, place ^ i) for i in range(len(received))])
+
+
+def spectra_kernel(samples_ref, window_ref, table_ref, out_ref, filtered):
+    rows = samples_ref.shape[0]
+    frames = [
+        samples_ref[:, f * FCH : (f + 1) * FCH].astype(jnp.float32)
+        for f in range(SPEC + TAPS - 1)
+    ]
+    for t in range(SPEC):
+        total = window_ref[0:1, :] * frames[t]
+        for tap in range(1, TAPS):
+            total = total + window_ref[tap : tap + 1, :] * frames[t + tap]
+        upper = total.astype(jnp.bfloat16)
+        lower = (total - upper.astype(jnp.float32)).astype(jnp.bfloat16)
+        here = slice(t * rows, (t + 1) * rows)
+        filtered[here, 0:FCH] = upper
+        filtered[here, FCH : 2 * FCH] = upper
+        filtered[here, 2 * FCH : 3 * FCH] = lower
+    out_ref[...] = jnp.dot(
+        filtered[...], table_ref[...], preferred_element_type=jnp.float32
+    )
 
 
 def spectra(samples):
     rows = samples.shape[0]
-    frames = samples.astype(jnp.float32).reshape(rows, SPEC + TAPS - 1, FCH)
-    window = pfb_window()
-    filtered = window[0] * frames[:, 0:SPEC, :]
-    for tap in range(1, TAPS):
-        filtered = filtered + window[tap] * frames[:, tap : tap + SPEC, :]
-    return jnp.einsum(
-        "itp,pc->itc",
-        filtered,
-        dft_table(),
-        precision=lax.Precision.HIGH,
-        preferred_element_type=jnp.float32,
-    )
+    return pl.pallas_call(
+        spectra_kernel,
+        out_shape=jax.ShapeDtypeStruct((SPEC * rows, 2 * FCH), jnp.float32),
+        scratch_shapes=[pltpu.VMEM((SPEC * rows, 3 * FCH), jnp.bfloat16)],
+        name="spectra",
+    )(samples, jnp.asarray(pfb_window()), jnp.asarray(dft_table()))
+
+
+def quarters(parts, lane):
+    joined = parts[3]
+    for i in (2, 1, 0):
+        joined = jnp.where(lane < (i + 1) * AVG, parts[i], joined)
+    return joined
+
+
+def voltages_kernel(place_ref, spectra_ref, *refs):
+    gain_refs, out_refs, (gains, staged) = refs[0:4], refs[4:8], refs[8:]
+    rows = gain_refs[0].shape[1]
+    member = place_ref[0]
+    lanes = 4 * AVG
+    lane = lax.broadcasted_iota(jnp.int32, (rows, lanes), 1)
+    for by in range(4):
+        gains[member ^ by] = gain_refs[by][...]
+    for s in range(4):
+        gain = [
+            quarters(
+                [pltpu.roll(gains[m, part], (m - s) * AVG % lanes, 1) for m in range(4)], lane
+            )
+            for part in range(2)
+        ]
+        band = slice(s * lanes, (s + 1) * lanes)
+        for first in range(0, SPEC, 4):
+            turned_re, turned_im = [], []
+            for q in range(4):
+                here = slice((first + q) * rows, (first + q + 1) * rows)
+                real = spectra_ref[here, band]
+                imag = spectra_ref[here, FCH + s * lanes : FCH + (s + 1) * lanes]
+                volt_re = gain[0] * real - gain[1] * imag
+                volt_im = gain[0] * imag + gain[1] * real
+                turned_re.append(pltpu.roll(volt_re, q * AVG, 1) if q else volt_re)
+                turned_im.append(pltpu.roll(volt_im, q * AVG, 1) if q else volt_im)
+            for m in range(4):
+                for part, turned_part in enumerate((turned_re, turned_im)):
+                    values = quarters([turned_part[(i - m) % 4] for i in range(4)], lane)
+                    start = part * SPEC * AVG + first * AVG
+                    staged[m, s, :, start : start + lanes] = values.astype(jnp.bfloat16)
+    for by in range(4):
+        out_refs[by][...] = staged[member ^ by]
+
+
+def voltages(member, spectra_here, gain_parts):
+    rows = gain_parts[0].shape[1]
+    piece = jax.ShapeDtypeStruct((4, rows, 2 * SPEC * AVG), jnp.bfloat16)
+    vmem = pl.BlockSpec(memory_space=pltpu.VMEM)
+    return pl.pallas_call(
+        voltages_kernel,
+        in_specs=[pl.BlockSpec(memory_space=pltpu.SMEM)] + [vmem] * 5,
+        out_specs=[vmem] * 4,
+        out_shape=[piece] * 4,
+        scratch_shapes=[
+            pltpu.VMEM((4,) + gain_parts[0].shape, jnp.float32),
+            pltpu.VMEM((4,) + piece.shape, jnp.bfloat16),
+        ],
+        name="voltages",
+    )(member.reshape(1), spectra_here, *gain_parts)
 
 
 def turned(block):
@@ -82,21 +164,12 @@
     rows = samples.shape[0]
 
     gain_parts = input_gains.reshape(2, members, rows, bins * AVG).transpose(1, 0, 2, 3)
-    gains = exchange(gain_parts, team, member)
-    gains = gains.reshape(members, 2, rows, bins, AVG).transpose(1, 2, 3, 0, 4)
-
-    shaped = spectra(samples).reshape(rows, SPEC, 2, bins, members, AVG)
-    real, imag = shaped[:, :, 0], shaped[:, :, 1]
-    gain_re, gain_im = gains[0][:, None], gains[1][:, None]
-    volt_re = (gain_re * real - gain_im * imag).astype(jnp.bfloat16)
-    volt_im = (gain_re * imag + gain_im * real).astype(jnp.bfloat16)
-    packed = jnp.stack([volt_re, volt_im], axis=1)
-    packed = packed.transpose(4, 3, 0, 1, 2, 5)
-    packed = packed.reshape(members, bins, rows, 2 * SPEC * AVG)
-
-    by_member = exchange(packed, team, member)
+    gain_parts = exchange([pick(gain_parts, member ^ by) for by in range(members)], team)
+    by_member = in_order(
+        exchange(voltages(member, spectra(samples), gain_parts), team), member
+    )
     by_bin = by_member.transpose(1, 0, 2, 3).reshape(bins, members * rows, -1)
-    block = exchange(by_bin, "y", y_place)
+    block = in_order(exchange([pick(by_bin, y_place ^ by) for by in range(bins)], "y"), y_place)
     block = block.reshape(bins * members * rows, -1)
     height = block.shape[0]
 

time: 113 us -> 102 us (0.903)
  local copies, waits for them, and re-layouts: 15.1 us -> 4.41 us
  Pallas kernels: 0 us -> 6.7 us
  matrix products: 10.7 us -> 7.63 us
  other arithmetic: 5.37 us -> 2.55 us
    reshape x4 -> x0, local copies, waits for them, and re-layouts: 7.15 us -> none  [the longest x1 3.52 us: local(): shaped = spectra(samples).reshape(rows, SPEC, 2, bins, members, AVG)]
    pallas_call x0 -> x2, Pallas kernels: none -> 6.7 us  [the longest x1 4.16 us: spectra(): pl.pallas_call(spectra_kernel, out_shape=jax.ShapeDtypeStruct((SPEC * row...]
    slice x2 -> x0, local copies, waits for them, and re-layouts: 4.61 us -> none  [the longest x1 4.61 us: local(): real, imag = (shaped[:, :, 0], shaped[:, :, 1])]
    convert_element_type x1 -> x0, other arithmetic: 3.21 us -> none  [local(): volt_re = (gain_re * real - gain_im * imag).astype(jnp.bfloat16)]
    dot_general x1 -> x0, matrix products: 3.08 us -> none  [spectra(): jnp.einsum('itp,pc->itc', filtered, dft_table(), precision=lax.Precision....]
  transfers between devices with their start and end apart: 22 -> 22, of which waited for: 13 -> 13; matrix products, arithmetic and copies ran while one was open for 20% -> 9% of each run, Pallas kernels for 0% -> 4%
where the time goes in v2:
time: 102 us; the launch traced here: 101 us
  waiting for transfers between devices  45.7 us (45%)
  starting transfers between devices  33.1 us (32%)
  matrix products  7.63 us (7%)
  Pallas kernels  6.7 us (7%)
  local copies, waits for them, and re-layouts  4.41 us (4%)
  other arithmetic  2.55 us (2%)
    ppermute x3, waiting for transfers between devices, local(): behind = lax.ppermute(behind, 'z', ring_pairs(z_size, -1))  16.9 us
    ppermute x9, waiting for transfers between devices, exchange(): lax.ppermute(pieces[by], axis, xor_pairs(count, by))  13.6 us
    ppermute x9, starting transfers between devices, exchange(): lax.ppermute(pieces[by], axis, xor_pairs(count, by))  11 us
    ppermute x3, starting transfers between devices, local(): behind = lax.ppermute(behind, 'z', ring_pairs(z_size, -1))  10.9 us
    dot_general x16, matrix products, product(): jnp.einsum('rk,pk->rp', lhs, columns, preferred_element_type=jnp.float32)  7.63 us
    ppermute x4, waiting for transfers between devices, local(): given = lax.ppermute(jnp.stack(made), 'xl', ring_pairs(2, 1))  5.16 us
    ppermute x4, starting transfers between devices, local(): given = lax.ppermute(jnp.stack(made), 'xl', ring_pairs(2, 1))  4.39 us
    pallas_call x1, Pallas kernels, spectra(): pl.pallas_call(spectra_kernel, out_shape=jax.ShapeDtypeStruct((SPEC * row...  4.16 us
  transfers between devices with their start and end apart: 22, of which 13 were waited for; matrix products, arithmetic and copies ran while one was open for 9% of the time, Pallas kernels for 4%

profile of v2, /device:TPU:6, one launch (start us, length us, event | category | flops | bytes accessed | tf_op | source)
XLA Modules:
  0.0 100.6 jit_solution(2378873033405018896)
XLA Ops:
  1.9 1.4 %collective-permute-start.1 = (f32[2,16,128]{2,1,0:T(8,128)S(1)}, f32[2,16,128]{2,1,0:T(8,128)S(1)}, u32[]{:S(2)}, u32[]{:S(2)}) collective-permute-start(f32[2,16,128]{2,1,0:T(8,128)S(1)} %get-tuple-element.36), channel_id=1, source_target_pairs={{0,2},{1,3},{2,0},{3,1},{4,6},{5,7},{6,4},{7,5},{8,10},{9,11},{10,... | collective-permute-start | bytes 49160 | tf_op jit(solution)/shard_map/ppermute | solution.py:51
  3.3 2.0 %collective-permute-start.2 = (f32[2,16,128]{2,1,0:T(8,128)S(1)}, f32[2,16,128]{2,1,0:T(8,128)S(1)}, u32[]{:S(2)}, u32[]{:S(2)}) collective-permute-start(f32[2,16,128]{2,1,0:T(8,128)S(1)} %get-tuple-element.35), channel_id=1, source_target_pairs={{0,3},{1,2},{2,1},{3,0},{4,7},{5,6},{6,5},{7,4},{8,11},{9,10},{10,... | collective-permute-start | bytes 49160 | tf_op jit(solution)/shard_map/ppermute | solution.py:51
  5.2 4.2 %spectra.1.spectra_ref = f32[256,1024]{1,0:T(8,128)} custom-call(bf16[16,11776]{1,0:T(8,128)(2,1)} %samples_ref.1, f32[8,512]{1,0:T(8,128)} %constant.138.clone.window_ref, bf16[1536,1024]{1,0:T(8,128)(2,1)} %constant.139.clone.table_ref), custom_call_target="tpu_custom_call" | custom-call | tf_op jit(solution)/shard_map/spectra/pallas_call | solution.py:83
  10.0 2.5 %voltages.1 = (bf16[4,16,1024]{2,1,0:T(8,128)(2,1)}, bf16[4,16,1024]{2,1,0:T(8,128)(2,1)}, bf16[4,16,1024]{2,1,0:T(8,128)(2,1)}, bf16[4,16,1024]{2,1,0:T(8,128)(2,1)}) custom-call(s32[1]{0:T(128)} %bitcast.place_ref, f32[256,1024]{1,0:T(8,128)} %spectra.1.spectra_ref, f32[2,16,128]{2,1,0:T(8,128)} %get-tuple-element.38.refs_0_, f32[2,16,128]{2,1,0:T(8,128)} %copy-done.1, ...), custom_call_target="tpu_custom_call" | custom-call | tf_op jit(solution)/shard_map/voltages/pallas_call | solution.py:137
  12.6 1.3 %collective-permute-start.5 = (bf16[4,16,1024]{2,1,0:T(8,128)(2,1)}, bf16[4,16,1024]{2,1,0:T(8,128)(2,1)S(1)}, u32[]{:S(2)}, u32[]{:S(2)}) collective-permute-start(bf16[4,16,1024]{2,1,0:T(8,128)(2,1)} %get-tuple-element.12), channel_id=1, source_target_pairs={{0,3},{1,2},{2,1},{3,0},{4,7},{5,6},{6,5},{7,4},{8,11},{9,10},{10,... | collective-permute-start | bytes 393224 | tf_op jit(solution)/shard_map/ppermute | solution.py:51
  13.9 2.1 %collective-permute-start.4 = (bf16[4,16,1024]{2,1,0:T(8,128)(2,1)}, bf16[4,16,1024]{2,1,0:T(8,128)(2,1)S(1)}, u32[]{:S(2)}, u32[]{:S(2)}) collective-permute-start(bf16[4,16,1024]{2,1,0:T(8,128)(2,1)} %get-tuple-element.11), channel_id=1, source_target_pairs={{0,2},{1,3},{2,0},{3,1},{4,6},{5,7},{6,4},{7,5},{8,10},{9,11},{10,... | collective-permute-start | bytes 393224 | tf_op jit(solution)/shard_map/ppermute | solution.py:51
  16.0 3.7 %collective-permute-done.5 = bf16[4,16,1024]{2,1,0:T(8,128)(2,1)S(1)} collective-permute-done((bf16[4,16,1024]{2,1,0:T(8,128)(2,1)}, bf16[4,16,1024]{2,1,0:T(8,128)(2,1)S(1)}, u32[]{:S(2)}, u32[]{:S(2)}) %collective-permute-start.5) | collective-permute-done | bytes 131104 | tf_op jit(solution)/shard_map/ppermute | solution.py:51
  19.7 3.2 %collective-permute-done.4 = bf16[4,16,1024]{2,1,0:T(8,128)(2,1)S(1)} collective-permute-done((bf16[4,16,1024]{2,1,0:T(8,128)(2,1)}, bf16[4,16,1024]{2,1,0:T(8,128)(2,1)S(1)}, u32[]{:S(2)}, u32[]{:S(2)}) %collective-permute-start.4) | collective-permute-done | bytes 131104 | tf_op jit(solution)/shard_map/ppermute | solution.py:51
  24.1 3.1 %collective-permute-start.8 = (bf16[64,1024]{1,0:T(8,128)(2,1)S(1)}, bf16[64,1024]{1,0:T(8,128)(2,1)S(1)}, u32[]{:S(2)}, u32[]{:S(2)}) collective-permute-start(bf16[64,1024]{1,0:T(8,128)(2,1)S(1)} %get-tuple-element.28), channel_id=1, source_target_pairs={{0,12},{4,8},{8,4},{12,0},{1,13},{5,9},{9,5},{13,1},{2,14},{6,10},... | collective-permute-start | bytes 393224 | tf_op jit(solution)/shard_map/ppermute | solution.py:51
  28.3 4.4 %collective-permute-done.8 = bf16[64,1024]{1,0:T(8,128)(2,1)S(1)} collective-permute-done((bf16[64,1024]{1,0:T(8,128)(2,1)S(1)}, bf16[64,1024]{1,0:T(8,128)(2,1)S(1)}, u32[]{:S(2)}, u32[]{:S(2)}) %collective-permute-start.8) | collective-permute-done | bytes 131104 | tf_op jit(solution)/shard_map/ppermute | solution.py:51
  32.7 2.3 %collective-permute-done.7 = bf16[64,1024]{1,0:T(8,128)(2,1)S(1)} collective-permute-done((bf16[64,1024]{1,0:T(8,128)(2,1)S(1)}, bf16[64,1024]{1,0:T(8,128)(2,1)S(1)}, u32[]{:S(2)}, u32[]{:S(2)}) %collective-permute-start.7) | collective-permute-done | bytes 131104 | tf_op jit(solution)/shard_map/ppermute | solution.py:51
  36.1 1.9 %collective-permute-start.10 = (bf16[256,1024]{1,0:T(8,128)(2,1)S(1)}, bf16[256,1024]{1,0:T(8,128)(2,1)S(1)}, u32[]{:S(2)}, u32[]{:S(2)}) collective-permute-start(bf16[256,1024]{1,0:T(8,128)(2,1)S(1)} %bitcast.80), channel_id=1, source_target_pairs={{0,16},{16,32},{32,48},{48,64},{64,80},{80,96},{96,112},{112,0},{1... | collective-permute-start | bytes 1572872 | tf_op jit(solution)/shard_map/ppermute | solution.py:198
  38.0 3.9 %collective-permute-start.11 = (bf16[256,1024]{1,0:T(8,128)(2,1)S(1)}, bf16[256,1024]{1,0:T(8,128)(2,1)S(1)}, u32[]{:S(2)}, u32[]{:S(2)}) collective-permute-start(bf16[256,1024]{1,0:T(8,128)(2,1)S(1)} %bitcast.81), channel_id=1, source_target_pairs={{0,112},{16,0},{32,16},{48,32},{64,48},{80,64},{96,80},{112,96},{1... | collective-permute-start | bytes 1572872 | tf_op jit(solution)/shard_map/ppermute | solution.py:199
  43.5 3.4 %collective-permute-done.9 = bf16[256,1024]{1,0:T(8,128)(2,1)S(1)} collective-permute-done((bf16[256,1024]{1,0:T(8,128)(2,1)S(1)}, bf16[256,1024]{1,0:T(8,128)(2,1)S(1)}, u32[]{:S(2)}, u32[]{:S(2)}) %collective-permute-start.9) | collective-permute-done | bytes 524320 | tf_op jit(solution)/shard_map/ppermute | solution.py:176
  47.0 3.9 %collective-permute-done.11 = bf16[256,1024]{1,0:T(8,128)(2,1)S(1)} collective-permute-done((bf16[256,1024]{1,0:T(8,128)(2,1)S(1)}, bf16[256,1024]{1,0:T(8,128)(2,1)S(1)}, u32[]{:S(2)}, u32[]{:S(2)}) %collective-permute-start.11) | collective-permute-done | bytes 524320 | tf_op jit(solution)/shard_map/ppermute | solution.py:199
  54.0 3.7 %collective-permute-start.14 = (bf16[256,1024]{1,0:T(8,128)(2,1)S(1)}, bf16[256,1024]{1,0:T(8,128)(2,1)S(1)}, u32[]{:S(2)}, u32[]{:S(2)}) collective-permute-start(bf16[256,1024]{1,0:T(8,128)(2,1)S(1)} %collective-permute-done.11), channel_id=1, source_target_pairs={{0,112},{16,0},{32,16},{48,32},{64,48},{80,64},{96,80},{112,96},{1... | collective-permute-start | bytes 1572872 | tf_op jit(solution)/shard_map/ppermute | solution.py:199
  58.9 6.5 %collective-permute-done.14 = bf16[256,1024]{1,0:T(8,128)(2,1)S(1)} collective-permute-done((bf16[256,1024]{1,0:T(8,128)(2,1)S(1)}, bf16[256,1024]{1,0:T(8,128)(2,1)S(1)}, u32[]{:S(2)}, u32[]{:S(2)}) %collective-permute-start.14) | collective-permute-done | bytes 524320 | tf_op jit(solution)/shard_map/ppermute | solution.py:199
  65.9 3.5 %collective-permute-done.13 = bf16[256,1024]{1,0:T(8,128)(2,1)S(1)} collective-permute-done((bf16[256,1024]{1,0:T(8,128)(2,1)S(1)}, bf16[256,1024]{1,0:T(8,128)(2,1)S(1)}, u32[]{:S(2)}, u32[]{:S(2)}) %collective-permute-start.13) | collective-permute-done | bytes 524320 | tf_op jit(solution)/shard_map/ppermute | solution.py:198
  71.6 3.2 %collective-permute-start.17 = (bf16[256,1024]{1,0:T(8,128)(2,1)S(1)}, bf16[256,1024]{1,0:T(8,128)(2,1)S(1)}, u32[]{:S(2)}, u32[]{:S(2)}) collective-permute-start(bf16[256,1024]{1,0:T(8,128)(2,1)S(1)} %collective-permute-done.14), channel_id=1, source_target_pairs={{0,112},{16,0},{32,16},{48,32},{64,48},{80,64},{96,80},{112,96},{1... | collective-permute-start | bytes 1572872 | tf_op jit(solution)/shard_map/ppermute | solution.py:199
  75.5 6.4 %collective-permute-done.17 = bf16[256,1024]{1,0:T(8,128)(2,1)S(1)} collective-permute-done((bf16[256,1024]{1,0:T(8,128)(2,1)S(1)}, bf16[256,1024]{1,0:T(8,128)(2,1)S(1)}, u32[]{:S(2)}, u32[]{:S(2)}) %collective-permute-start.17) | collective-permute-done | bytes 524320 | tf_op jit(solution)/shard_map/ppermute | solution.py:199
  82.9 1.7 %collective-permute-start.18 = (bf16[2,512,256]{2,1,0:T(8,128)(2,1)S(1)}, bf16[2,512,256]{2,1,0:T(8,128)(2,1)S(1)}, u32[]{:S(2)}, u32[]{:S(2)}) collective-permute-start(bf16[2,512,256]{2,1,0:T(8,128)(2,1)S(1)} %pad_maximum_fusion.5), channel_id=1, source_target_pairs={{0,128},{128,0},{1,129},{129,1},{2,130},{130,2},{3,131},{131,3},{4... | collective-permute-start | bytes 1572872 | tf_op jit(solution)/shard_map/ppermute | solution.py:207
  84.8 3.8 %collective-permute-start.20 = (bf16[128,1024]{1,0:T(8,128)(2,1)S(1)}, bf16[128,1024]{1,0:T(8,128)(2,1)S(1)}, u32[]{:S(2)}, u32[]{:S(2)}) collective-permute-start(bf16[128,1024]{1,0:T(8,128)(2,1)S(1)} %slice.59), channel_id=1, source_target_pairs={{0,112},{16,0},{32,16},{48,32},{64,48},{80,64},{96,80},{112,96},{1... | collective-permute-start | bytes 786440 | tf_op jit(solution)/shard_map/ppermute | solution.py:204
  89.8 2.9 %collective-permute-done.19 = bf16[128,1024]{1,0:T(8,128)(2,1)S(1)} collective-permute-done((bf16[128,1024]{1,0:T(8,128)(2,1)S(1)}, bf16[128,1024]{1,0:T(8,128)(2,1)S(1)}, u32[]{:S(2)}, u32[]{:S(2)}) %collective-permute-start.19) | collective-permute-done | bytes 262176 | tf_op jit(solution)/shard_map/ppermute | solution.py:203
  95.3 4.5 %collective-permute-done.21 = bf16[1,512,256]{2,1,0:T(8,128)(2,1)S(1)} collective-permute-done((bf16[1,512,256]{2,1,0:T(8,128)(2,1)S(1)}, bf16[1,512,256]{2,1,0:T(8,128)(2,1)S(1)}, u32[]{:S(2)}, u32[]{:S(2)}) %collective-permute-start.21) | collective-permute-done | bytes 262176 | tf_op jit(solution)/shard_map/ppermute | solution.py:207
  (86 shorter events, 20.5 us)
Async XLA Ops:
  1.9 7.5 %collective-permute-start = (f32[2,16,128]{2,1,0:T(8,128)S(1)}, f32[2,16,128]{2,1,0:T(8,128)S(1)}, u32[]{:S(2)}, u32[]{:S(2)}) collective-permute-start(f32[2,16,128]{2,1,0:T(8,128)S(1)} %get-tuple-element.37), channel_id=1, source_target_pairs={{0,1},{1,0},{2,3},{3,2},{4,5},{5,4},{6,7},{7,6},{8,9},{9,8},{10,11... | collective-permute-start | bytes 49160 | tf_op jit(solution)/shard_map/ppermute | solution.py:51
  1.9 7.5 %collective-permute-start.1 = (f32[2,16,128]{2,1,0:T(8,128)S(1)}, f32[2,16,128]{2,1,0:T(8,128)S(1)}, u32[]{:S(2)}, u32[]{:S(2)}) collective-permute-start(f32[2,16,128]{2,1,0:T(8,128)S(1)} %get-tuple-element.36), channel_id=1, source_target_pairs={{0,2},{1,3},{2,0},{3,1},{4,6},{5,7},{6,4},{7,5},{8,10},{9,11},{10,... | collective-permute-start | bytes 49160 | tf_op jit(solution)/shard_map/ppermute | solution.py:51
  3.3 6.1 %collective-permute-start.2 = (f32[2,16,128]{2,1,0:T(8,128)S(1)}, f32[2,16,128]{2,1,0:T(8,128)S(1)}, u32[]{:S(2)}, u32[]{:S(2)}) collective-permute-start(f32[2,16,128]{2,1,0:T(8,128)S(1)} %get-tuple-element.35), channel_id=1, source_target_pairs={{0,3},{1,2},{2,1},{3,0},{4,7},{5,6},{6,5},{7,4},{8,11},{9,10},{10,... | collective-permute-start | bytes 49160 | tf_op jit(solution)/shard_map/ppermute | solution.py:51
  9.4 0.6 copy-start.2
  12.6 7.1 %collective-permute-start.5 = (bf16[4,16,1024]{2,1,0:T(8,128)(2,1)}, bf16[4,16,1024]{2,1,0:T(8,128)(2,1)S(1)}, u32[]{:S(2)}, u32[]{:S(2)}) collective-permute-start(bf16[4,16,1024]{2,1,0:T(8,128)(2,1)} %get-tuple-element.12), channel_id=1, source_target_pairs={{0,3},{1,2},{2,1},{3,0},{4,7},{5,6},{6,5},{7,4},{8,11},{9,10},{10,... | collective-permute-start | bytes 393224 | tf_op jit(solution)/shard_map/ppermute | solution.py:51
  13.9 9.0 %collective-permute-start.4 = (bf16[4,16,1024]{2,1,0:T(8,128)(2,1)}, bf16[4,16,1024]{2,1,0:T(8,128)(2,1)S(1)}, u32[]{:S(2)}, u32[]{:S(2)}) collective-permute-start(bf16[4,16,1024]{2,1,0:T(8,128)(2,1)} %get-tuple-element.11), channel_id=1, source_target_pairs={{0,2},{1,3},{2,0},{3,1},{4,6},{5,7},{6,4},{7,5},{8,10},{9,11},{10,... | collective-permute-start | bytes 393224 | tf_op jit(solution)/shard_map/ppermute | solution.py:51
  16.0 6.9 %collective-permute-start.3 = (bf16[4,16,1024]{2,1,0:T(8,128)(2,1)}, bf16[4,16,1024]{2,1,0:T(8,128)(2,1)S(1)}, u32[]{:S(2)}, u32[]{:S(2)}) collective-permute-start(bf16[4,16,1024]{2,1,0:T(8,128)(2,1)} %get-tuple-element.10), channel_id=1, source_target_pairs={{0,1},{1,0},{2,3},{3,2},{4,5},{5,4},{6,7},{7,6},{8,9},{9,8},{10,11... | collective-permute-start | bytes 393224 | tf_op jit(solution)/shard_map/ppermute | solution.py:51
  24.1 8.6 %collective-permute-start.8 = (bf16[64,1024]{1,0:T(8,128)(2,1)S(1)}, bf16[64,1024]{1,0:T(8,128)(2,1)S(1)}, u32[]{:S(2)}, u32[]{:S(2)}) collective-permute-start(bf16[64,1024]{1,0:T(8,128)(2,1)S(1)} %get-tuple-element.28), channel_id=1, source_target_pairs={{0,12},{4,8},{8,4},{12,0},{1,13},{5,9},{9,5},{13,1},{2,14},{6,10},... | collective-permute-start | bytes 393224 | tf_op jit(solution)/shard_map/ppermute | solution.py:51
  27.2 7.8 %collective-permute-start.7 = (bf16[64,1024]{1,0:T(8,128)(2,1)S(1)}, bf16[64,1024]{1,0:T(8,128)(2,1)S(1)}, u32[]{:S(2)}, u32[]{:S(2)}) collective-permute-start(bf16[64,1024]{1,0:T(8,128)(2,1)S(1)} %get-tuple-element.29), channel_id=1, source_target_pairs={{0,8},{4,12},{8,0},{12,4},{1,9},{5,13},{9,1},{13,5},{2,10},{6,14},... | collective-permute-start | bytes 393224 | tf_op jit(solution)/shard_map/ppermute | solution.py:51
  27.8 7.1 %collective-permute-start.6 = (bf16[64,1024]{1,0:T(8,128)(2,1)S(1)}, bf16[64,1024]{1,0:T(8,128)(2,1)S(1)}, u32[]{:S(2)}, u32[]{:S(2)}) collective-permute-start(bf16[64,1024]{1,0:T(8,128)(2,1)S(1)} %get-tuple-element.30), channel_id=1, source_target_pairs={{0,4},{4,0},{8,12},{12,8},{1,5},{5,1},{9,13},{13,9},{2,6},{6,2},{1... | collective-permute-start | bytes 393224 | tf_op jit(solution)/shard_map/ppermute | solution.py:51
  35.2 11.8 %collective-permute-start.9 = (bf16[256,1024]{1,0:T(8,128)(2,1)S(1)}, bf16[256,1024]{1,0:T(8,128)(2,1)S(1)}, u32[]{:S(2)}, u32[]{:S(2)}) collective-permute-start(bf16[256,1024]{1,0:T(8,128)(2,1)S(1)} %bitcast.79), channel_id=1, source_target_pairs={{0,128},{128,0},{1,129},{129,1},{2,130},{130,2},{3,131},{131,3},{4... | collective-permute-start | bytes 1572872 | tf_op jit(solution)/shard_map/ppermute | solution.py:176
  36.1 15.6 %collective-permute-start.10 = (bf16[256,1024]{1,0:T(8,128)(2,1)S(1)}, bf16[256,1024]{1,0:T(8,128)(2,1)S(1)}, u32[]{:S(2)}, u32[]{:S(2)}) collective-permute-start(bf16[256,1024]{1,0:T(8,128)(2,1)S(1)} %bitcast.80), channel_id=1, source_target_pairs={{0,16},{16,32},{32,48},{48,64},{64,80},{80,96},{96,112},{112,0},{1... | collective-permute-start | bytes 1572872 | tf_op jit(solution)/shard_map/ppermute | solution.py:198
  38.0 12.9 %collective-permute-start.11 = (bf16[256,1024]{1,0:T(8,128)(2,1)S(1)}, bf16[256,1024]{1,0:T(8,128)(2,1)S(1)}, u32[]{:S(2)}, u32[]{:S(2)}) collective-permute-start(bf16[256,1024]{1,0:T(8,128)(2,1)S(1)} %bitcast.81), channel_id=1, source_target_pairs={{0,112},{16,0},{32,16},{48,32},{64,48},{80,64},{96,80},{112,96},{1... | collective-permute-start | bytes 1572872 | tf_op jit(solution)/shard_map/ppermute | solution.py:199
  52.2 18.7 %collective-permute-start.12 = (bf16[2,512,256]{2,1,0:T(8,128)(2,1)S(1)}, bf16[2,512,256]{2,1,0:T(8,128)(2,1)S(1)}, u32[]{:S(2)}, u32[]{:S(2)}) collective-permute-start(bf16[2,512,256]{2,1,0:T(8,128)(2,1)S(1)} %pad_maximum_fusion.3), channel_id=1, source_target_pairs={{0,128},{128,0},{1,129},{129,1},{2,130},{130,2},{3,131},{131,3},{4... | collective-permute-start | bytes 1572872 | tf_op jit(solution)/shard_map/ppermute | solution.py:207
  54.0 11.5 %collective-permute-start.14 = (bf16[256,1024]{1,0:T(8,128)(2,1)S(1)}, bf16[256,1024]{1,0:T(8,128)(2,1)S(1)}, u32[]{:S(2)}, u32[]{:S(2)}) collective-permute-start(bf16[256,1024]{1,0:T(8,128)(2,1)S(1)} %collective-permute-done.11), channel_id=1, source_target_pairs={{0,112},{16,0},{32,16},{48,32},{64,48},{80,64},{96,80},{112,96},{1... | collective-permute-start | bytes 1572872 | tf_op jit(solution)/shard_map/ppermute | solution.py:199
  58.2 11.3 %collective-permute-start.13 = (bf16[256,1024]{1,0:T(8,128)(2,1)S(1)}, bf16[256,1024]{1,0:T(8,128)(2,1)S(1)}, u32[]{:S(2)}, u32[]{:S(2)}) collective-permute-start(bf16[256,1024]{1,0:T(8,128)(2,1)S(1)} %collective-permute-done.10), channel_id=1, source_target_pairs={{0,16},{16,32},{32,48},{48,64},{64,80},{80,96},{96,112},{112,0},{1... | collective-permute-start | bytes 1572872 | tf_op jit(solution)/shard_map/ppermute | solution.py:198
  70.0 18.6 %collective-permute-start.15 = (bf16[2,512,256]{2,1,0:T(8,128)(2,1)S(1)}, bf16[2,512,256]{2,1,0:T(8,128)(2,1)S(1)}, u32[]{:S(2)}, u32[]{:S(2)}) collective-permute-start(bf16[2,512,256]{2,1,0:T(8,128)(2,1)S(1)} %pad_maximum_fusion.4), channel_id=1, source_target_pairs={{0,128},{128,0},{1,129},{129,1},{2,130},{130,2},{3,131},{131,3},{4... | collective-permute-start | bytes 1572872 | tf_op jit(solution)/shard_map/ppermute | solution.py:207
  71.5 10.8 %collective-permute-start.16 = (bf16[256,1024]{1,0:T(8,128)(2,1)S(1)}, bf16[256,1024]{1,0:T(8,128)(2,1)S(1)}, u32[]{:S(2)}, u32[]{:S(2)}) collective-permute-start(bf16[256,1024]{1,0:T(8,128)(2,1)S(1)} %collective-permute-done.13), channel_id=1, source_target_pairs={{0,16},{16,32},{32,48},{48,64},{64,80},{80,96},{96,112},{112,0},{1... | collective-permute-start | bytes 1572872 | tf_op jit(solution)/shard_map/ppermute | solution.py:198
  71.6 10.3 %collective-permute-start.17 = (bf16[256,1024]{1,0:T(8,128)(2,1)S(1)}, bf16[256,1024]{1,0:T(8,128)(2,1)S(1)}, u32[]{:S(2)}, u32[]{:S(2)}) collective-permute-start(bf16[256,1024]{1,0:T(8,128)(2,1)S(1)} %collective-permute-done.14), channel_id=1, source_target_pairs={{0,112},{16,0},{32,16},{48,32},{64,48},{80,64},{96,80},{112,96},{1... | collective-permute-start | bytes 1572872 | tf_op jit(solution)/shard_map/ppermute | solution.py:199
  82.9 12.1 %collective-permute-start.18 = (bf16[2,512,256]{2,1,0:T(8,128)(2,1)S(1)}, bf16[2,512,256]{2,1,0:T(8,128)(2,1)S(1)}, u32[]{:S(2)}, u32[]{:S(2)}) collective-permute-start(bf16[2,512,256]{2,1,0:T(8,128)(2,1)S(1)} %pad_maximum_fusion.5), channel_id=1, source_target_pairs={{0,128},{128,0},{1,129},{129,1},{2,130},{130,2},{3,131},{131,3},{4... | collective-permute-start | bytes 1572872 | tf_op jit(solution)/shard_map/ppermute | solution.py:207
  84.7 8.1 %collective-permute-start.19 = (bf16[128,1024]{1,0:T(8,128)(2,1)S(1)}, bf16[128,1024]{1,0:T(8,128)(2,1)S(1)}, u32[]{:S(2)}, u32[]{:S(2)}) collective-permute-start(bf16[128,1024]{1,0:T(8,128)(2,1)S(1)} %slice.58), channel_id=1, source_target_pairs={{0,16},{16,32},{32,48},{48,64},{64,80},{80,96},{96,112},{112,0},{1... | collective-permute-start | bytes 786440 | tf_op jit(solution)/shard_map/ppermute | solution.py:203
  84.8 8.0 %collective-permute-start.20 = (bf16[128,1024]{1,0:T(8,128)(2,1)S(1)}, bf16[128,1024]{1,0:T(8,128)(2,1)S(1)}, u32[]{:S(2)}, u32[]{:S(2)}) collective-permute-start(bf16[128,1024]{1,0:T(8,128)(2,1)S(1)} %slice.59), channel_id=1, source_target_pairs={{0,112},{16,0},{32,16},{48,32},{64,48},{80,64},{96,80},{112,96},{1... | collective-permute-start | bytes 786440 | tf_op jit(solution)/shard_map/ppermute | solution.py:204
  93.3 6.5 %collective-permute-start.21 = (bf16[1,512,256]{2,1,0:T(8,128)(2,1)S(1)}, bf16[1,512,256]{2,1,0:T(8,128)(2,1)S(1)}, u32[]{:S(2)}, u32[]{:S(2)}) collective-permute-start(bf16[1,512,256]{2,1,0:T(8,128)(2,1)S(1)} %fusion.7), channel_id=1, source_target_pairs={{0,128},{128,0},{1,129},{129,1},{2,130},{130,2},{3,131},{131,3},{4... | collective-permute-start | bytes 786440 | tf_op jit(solution)/shard_map/ppermute | solution.py:207
  95.3 4.5 %copy-start = (f32[1,1,2,256,4096]{4,3,2,1,0:T(8,128)}, f32[1,1,2,256,4096]{4,3,2,1,0:T(8,128)S(1)}, u32[]{:S(2)}) copy-start(f32[1,1,2,256,4096]{4,3,2,1,0:T(8,128)S(1)} %constant_dynamic-update-slice_fusion) | copy-start | bytes 25165828
  (2 other events, 1.2 us)

commit v3 on v2

v3 whole, which is shorter than its diff:
```python
import functools
import math

import jax
import jax.numpy as jnp
import ml_dtypes
import numpy as np
from jax import lax
from jax.experimental import pallas as pl
from jax.experimental.pallas import tpu as pltpu
from jax.sharding import Mesh
from jax.sharding import PartitionSpec as P

FCH = 512
TAPS = 8
AVG = 32
SPEC = 16
SCALE = 1.0 / (AVG * SPEC)


ANY = pl.BlockSpec(memory_space=pl.ANY)
VMEM = pl.BlockSpec(memory_space=pltpu.VMEM)
SMEM = pl.BlockSpec(memory_space=pltpu.SMEM)


def room(mebibytes):
    return pltpu.CompilerParams(vmem_limit_bytes=mebibytes << 20)


def ring_pairs(count, by):
    return [(i, (i + by) % count) for i in range(count)]


def xor_pairs(count, by):
    return [(i, i ^ by) for i in range(count)]


def pfb_window():
    position = np.arange(TAPS * FCH) + 0.5
    taper = np.sin(np.pi * position / (TAPS * FCH)) ** 2
    table = np.sinc(position / FCH - TAPS / 2) * taper
    return table.reshape(TAPS, FCH).astype(np.float32)


def dft_table():
    position = np.arange(FCH)
    angle = (position[:, None] * position[None, :] % FCH) * (2.0 * math.pi / FCH)
    table = np.concatenate([np.cos(angle), -np.sin(angle)], axis=1) / math.sqrt(FCH)
    upper = table.astype(ml_dtypes.bfloat16)
    lower = (table - upper.astype(np.float64)).astype(ml_dtypes.bfloat16)
    return np.concatenate([upper, lower], axis=0)


def pick(stacked, slot):
    return lax.dynamic_index_in_dim(stacked, slot, 0, keepdims=False)


def in_vmem(array):
    return pltpu.with_memory_space_constraint(array, pltpu.VMEM)


def after(array, *others):
    return lax.optimization_barrier((array, *others))[0]


def exchange(pieces, axis):
    count = len(pieces)
    return [pieces[0]] + [
        lax.ppermute(pieces[by], axis, xor_pairs(count, by)) for by in range(1, count)
    ]


def spectra_kernel(samples_any, window_ref, table_any, out_ref, samples_ref, table_ref, *more):
    upper, lower, sems = more
    samples_copy = pltpu.make_async_copy(samples_any, samples_ref, sems.at[0])
    table_copy = pltpu.make_async_copy(table_any, table_ref, sems.at[1])
    samples_copy.start()
    table_copy.start()
    samples_copy.wait()
    rows = samples_ref.shape[0]
    frames = [
        samples_ref[:, f * FCH : (f + 1) * FCH].astype(jnp.float32)
        for f in range(SPEC + TAPS - 1)
    ]
    for t in range(SPEC):
        total = window_ref[0:1, :] * frames[t]
        for tap in range(1, TAPS):
            total = total + window_ref[tap : tap + 1, :] * frames[t + tap]
        here = slice(t * rows, (t + 1) * rows)
        rounded = total.astype(jnp.bfloat16)
        upper[here, :] = rounded
        lower[here, :] = (total - rounded.astype(jnp.float32)).astype(jnp.bfloat16)

    def dot(lhs, rhs):
        return jnp.dot(lhs, rhs, preferred_element_type=jnp.float32)

    table_copy.wait()
    out_ref[...] = (
        dot(upper[...], table_ref[0:FCH, :])
        + dot(upper[...], table_ref[FCH : 2 * FCH, :])
        + dot(lower[...], table_ref[0:FCH, :])
    )


def spectra(samples):
    rows = samples.shape[0]
    table = jnp.asarray(dft_table())
    part = pltpu.VMEM((SPEC * rows, FCH), jnp.bfloat16)
    return pl.pallas_call(
        spectra_kernel,
        in_specs=[ANY, VMEM, ANY],
        out_shape=pltpu.VMEM((SPEC * rows, 2 * FCH), jnp.float32),
        scratch_shapes=[
            pltpu.VMEM(samples.shape, samples.dtype),
            pltpu.VMEM(table.shape, table.dtype),
            part,
            part,
            pltpu.SemaphoreType.DMA((2,)),
        ],
        compiler_params=room(20),
        name="spectra",
    )(
        pltpu.with_memory_space_constraint(samples, pltpu.HBM),
        jnp.asarray(pfb_window()),
        pltpu.with_memory_space_constraint(table, pltpu.HBM),
    )


def quarters(parts, lane):
    joined = parts[3]
    for i in (2, 1, 0):
        joined = jnp.where(lane < (i + 1) * AVG, parts[i], joined)
    return joined


def voltages_kernel(place_ref, spectra_ref, *refs):
    gain_refs, out_ref, gains = refs[0:4], refs[4], refs[5]
    rows = gain_refs[0].shape[1]
    member = place_ref[0]
    lanes = 4 * AVG
    lane = lax.broadcasted_iota(jnp.int32, (rows, lanes), 1)
    for by in range(4):
        gains[member ^ by] = gain_refs[by][...]
    for s in range(4):
        gain = [
            quarters(
                [pltpu.roll(gains[m, part], (m - s) * AVG % lanes, 1) for m in range(4)], lane
            )
            for part in range(2)
        ]
        band = slice(s * lanes, (s + 1) * lanes)
        for first in range(0, SPEC, 4):
            turned_re, turned_im = [], []
            for q in range(4):
                here = slice((first + q) * rows, (first + q + 1) * rows)
                real = spectra_ref[here, band]
                imag = spectra_ref[here, FCH + s * lanes : FCH + (s + 1) * lanes]
                volt_re = gain[0] * real - gain[1] * imag
                volt_im = gain[0] * imag + gain[1] * real
                turned_re.append(pltpu.roll(volt_re, q * AVG, 1) if q else volt_re)
                turned_im.append(pltpu.roll(volt_im, q * AVG, 1) if q else volt_im)
            for m in range(4):
                for part, turned_part in enumerate((turned_re, turned_im)):
                    values = quarters([turned_part[(i - m) % 4] for i in range(4)], lane)
                    start = (part * SPEC + first) * AVG
                    out_ref[s, m, :, start : start + lanes] = values.astype(jnp.bfloat16)


def voltages(member, spectra_here, gain_parts):
    rows = gain_parts[0].shape[1]
    vmem = pl.BlockSpec(memory_space=pltpu.VMEM)
    return pl.pallas_call(
        voltages_kernel,
        in_specs=[pl.BlockSpec(memory_space=pltpu.SMEM)] + [vmem] * 5,
        out_specs=vmem,
        out_shape=pltpu.VMEM((4, 4, rows, 2 * SPEC * AVG), jnp.bfloat16),
        scratch_shapes=[pltpu.VMEM((4,) + gain_parts[0].shape, jnp.float32)],
        compiler_params=room(12),
        name="voltages",
    )(member.reshape(1), in_vmem(spectra_here), *[in_vmem(part) for part in gain_parts])


def turned(block):
    half = block.shape[1] // 2
    return jnp.concatenate([block[:, half:], -block[:, :half]], axis=1)


def local(samples, input_gains):
    team = ("xh", "c")
    member = lax.axis_index(team)
    y_place = lax.axis_index("y")
    z_place = lax.axis_index("z")
    x_place = lax.axis_index("xl")
    members = lax.axis_size(team)
    bins = input_gains.shape[2]
    z_size = lax.axis_size("z")
    rows = samples.shape[0]

    gain_parts = input_gains.reshape(2, members, rows, bins * AVG).transpose(1, 0, 2, 3)
    gain_parts = exchange([pick(gain_parts, member ^ by) for by in range(members)], team)
    formed = voltages(member, spectra(samples), gain_parts)
    formed = formed.reshape(bins * members, rows, -1)
    block = lax.all_to_all(formed, ("y", "xh", "c"), 0, 0, tiled=True)
    block = block.reshape(bins * members * rows, -1)
    height = block.shape[0]
    half = height // 2
    far = 1 - x_place

    def across(piece):
        return lax.ppermute(piece, "xl", ring_pairs(2, 1))

    def onward(piece, by):
        return lax.ppermute(piece, "z", ring_pairs(z_size, by))

    def product(lhs, columns):
        return (
            jnp.einsum("rk,pk->rp", lhs, columns, preferred_element_type=jnp.float32) * SCALE
        )

    def put(values, x, by):
        nonlocal visibility
        values = values.astype(jnp.float32).reshape(2, height, -1)
        nought = jnp.zeros((), jnp.int32)
        start = (x * z_size + (z_place + by) % z_size) * height
        visibility = lax.dynamic_update_slice(visibility, values, (nought, nought, start))

    ahead, behind = {1: onward(block, 1)}, {1: onward(block, -1)}
    other = across(block)
    for step in range(2, z_size // 2):
        ahead[step] = onward(ahead[step - 1], 1)
        behind[step] = onward(behind[step - 1], -1)
    opposite = jnp.concatenate(
        [onward(ahead[step][:half], 1), onward(behind[step][half:], -1)], axis=0
    )

    own_left = jnp.concatenate([block, turned(block)], axis=0)
    other_left = jnp.concatenate([other, turned(other)], axis=0)

    def swap(columns, *waits):
        made = product(other_left, columns).astype(jnp.bfloat16)
        return across(after(made, *waits))

    blocks = []

    def own(columns, by, *waits, x=x_place):
        blocks.append((product(own_left, after(columns, *waits)), x, by))

    own(block, 0)
    given_a1, given_b1 = swap(ahead[1]), swap(behind[1])
    own(other, 0, x=far)
    own(ahead[1], -1)
    given_a2, given_b2 = swap(ahead[2], given_a1), swap(behind[2], given_b1)
    own(behind[1], 1)
    own(ahead[2], -2)
    own(behind[2], 2)
    given_a3, given_b3 = swap(ahead[3], given_a2), swap(behind[3], given_b2)
    own(ahead[3], -3)
    own(behind[3], 3)
    given_4 = swap(opposite, given_a3)
    own(opposite, 4)
    visibility = jnp.zeros((2, height, height * z_size * 2), jnp.float32)
    blocks[0] = (after(blocks[0][0], given_a3), *blocks[0][1:])
    for values, x, by in blocks:
        put(values, x, by)
    put(given_a1, far, -1)
    put(given_b1, far, 1)
    put(given_a2, far, -2)
    put(given_b2, far, 2)
    put(given_a3, far, -3)
    put(given_b3, far, 3)
    put(given_4, far, 4)
    return visibility[None, None]


def solution(mesh):
    fine = Mesh(
        mesh.devices.reshape(2, 8, 4, 2, 2), ("xl", "z", "y", "xh", "c")
    )
    everything = ("xl", "z", "y", "xh", "c")
    return jax.shard_map(
        local,
        mesh=fine,
        in_specs=(P(everything, None), P(None, ("xl", "z", "y"), None, ("xh", "c"))),
        out_specs=P(("xl", "z", "y"), ("xh", "c"), None, None, None),
        check_vma=False,
    )
```

time: 102 us -> 94.4 us (0.925)
  blocking collectives: 0 us -> 17 us
  waiting for transfers between devices: 45.7 us -> 32.5 us
  starting transfers between devices: 33.1 us -> 27.7 us
  Pallas kernels: 6.7 us -> 3.2 us
  other arithmetic: 2.55 us -> 1.22 us
    all_to_all x0 -> x1, blocking collectives: none -> 17 us  [local(): block = lax.all_to_all(formed, ('y', 'xh', 'c'), 0, 0, tiled=True)]
    ppermute x9 -> x3, waiting for transfers between devices: 13.6 us -> 0.01 us  [exchange(): lax.ppermute(pieces[by], axis, xor_pairs(count, by))]
    ppermute x9 -> x3, starting transfers between devices: 11 us -> 3.46 us  [exchange(): lax.ppermute(pieces[by], axis, xor_pairs(count, by))]
    ppermute x13 -> x16, starting transfers between devices: 22.1 us -> 24.3 us  [the longest x8 15.9 us: onward(): return lax.ppermute(piece, 'z', ring_pairs(z_size, by))]
    pallas_call x1, Pallas kernels: 2.55 us -> 0.48 us  [voltages(): pl.pallas_call(voltages_kernel, in_specs=[pl.BlockSpec(memory_space=pltpu...]
    pallas_call x1, Pallas kernels: 4.16 us -> 2.72 us  [spectra(): pl.pallas_call(spectra_kernel, in_specs=[ANY, VMEM, ANY], out_shape=pltpu...]
    another operation x6 -> x0, other arithmetic: 1.26 us -> none  [the longest x2 1.04 us: in_order(): stacked = jnp.stack(received)]
    unnamed x10 -> x6, local copies, waits for them, and re-layouts: 1.67 us -> 2.44 us
  transfers between devices with their start and end apart: 22 -> 19, of which waited for: 13 -> 8; matrix products, arithmetic and copies ran while one was open for 9% -> 10% of each run, Pallas kernels for 4% -> 3%
where the time goes in v3:
time: 94.4 us; the launch traced here: 94 us
  waiting for transfers between devices  32.5 us (34%)
  starting transfers between devices  27.7 us (29%)
  blocking collectives  17 us (18%)
  matrix products  7.61 us (8%)
  local copies, waits for them, and re-layouts  4.3 us (5%)
  Pallas kernels  3.2 us (3%)
  other arithmetic  1.22 us (1%)
    ppermute x8, waiting for transfers between devices, onward(): return lax.ppermute(piece, 'z', ring_pairs(z_size, by))  20.2 us
    all_to_all x1, blocking collectives, local(): block = lax.all_to_all(formed, ('y', 'xh', 'c'), 0, 0, tiled=True)  17 us
    ppermute x8, starting transfers between devices, onward(): return lax.ppermute(piece, 'z', ring_pairs(z_size, by))  15.9 us
    ppermute x8, waiting for transfers between devices, across(): return lax.ppermute(piece, 'xl', ring_pairs(2, 1))  12.3 us
    ppermute x8, starting transfers between devices, across(): return lax.ppermute(piece, 'xl', ring_pairs(2, 1))  8.33 us
    dot_general x16, matrix products, product(): jnp.einsum('rk,pk->rp', lhs, columns, preferred_element_type=jnp.float32)  7.61 us
    ppermute x3, starting transfers between devices, exchange(): lax.ppermute(pieces[by], axis, xor_pairs(count, by))  3.46 us
    pallas_call x1, Pallas kernels, spectra(): pl.pallas_call(spectra_kernel, in_specs=[ANY, VMEM, ANY], out_shape=pltpu...  2.72 us
  transfers between devices with their start and end apart: 19, of which 8 were waited for; matrix products, arithmetic and copies ran while one was open for 10% of the time, Pallas kernels for 3%

profile of v3, /device:TPU:6, one launch (start us, length us, event | category | flops | bytes accessed | tf_op | source)
XLA Modules:
  0.0 94.0 jit_solution(6466382095986310135)
XLA Ops:
  0.0 1.1 %copy.9 = f32[2,64,4,32]{3,2,1,0:T(4,128)S(1)} copy(f32[2,64,4,32]{1,3,2,0:T(8,128)} %param.5) | data formatting | bytes 131072 | tf_op args[1]
  1.4 1.5 %collective-permute-start.1 = (f32[2,16,128]{2,1,0:T(8,128)S(1)}, f32[2,16,128]{2,1,0:T(8,128)S(1)}, u32[]{:S(2)}, u32[]{:S(2)}) collective-permute-start(f32[2,16,128]{2,1,0:T(8,128)S(1)} %get-tuple-element.22), channel_id=1, source_target_pairs={{0,2},{1,3},{2,0},{3,1},{4,6},{5,7},{6,4},{7,5},{8,10},{9,11},{10,... | collective-permute-start | bytes 49160 | tf_op jit(solution)/shard_map/ppermute | solution.py:69
  2.9 1.9 %collective-permute-start.2 = (f32[2,16,128]{2,1,0:T(8,128)S(1)}, f32[2,16,128]{2,1,0:T(8,128)S(1)}, u32[]{:S(2)}, u32[]{:S(2)}) collective-permute-start(f32[2,16,128]{2,1,0:T(8,128)S(1)} %get-tuple-element.21), channel_id=1, source_target_pairs={{0,3},{1,2},{2,1},{3,0},{4,7},{5,6},{6,5},{7,4},{8,11},{9,10},{10,... | collective-permute-start | bytes 49160 | tf_op jit(solution)/shard_map/ppermute | solution.py:69
  5.5 2.7 %spectra.1.spectra_ref = f32[256,1024]{1,0:T(8,128)S(1)} custom-call(bf16[16,11776]{1,0:T(8,128)(2,1)} %samples_any.1, f32[8,512]{1,0:T(8,128)S(1)} %copy-done, bf16[1024,1024]{1,0:T(8,128)(2,1)} %constant.125.clone.table_any), custom_call_target="tpu_custom_call" | custom-call | tf_op jit(solution)/shard_map/spectra/pallas_call | solution.py:109
  8.7 17.0 %all_to_all.5 = bf16[16,16,1024]{2,1,0:T(8,128)(2,1)S(1)} all-to-all(bf16[16,16,1024]{2,1,0:T(8,128)(2,1)S(1)} %bitcast.50), channel_id=1, replica_groups=mesh['xl'=2,'z'=8,'y'=4,'xh'=2,'c'=2] {'y','xh','c'}, dimensions={0} | all-to-all | bytes 1048576 | tf_op jit(solution)/shard_map/all_to_all | solution.py:203
  26.5 1.9 %collective-permute-start.4 = (bf16[256,1024]{1,0:T(8,128)(2,1)S(1)}, bf16[256,1024]{1,0:T(8,128)(2,1)S(1)}, u32[]{:S(2)}, u32[]{:S(2)}) collective-permute-start(bf16[256,1024]{1,0:T(8,128)(2,1)S(1)} %bitcast.52), channel_id=1, source_target_pairs={{0,16},{16,32},{32,48},{48,64},{64,80},{80,96},{96,112},{112,0},{1... | collective-permute-start | bytes 1572872 | tf_op jit(solution)/shard_map/ppermute | solution.py:213
  28.5 4.0 %collective-permute-start.10 = (bf16[256,1024]{1,0:T(8,128)(2,1)S(1)}, bf16[256,1024]{1,0:T(8,128)(2,1)S(1)}, u32[]{:S(2)}, u32[]{:S(2)}) collective-permute-start(bf16[256,1024]{1,0:T(8,128)(2,1)S(1)} %bitcast.54), channel_id=1, source_target_pairs={{0,112},{16,0},{32,16},{48,32},{64,48},{80,64},{96,80},{112,96},{1... | collective-permute-start | bytes 1572872 | tf_op jit(solution)/shard_map/ppermute | solution.py:213
  33.0 6.7 %collective-permute-done.3 = bf16[256,1024]{1,0:T(8,128)(2,1)S(1)} collective-permute-done((bf16[256,1024]{1,0:T(8,128)(2,1)S(1)}, bf16[256,1024]{1,0:T(8,128)(2,1)S(1)}, u32[]{:S(2)}, u32[]{:S(2)}) %collective-permute-start.3) | collective-permute-done | bytes 524320 | tf_op jit(solution)/shard_map/ppermute | solution.py:210
  39.7 4.6 %collective-permute-done.4 = bf16[256,1024]{1,0:T(8,128)(2,1)S(1)} collective-permute-done((bf16[256,1024]{1,0:T(8,128)(2,1)S(1)}, bf16[256,1024]{1,0:T(8,128)(2,1)S(1)}, u32[]{:S(2)}, u32[]{:S(2)}) %collective-permute-start.4) | collective-permute-done | bytes 524320 | tf_op jit(solution)/shard_map/ppermute | solution.py:213
  44.8 1.3 %collective-permute-start.7 = (bf16[512,256]{1,0:T(8,128)(2,1)S(1)}, bf16[512,256]{1,0:T(8,128)(2,1)S(1)}, u32[]{:S(2)}, u32[]{:S(2)}) collective-permute-start(bf16[512,256]{1,0:T(8,128)(2,1)S(1)} %fusion.2), channel_id=1, source_target_pairs={{0,128},{128,0},{1,129},{129,1},{2,130},{130,2},{3,131},{131,3},{4... | collective-permute-start | bytes 786440 | tf_op jit(solution)/shard_map/ppermute | solution.py:210
  47.0 3.3 %collective-permute-start.11 = (bf16[256,1024]{1,0:T(8,128)(2,1)S(1)}, bf16[256,1024]{1,0:T(8,128)(2,1)S(1)}, u32[]{:S(2)}, u32[]{:S(2)}) collective-permute-start(bf16[256,1024]{1,0:T(8,128)(2,1)S(1)} %collective-permute-done.10), channel_id=1, source_target_pairs={{0,112},{16,0},{32,16},{48,32},{64,48},{80,64},{96,80},{112,96},{1... | collective-permute-start | bytes 1572872 | tf_op jit(solution)/shard_map/ppermute | solution.py:213
  51.3 0.9 collective-permute-start.15
  52.2 7.9 %collective-permute-done.5 = bf16[256,1024]{1,0:T(8,128)(2,1)S(1)} collective-permute-done((bf16[256,1024]{1,0:T(8,128)(2,1)S(1)}, bf16[256,1024]{1,0:T(8,128)(2,1)S(1)}, u32[]{:S(2)}, u32[]{:S(2)}) %collective-permute-start.5) | collective-permute-done | bytes 524320 | tf_op jit(solution)/shard_map/ppermute | solution.py:213
  60.6 0.9 collective-permute-start.8
  62.5 3.3 %collective-permute-start.12 = (bf16[256,1024]{1,0:T(8,128)(2,1)S(1)}, bf16[256,1024]{1,0:T(8,128)(2,1)S(1)}, u32[]{:S(2)}, u32[]{:S(2)}) collective-permute-start(bf16[256,1024]{1,0:T(8,128)(2,1)S(1)} %collective-permute-done.11), channel_id=1, source_target_pairs={{0,112},{16,0},{32,16},{48,32},{64,48},{80,64},{96,80},{112,96},{1... | collective-permute-start | bytes 1572872 | tf_op jit(solution)/shard_map/ppermute | solution.py:213
  66.3 1.3 %collective-permute-start.16 = (bf16[512,256]{1,0:T(8,128)(2,1)S(1)}, bf16[512,256]{1,0:T(8,128)(2,1)S(1)}, u32[]{:S(2)}, u32[]{:S(2)}) collective-permute-start(bf16[512,256]{1,0:T(8,128)(2,1)S(1)} %fusion.4), channel_id=1, source_target_pairs={{0,128},{128,0},{1,129},{129,1},{2,130},{130,2},{3,131},{131,3},{4... | collective-permute-start | bytes 786440 | tf_op jit(solution)/shard_map/ppermute | solution.py:210
  67.6 6.8 %collective-permute-done.6 = bf16[256,1024]{1,0:T(8,128)(2,1)S(1)} collective-permute-done((bf16[256,1024]{1,0:T(8,128)(2,1)S(1)}, bf16[256,1024]{1,0:T(8,128)(2,1)S(1)}, u32[]{:S(2)}, u32[]{:S(2)}) %collective-permute-start.6) | collective-permute-done | bytes 524320 | tf_op jit(solution)/shard_map/ppermute | solution.py:213
  74.8 1.3 %collective-permute-start.9 = (bf16[512,256]{1,0:T(8,128)(2,1)S(1)}, bf16[512,256]{1,0:T(8,128)(2,1)S(1)}, u32[]{:S(2)}, u32[]{:S(2)}) collective-permute-start(bf16[512,256]{1,0:T(8,128)(2,1)S(1)} %fusion), channel_id=1, source_target_pairs={{0,128},{128,0},{1,129},{129,1},{2,130},{130,2},{3,131},{131,3},{4... | collective-permute-start | bytes 786440 | tf_op jit(solution)/shard_map/ppermute | solution.py:210
  76.8 3.3 %collective-permute-start.14 = (bf16[128,1024]{1,0:T(8,128)(2,1)S(1)}, bf16[128,1024]{1,0:T(8,128)(2,1)S(1)}, u32[]{:S(2)}, u32[]{:S(2)}) collective-permute-start(bf16[128,1024]{1,0:T(8,128)(2,1)S(1)} %slice.29), channel_id=1, source_target_pairs={{0,112},{16,0},{32,16},{48,32},{64,48},{80,64},{96,80},{112,96},{1... | collective-permute-start | bytes 786440 | tf_op jit(solution)/shard_map/ppermute | solution.py:213
  81.9 1.4 %collective-permute-done.9 = bf16[512,256]{1,0:T(8,128)(2,1)S(1)} collective-permute-done((bf16[512,256]{1,0:T(8,128)(2,1)S(1)}, bf16[512,256]{1,0:T(8,128)(2,1)S(1)}, u32[]{:S(2)}, u32[]{:S(2)}) %collective-permute-start.9) | collective-permute-done | bytes 262176 | tf_op jit(solution)/shard_map/ppermute | solution.py:210
  83.4 0.9 collective-permute-done.13
  86.2 1.0 %broadcast_in_dim.50 = f32[1,1,2,256,4096]{4,3,2,1,0:T(8,128)S(1)} broadcast(f32[]{:T(128)} %constant.108.clone.1), dimensions={} | broadcast | bytes 8388612 | tf_op jit(solution)/shard_map/broadcast_in_dim | solution.py:272
  88.3 1.5 %collective-permute-done.17 = bf16[512,256]{1,0:T(8,128)(2,1)S(1)} collective-permute-done((bf16[512,256]{1,0:T(8,128)(2,1)S(1)}, bf16[512,256]{1,0:T(8,128)(2,1)S(1)}, u32[]{:S(2)}, u32[]{:S(2)}) %collective-permute-start.17) | collective-permute-done | bytes 262176 | tf_op jit(solution)/shard_map/ppermute | solution.py:210
  89.8 2.7 %collective-permute-done.18 = bf16[512,256]{1,0:T(8,128)(2,1)S(1)} collective-permute-done((bf16[512,256]{1,0:T(8,128)(2,1)S(1)}, bf16[512,256]{1,0:T(8,128)(2,1)S(1)}, u32[]{:S(2)}, u32[]{:S(2)}) %collective-permute-start.18) | collective-permute-done | bytes 262176 | tf_op jit(solution)/shard_map/ppermute | solution.py:210
  (63 shorter events, 14.4 us)
Async XLA Ops:
  1.3 6.9 %collective-permute-start = (f32[2,16,128]{2,1,0:T(8,128)S(1)}, f32[2,16,128]{2,1,0:T(8,128)S(1)}, u32[]{:S(2)}, u32[]{:S(2)}) collective-permute-start(f32[2,16,128]{2,1,0:T(8,128)S(1)} %get-tuple-element.23), channel_id=1, source_target_pairs={{0,1},{1,0},{2,3},{3,2},{4,5},{5,4},{6,7},{7,6},{8,9},{9,8},{10,11... | collective-permute-start | bytes 49160 | tf_op jit(solution)/shard_map/ppermute | solution.py:69
  1.4 6.8 %collective-permute-start.1 = (f32[2,16,128]{2,1,0:T(8,128)S(1)}, f32[2,16,128]{2,1,0:T(8,128)S(1)}, u32[]{:S(2)}, u32[]{:S(2)}) collective-permute-start(f32[2,16,128]{2,1,0:T(8,128)S(1)} %get-tuple-element.22), channel_id=1, source_target_pairs={{0,2},{1,3},{2,0},{3,1},{4,6},{5,7},{6,4},{7,5},{8,10},{9,11},{10,... | collective-permute-start | bytes 49160 | tf_op jit(solution)/shard_map/ppermute | solution.py:69
  2.9 5.3 %collective-permute-start.2 = (f32[2,16,128]{2,1,0:T(8,128)S(1)}, f32[2,16,128]{2,1,0:T(8,128)S(1)}, u32[]{:S(2)}, u32[]{:S(2)}) collective-permute-start(f32[2,16,128]{2,1,0:T(8,128)S(1)} %get-tuple-element.21), channel_id=1, source_target_pairs={{0,3},{1,2},{2,1},{3,0},{4,7},{5,6},{6,5},{7,4},{8,11},{9,10},{10,... | collective-permute-start | bytes 49160 | tf_op jit(solution)/shard_map/ppermute | solution.py:69
  4.7 0.7 copy-start
  25.7 13.9 %collective-permute-start.3 = (bf16[256,1024]{1,0:T(8,128)(2,1)S(1)}, bf16[256,1024]{1,0:T(8,128)(2,1)S(1)}, u32[]{:S(2)}, u32[]{:S(2)}) collective-permute-start(bf16[256,1024]{1,0:T(8,128)(2,1)S(1)} %bitcast.51), channel_id=1, source_target_pairs={{0,128},{128,0},{1,129},{129,1},{2,130},{130,2},{3,131},{131,3},{4... | collective-permute-start | bytes 1572872 | tf_op jit(solution)/shard_map/ppermute | solution.py:210
  26.5 17.8 %collective-permute-start.4 = (bf16[256,1024]{1,0:T(8,128)(2,1)S(1)}, bf16[256,1024]{1,0:T(8,128)(2,1)S(1)}, u32[]{:S(2)}, u32[]{:S(2)}) collective-permute-start(bf16[256,1024]{1,0:T(8,128)(2,1)S(1)} %bitcast.52), channel_id=1, source_target_pairs={{0,16},{16,32},{32,48},{48,64},{64,80},{80,96},{96,112},{112,0},{1... | collective-permute-start | bytes 1572872 | tf_op jit(solution)/shard_map/ppermute | solution.py:213
  28.5 18.6 %collective-permute-start.10 = (bf16[256,1024]{1,0:T(8,128)(2,1)S(1)}, bf16[256,1024]{1,0:T(8,128)(2,1)S(1)}, u32[]{:S(2)}, u32[]{:S(2)}) collective-permute-start(bf16[256,1024]{1,0:T(8,128)(2,1)S(1)} %bitcast.54), channel_id=1, source_target_pairs={{0,112},{16,0},{32,16},{48,32},{64,48},{80,64},{96,80},{112,96},{1... | collective-permute-start | bytes 1572872 | tf_op jit(solution)/shard_map/ppermute | solution.py:213
  44.8 15.8 %collective-permute-start.7 = (bf16[512,256]{1,0:T(8,128)(2,1)S(1)}, bf16[512,256]{1,0:T(8,128)(2,1)S(1)}, u32[]{:S(2)}, u32[]{:S(2)}) collective-permute-start(bf16[512,256]{1,0:T(8,128)(2,1)S(1)} %fusion.2), channel_id=1, source_target_pairs={{0,128},{128,0},{1,129},{129,1},{2,130},{130,2},{3,131},{131,3},{4... | collective-permute-start | bytes 786440 | tf_op jit(solution)/shard_map/ppermute | solution.py:210
  46.1 14.0 %collective-permute-start.5 = (bf16[256,1024]{1,0:T(8,128)(2,1)S(1)}, bf16[256,1024]{1,0:T(8,128)(2,1)S(1)}, u32[]{:S(2)}, u32[]{:S(2)}) collective-permute-start(bf16[256,1024]{1,0:T(8,128)(2,1)S(1)} %collective-permute-done.4), channel_id=1, source_target_pairs={{0,16},{16,32},{32,48},{48,64},{64,80},{80,96},{96,112},{112,0},{1... | collective-permute-start | bytes 1572872 | tf_op jit(solution)/shard_map/ppermute | solution.py:213
  47.0 15.0 %collective-permute-start.11 = (bf16[256,1024]{1,0:T(8,128)(2,1)S(1)}, bf16[256,1024]{1,0:T(8,128)(2,1)S(1)}, u32[]{:S(2)}, u32[]{:S(2)}) collective-permute-start(bf16[256,1024]{1,0:T(8,128)(2,1)S(1)} %collective-permute-done.10), channel_id=1, source_target_pairs={{0,112},{16,0},{32,16},{48,32},{64,48},{80,64},{96,80},{112,96},{1... | collective-permute-start | bytes 1572872 | tf_op jit(solution)/shard_map/ppermute | solution.py:213
  51.3 15.0 %collective-permute-start.15 = (bf16[512,256]{1,0:T(8,128)(2,1)S(1)}, bf16[512,256]{1,0:T(8,128)(2,1)S(1)}, u32[]{:S(2)}, u32[]{:S(2)}) collective-permute-start(bf16[512,256]{1,0:T(8,128)(2,1)S(1)} %fusion.3), channel_id=1, source_target_pairs={{0,128},{128,0},{1,129},{129,1},{2,130},{130,2},{3,131},{131,3},{4... | collective-permute-start | bytes 786440 | tf_op jit(solution)/shard_map/ppermute | solution.py:210
  60.6 14.2 %collective-permute-start.8 = (bf16[512,256]{1,0:T(8,128)(2,1)S(1)}, bf16[512,256]{1,0:T(8,128)(2,1)S(1)}, u32[]{:S(2)}, u32[]{:S(2)}) collective-permute-start(bf16[512,256]{1,0:T(8,128)(2,1)S(1)} %fusion.1), channel_id=1, source_target_pairs={{0,128},{128,0},{1,129},{129,1},{2,130},{130,2},{3,131},{131,3},{4... | collective-permute-start | bytes 786440 | tf_op jit(solution)/shard_map/ppermute | solution.py:210
  61.5 12.8 %collective-permute-start.6 = (bf16[256,1024]{1,0:T(8,128)(2,1)S(1)}, bf16[256,1024]{1,0:T(8,128)(2,1)S(1)}, u32[]{:S(2)}, u32[]{:S(2)}) collective-permute-start(bf16[256,1024]{1,0:T(8,128)(2,1)S(1)} %collective-permute-done.5), channel_id=1, source_target_pairs={{0,16},{16,32},{32,48},{48,64},{64,80},{80,96},{96,112},{112,0},{1... | collective-permute-start | bytes 1572872 | tf_op jit(solution)/shard_map/ppermute | solution.py:213
  62.5 14.2 %collective-permute-start.12 = (bf16[256,1024]{1,0:T(8,128)(2,1)S(1)}, bf16[256,1024]{1,0:T(8,128)(2,1)S(1)}, u32[]{:S(2)}, u32[]{:S(2)}) collective-permute-start(bf16[256,1024]{1,0:T(8,128)(2,1)S(1)} %collective-permute-done.11), channel_id=1, source_target_pairs={{0,112},{16,0},{32,16},{48,32},{64,48},{80,64},{96,80},{112,96},{1... | collective-permute-start | bytes 1572872 | tf_op jit(solution)/shard_map/ppermute | solution.py:213
  66.3 14.2 %collective-permute-start.16 = (bf16[512,256]{1,0:T(8,128)(2,1)S(1)}, bf16[512,256]{1,0:T(8,128)(2,1)S(1)}, u32[]{:S(2)}, u32[]{:S(2)}) collective-permute-start(bf16[512,256]{1,0:T(8,128)(2,1)S(1)} %fusion.4), channel_id=1, source_target_pairs={{0,128},{128,0},{1,129},{129,1},{2,130},{130,2},{3,131},{131,3},{4... | collective-permute-start | bytes 786440 | tf_op jit(solution)/shard_map/ppermute | solution.py:210
  74.8 8.5 %collective-permute-start.9 = (bf16[512,256]{1,0:T(8,128)(2,1)S(1)}, bf16[512,256]{1,0:T(8,128)(2,1)S(1)}, u32[]{:S(2)}, u32[]{:S(2)}) collective-permute-start(bf16[512,256]{1,0:T(8,128)(2,1)S(1)} %fusion), channel_id=1, source_target_pairs={{0,128},{128,0},{1,129},{129,1},{2,130},{130,2},{3,131},{131,3},{4... | collective-permute-start | bytes 786440 | tf_op jit(solution)/shard_map/ppermute | solution.py:210
  76.6 7.7 %collective-permute-start.13 = (bf16[128,1024]{1,0:T(8,128)(2,1)S(1)}, bf16[128,1024]{1,0:T(8,128)(2,1)S(1)}, u32[]{:S(2)}, u32[]{:S(2)}) collective-permute-start(bf16[128,1024]{1,0:T(8,128)(2,1)S(1)} %slice.28), channel_id=1, source_target_pairs={{0,16},{16,32},{32,48},{48,64},{64,80},{80,96},{96,112},{112,0},{1... | collective-permute-start | bytes 786440 | tf_op jit(solution)/shard_map/ppermute | solution.py:213
  76.8 7.6 %collective-permute-start.14 = (bf16[128,1024]{1,0:T(8,128)(2,1)S(1)}, bf16[128,1024]{1,0:T(8,128)(2,1)S(1)}, u32[]{:S(2)}, u32[]{:S(2)}) collective-permute-start(bf16[128,1024]{1,0:T(8,128)(2,1)S(1)} %slice.29), channel_id=1, source_target_pairs={{0,112},{16,0},{32,16},{48,32},{64,48},{80,64},{96,80},{112,96},{1... | collective-permute-start | bytes 786440 | tf_op jit(solution)/shard_map/ppermute | solution.py:213
  80.6 9.2 %collective-permute-start.17 = (bf16[512,256]{1,0:T(8,128)(2,1)S(1)}, bf16[512,256]{1,0:T(8,128)(2,1)S(1)}, u32[]{:S(2)}, u32[]{:S(2)}) collective-permute-start(bf16[512,256]{1,0:T(8,128)(2,1)S(1)} %fusion.5), channel_id=1, source_target_pairs={{0,128},{128,0},{1,129},{129,1},{2,130},{130,2},{3,131},{131,3},{4... | collective-permute-start | bytes 786440 | tf_op jit(solution)/shard_map/ppermute | solution.py:210
  85.3 7.2 %collective-permute-start.18 = (bf16[512,256]{1,0:T(8,128)(2,1)S(1)}, bf16[512,256]{1,0:T(8,128)(2,1)S(1)}, u32[]{:S(2)}, u32[]{:S(2)}) collective-permute-start(bf16[512,256]{1,0:T(8,128)(2,1)S(1)} %fusion.6), channel_id=1, source_target_pairs={{0,128},{128,0},{1,129},{129,1},{2,130},{130,2},{3,131},{131,3},{4... | collective-permute-start | bytes 786440 | tf_op jit(solution)/shard_map/ppermute | solution.py:210
  89.8 3.4 %copy-start.1 = (f32[1,1,2,256,4096]{4,3,2,1,0:T(8,128)}, f32[1,1,2,256,4096]{4,3,2,1,0:T(8,128)S(1)}, u32[]{:S(2)}) copy-start(f32[1,1,2,256,4096]{4,3,2,1,0:T(8,128)S(1)} %convert_dynamic-update-slice_fusion.1) | copy-start | bytes 25165828

commit v4 on v3

--- a/solution.py
+++ b/solution.py
@@ -70,13 +70,16 @@
     ]
 
 
-def spectra_kernel(samples_any, window_ref, table_any, out_ref, samples_ref, table_ref, *more):
-    upper, lower, sems = more
+def spectra_kernel(samples_any, window_any, table_any, out_ref, samples_ref, *more):
+    window_ref, table_ref, upper, lower, sems = more
     samples_copy = pltpu.make_async_copy(samples_any, samples_ref, sems.at[0])
     table_copy = pltpu.make_async_copy(table_any, table_ref, sems.at[1])
+    window_copy = pltpu.make_async_copy(window_any, window_ref, sems.at[2])
     samples_copy.start()
+    window_copy.start()
     table_copy.start()
     samples_copy.wait()
+    window_copy.wait()
     rows = samples_ref.shape[0]
     frames = [
         samples_ref[:, f * FCH : (f + 1) * FCH].astype(jnp.float32)
@@ -108,20 +111,21 @@
     part = pltpu.VMEM((SPEC * rows, FCH), jnp.bfloat16)
     return pl.pallas_call(
         spectra_kernel,
-        in_specs=[ANY, VMEM, ANY],
+        in_specs=[ANY, ANY, ANY],
         out_shape=pltpu.VMEM((SPEC * rows, 2 * FCH), jnp.float32),
         scratch_shapes=[
             pltpu.VMEM(samples.shape, samples.dtype),
+            pltpu.VMEM((TAPS, FCH), jnp.float32),
             pltpu.VMEM(table.shape, table.dtype),
             part,
             part,
-            pltpu.SemaphoreType.DMA((2,)),
+            pltpu.SemaphoreType.DMA((3,)),
         ],
         compiler_params=room(20),
         name="spectra",
     )(
         pltpu.with_memory_space_constraint(samples, pltpu.HBM),
-        jnp.asarray(pfb_window()),
+        pltpu.with_memory_space_constraint(jnp.asarray(pfb_window()), pltpu.HBM),
         pltpu.with_memory_space_constraint(table, pltpu.HBM),
     )
 
@@ -226,13 +230,6 @@
 
     ahead, behind = {1: onward(block, 1)}, {1: onward(block, -1)}
     other = across(block)
-    for step in range(2, z_size // 2):
-        ahead[step] = onward(ahead[step - 1], 1)
-        behind[step] = onward(behind[step - 1], -1)
-    opposite = jnp.concatenate(
-        [onward(ahead[step][:half], 1), onward(behind[step][half:], -1)], axis=0
-    )
-
     own_left = jnp.concatenate([block, turned(block)], axis=0)
     other_left = jnp.concatenate([other, turned(other)], axis=0)
 
@@ -245,17 +242,28 @@
     def own(columns, by, *waits, x=x_place):
         blocks.append((product(own_left, after(columns, *waits)), x, by))
 
+    def move(step, *waits):
+        ahead[step] = onward(after(ahead[step - 1], *waits), 1)
+        behind[step] = onward(after(behind[step - 1], *waits), -1)
+
     own(block, 0)
     given_a1, given_b1 = swap(ahead[1]), swap(behind[1])
+    move(2)
     own(other, 0, x=far)
     own(ahead[1], -1)
     given_a2, given_b2 = swap(ahead[2], given_a1), swap(behind[2], given_b1)
     own(behind[1], 1)
     own(ahead[2], -2)
+    move(3)
     own(behind[2], 2)
     given_a3, given_b3 = swap(ahead[3], given_a2), swap(behind[3], given_b2)
-    own(ahead[3], -3)
-    own(behind[3], 3)
+    own(ahead[3], -3, given_a3)
+    own(behind[3], 3, given_a3)
+    opposite = [
+        onward(ahead[3][:half], 1),
+        onward(behind[3][half:], -1),
+    ]
+    opposite = jnp.concatenate(opposite, axis=0)
     given_4 = swap(opposite, given_a3)
     own(opposite, 4)
     visibility = jnp.zeros((2, height, height * z_size * 2), jnp.float32)

time: 94.4 us -> 91 us (0.964)
  waiting for transfers between devices: 32.5 us -> 30.1 us
  local copies, waits for them, and re-layouts: 4.3 us -> 3.28 us
    ppermute x8, waiting for transfers between devices: 12.3 us -> 5.05 us  [across(): return lax.ppermute(piece, 'xl', ring_pairs(2, 1))]
    ppermute x8, waiting for transfers between devices: 20.2 us -> 25.1 us  [onward(): return lax.ppermute(piece, 'z', ring_pairs(z_size, by))]
    unnamed x6 -> x4, local copies, waits for them, and re-layouts: 2.44 us -> 1.42 us
  transfers between devices with their start and end apart: 19 -> 19, of which waited for: 8 -> 7; matrix products, arithmetic and copies ran while one was open for 10% -> 11% of each run, Pallas kernels for 3% -> 3%
where the time goes in v4:
time: 91 us; the launch traced here: 90.8 us
  waiting for transfers between devices  30.1 us (33%)
  starting transfers between devices  27.9 us (31%)
  blocking collectives  17 us (19%)
  matrix products  7.61 us (8%)
  local copies, waits for them, and re-layouts  3.28 us (4%)
  Pallas kernels  3.22 us (4%)
  other arithmetic  1.23 us (1%)
    ppermute x8, waiting for transfers between devices, onward(): return lax.ppermute(piece, 'z', ring_pairs(z_size, by))  25.1 us
    all_to_all x1, blocking collectives, local(): block = lax.all_to_all(formed, ('y', 'xh', 'c'), 0, 0, tiled=True)  17 us
    ppermute x8, starting transfers between devices, onward(): return lax.ppermute(piece, 'z', ring_pairs(z_size, by))  15.7 us
    ppermute x8, starting transfers between devices, across(): return lax.ppermute(piece, 'xl', ring_pairs(2, 1))  8.71 us
    dot_general x16, matrix products, product(): jnp.einsum('rk,pk->rp', lhs, columns, preferred_element_type=jnp.float32)  7.61 us
    ppermute x8, waiting for transfers between devices, across(): return lax.ppermute(piece, 'xl', ring_pairs(2, 1))  5.05 us
    ppermute x3, starting transfers between devices, exchange(): lax.ppermute(pieces[by], axis, xor_pairs(count, by))  3.46 us
    pallas_call x1, Pallas kernels, spectra(): pl.pallas_call(spectra_kernel, in_specs=[ANY, ANY, ANY], out_shape=pltpu....  2.75 us
  transfers between devices with their start and end apart: 19, of which 7 were waited for; matrix products, arithmetic and copies ran while one was open for 11% of the time, Pallas kernels for 3%

profile of v4, /device:TPU:6, one launch (start us, length us, event | category | flops | bytes accessed | tf_op | source)
XLA Modules:
  0.0 90.8 jit_solution(14966783384462128117)
XLA Ops:
  0.0 1.1 %copy.9 = f32[2,64,4,32]{3,2,1,0:T(4,128)S(1)} copy(f32[2,64,4,32]{1,3,2,0:T(8,128)} %param.5) | data formatting | bytes 131072 | tf_op args[1]
  1.4 1.5 %collective-permute-start.1 = (f32[2,16,128]{2,1,0:T(8,128)S(1)}, f32[2,16,128]{2,1,0:T(8,128)S(1)}, u32[]{:S(2)}, u32[]{:S(2)}) collective-permute-start(f32[2,16,128]{2,1,0:T(8,128)S(1)} %get-tuple-element.26), channel_id=1, source_target_pairs={{0,2},{1,3},{2,0},{3,1},{4,6},{5,7},{6,4},{7,5},{8,10},{9,11},{10,... | collective-permute-start | bytes 49160 | tf_op jit(solution)/shard_map/ppermute | solution.py:69
  2.9 1.9 %collective-permute-start.2 = (f32[2,16,128]{2,1,0:T(8,128)S(1)}, f32[2,16,128]{2,1,0:T(8,128)S(1)}, u32[]{:S(2)}, u32[]{:S(2)}) collective-permute-start(f32[2,16,128]{2,1,0:T(8,128)S(1)} %get-tuple-element.25), channel_id=1, source_target_pairs={{0,3},{1,2},{2,1},{3,0},{4,7},{5,6},{6,5},{7,4},{8,11},{9,10},{10,... | collective-permute-start | bytes 49160 | tf_op jit(solution)/shard_map/ppermute | solution.py:69
  4.7 2.7 %spectra.1.spectra_ref = f32[256,1024]{1,0:T(8,128)S(1)} custom-call(bf16[16,11776]{1,0:T(8,128)(2,1)} %samples_any.1, f32[8,512]{1,0:T(8,128)} %constant.126.clone.window_any, bf16[1024,1024]{1,0:T(8,128)(2,1)} %constant.125.clone.table_any), custom_call_target="tpu_custom_call" | custom-call | tf_op jit(solution)/shard_map/spectra/pallas_call | solution.py:112
  8.0 17.0 %all_to_all.5 = bf16[16,16,1024]{2,1,0:T(8,128)(2,1)S(1)} all-to-all(bf16[16,16,1024]{2,1,0:T(8,128)(2,1)S(1)} %bitcast.50), channel_id=1, replica_groups=mesh['xl'=2,'z'=8,'y'=4,'xh'=2,'c'=2] {'y','xh','c'}, dimensions={0} | all-to-all | bytes 1048576 | tf_op jit(solution)/shard_map/all_to_all | solution.py:207
  25.0 1.9 %collective-permute-start.4 = (bf16[256,1024]{1,0:T(8,128)(2,1)S(1)}, bf16[256,1024]{1,0:T(8,128)(2,1)S(1)}, u32[]{:S(2)}, u32[]{:S(2)}) collective-permute-start(bf16[256,1024]{1,0:T(8,128)(2,1)S(1)} %bitcast.51), channel_id=1, source_target_pairs={{0,16},{16,32},{32,48},{48,64},{64,80},{80,96},{96,112},{112,0},{1... | collective-permute-start | bytes 1572872 | tf_op jit(solution)/shard_map/ppermute | solution.py:217
  26.9 3.9 %collective-permute-start.10 = (bf16[256,1024]{1,0:T(8,128)(2,1)S(1)}, bf16[256,1024]{1,0:T(8,128)(2,1)S(1)}, u32[]{:S(2)}, u32[]{:S(2)}) collective-permute-start(bf16[256,1024]{1,0:T(8,128)(2,1)S(1)} %bitcast.52), channel_id=1, source_target_pairs={{0,112},{16,0},{32,16},{48,32},{64,48},{80,64},{96,80},{112,96},{1... | collective-permute-start | bytes 1572872 | tf_op jit(solution)/shard_map/ppermute | solution.py:217
  32.2 10.9 %collective-permute-done.4 = bf16[256,1024]{1,0:T(8,128)(2,1)S(1)} collective-permute-done((bf16[256,1024]{1,0:T(8,128)(2,1)S(1)}, bf16[256,1024]{1,0:T(8,128)(2,1)S(1)}, u32[]{:S(2)}, u32[]{:S(2)}) %collective-permute-start.4) | collective-permute-done | bytes 524320 | tf_op jit(solution)/shard_map/ppermute | solution.py:217
  43.1 3.2 %collective-permute-start.11 = (bf16[256,1024]{1,0:T(8,128)(2,1)S(1)}, bf16[256,1024]{1,0:T(8,128)(2,1)S(1)}, u32[]{:S(2)}, u32[]{:S(2)}) collective-permute-start(bf16[256,1024]{1,0:T(8,128)(2,1)S(1)} %collective-permute-done.10), channel_id=1, source_target_pairs={{0,112},{16,0},{32,16},{48,32},{64,48},{80,64},{96,80},{112,96},{1... | collective-permute-start | bytes 1572872 | tf_op jit(solution)/shard_map/ppermute | solution.py:217
  47.8 0.9 %collective-permute-start.7 = (bf16[512,256]{1,0:T(8,128)(2,1)S(1)}, bf16[512,256]{1,0:T(8,128)(2,1)S(1)}, u32[]{:S(2)}, u32[]{:S(2)}) collective-permute-start(bf16[512,256]{1,0:T(8,128)(2,1)S(1)} %fusion.2), channel_id=1, source_target_pairs={{0,128},{128,0},{1,129},{129,1},{2,130},{130,2},{3,131},{131,3},{4... | collective-permute-start | bytes 786440 | tf_op jit(solution)/shard_map/ppermute | solution.py:214
  49.7 1.3 %collective-permute-start.15 = (bf16[512,256]{1,0:T(8,128)(2,1)S(1)}, bf16[512,256]{1,0:T(8,128)(2,1)S(1)}, u32[]{:S(2)}, u32[]{:S(2)}) collective-permute-start(bf16[512,256]{1,0:T(8,128)(2,1)S(1)} %fusion.3), channel_id=1, source_target_pairs={{0,128},{128,0},{1,129},{129,1},{2,130},{130,2},{3,131},{131,3},{4... | collective-permute-start | bytes 786440 | tf_op jit(solution)/shard_map/ppermute | solution.py:214
  51.0 6.7 %collective-permute-done.5 = bf16[256,1024]{1,0:T(8,128)(2,1)S(1)} collective-permute-done((bf16[256,1024]{1,0:T(8,128)(2,1)S(1)}, bf16[256,1024]{1,0:T(8,128)(2,1)S(1)}, u32[]{:S(2)}, u32[]{:S(2)}) %collective-permute-start.5) | collective-permute-done | bytes 524320 | tf_op jit(solution)/shard_map/ppermute | solution.py:217
  58.7 0.9 %collective-permute-start.8 = (bf16[512,256]{1,0:T(8,128)(2,1)S(1)}, bf16[512,256]{1,0:T(8,128)(2,1)S(1)}, u32[]{:S(2)}, u32[]{:S(2)}) collective-permute-start(bf16[512,256]{1,0:T(8,128)(2,1)S(1)} %fusion.1), channel_id=1, source_target_pairs={{0,128},{128,0},{1,129},{129,1},{2,130},{130,2},{3,131},{131,3},{4... | collective-permute-start | bytes 786440 | tf_op jit(solution)/shard_map/ppermute | solution.py:214
  59.6 3.2 %collective-permute-start.12 = (bf16[256,1024]{1,0:T(8,128)(2,1)S(1)}, bf16[256,1024]{1,0:T(8,128)(2,1)S(1)}, u32[]{:S(2)}, u32[]{:S(2)}) collective-permute-start(bf16[256,1024]{1,0:T(8,128)(2,1)S(1)} %collective-permute-done.11), channel_id=1, source_target_pairs={{0,112},{16,0},{32,16},{48,32},{64,48},{80,64},{96,80},{112,96},{1... | collective-permute-start | bytes 1572872 | tf_op jit(solution)/shard_map/ppermute | solution.py:217
  63.3 1.3 %collective-permute-start.16 = (bf16[512,256]{1,0:T(8,128)(2,1)S(1)}, bf16[512,256]{1,0:T(8,128)(2,1)S(1)}, u32[]{:S(2)}, u32[]{:S(2)}) collective-permute-start(bf16[512,256]{1,0:T(8,128)(2,1)S(1)} %fusion.4), channel_id=1, source_target_pairs={{0,128},{128,0},{1,129},{129,1},{2,130},{130,2},{3,131},{131,3},{4... | collective-permute-start | bytes 786440 | tf_op jit(solution)/shard_map/ppermute | solution.py:214
  64.6 6.8 %collective-permute-done.6 = bf16[256,1024]{1,0:T(8,128)(2,1)S(1)} collective-permute-done((bf16[256,1024]{1,0:T(8,128)(2,1)S(1)}, bf16[256,1024]{1,0:T(8,128)(2,1)S(1)}, u32[]{:S(2)}, u32[]{:S(2)}) %collective-permute-start.6) | collective-permute-done | bytes 524320 | tf_op jit(solution)/shard_map/ppermute | solution.py:217
  71.9 0.9 %collective-permute-start.9 = (bf16[512,256]{1,0:T(8,128)(2,1)S(1)}, bf16[512,256]{1,0:T(8,128)(2,1)S(1)}, u32[]{:S(2)}, u32[]{:S(2)}) collective-permute-start(bf16[512,256]{1,0:T(8,128)(2,1)S(1)} %fusion), channel_id=1, source_target_pairs={{0,128},{128,0},{1,129},{129,1},{2,130},{130,2},{3,131},{131,3},{4... | collective-permute-start | bytes 786440 | tf_op jit(solution)/shard_map/ppermute | solution.py:214
  73.5 3.3 %collective-permute-start.14 = (bf16[128,1024]{1,0:T(8,128)(2,1)S(1)}, bf16[128,1024]{1,0:T(8,128)(2,1)S(1)}, u32[]{:S(2)}, u32[]{:S(2)}) collective-permute-start(bf16[128,1024]{1,0:T(8,128)(2,1)S(1)} %slice.29), channel_id=1, source_target_pairs={{0,112},{16,0},{32,16},{48,32},{64,48},{80,64},{96,80},{112,96},{1... | collective-permute-start | bytes 786440 | tf_op jit(solution)/shard_map/ppermute | solution.py:217
  77.3 1.3 %collective-permute-start.17 = (bf16[512,256]{1,0:T(8,128)(2,1)S(1)}, bf16[512,256]{1,0:T(8,128)(2,1)S(1)}, u32[]{:S(2)}, u32[]{:S(2)}) collective-permute-start(bf16[512,256]{1,0:T(8,128)(2,1)S(1)} %fusion.5), channel_id=1, source_target_pairs={{0,128},{128,0},{1,129},{129,1},{2,130},{130,2},{3,131},{131,3},{4... | collective-permute-start | bytes 786440 | tf_op jit(solution)/shard_map/ppermute | solution.py:214
  78.5 1.3 %collective-permute-done.9 = bf16[512,256]{1,0:T(8,128)(2,1)S(1)} collective-permute-done((bf16[512,256]{1,0:T(8,128)(2,1)S(1)}, bf16[512,256]{1,0:T(8,128)(2,1)S(1)}, u32[]{:S(2)}, u32[]{:S(2)}) %collective-permute-start.9) | collective-permute-done | bytes 262176 | tf_op jit(solution)/shard_map/ppermute | solution.py:214
  82.5 1.3 %collective-permute-start.18 = (bf16[512,256]{1,0:T(8,128)(2,1)S(1)}, bf16[512,256]{1,0:T(8,128)(2,1)S(1)}, u32[]{:S(2)}, u32[]{:S(2)}) collective-permute-start(bf16[512,256]{1,0:T(8,128)(2,1)S(1)} %fusion.6), channel_id=1, source_target_pairs={{0,128},{128,0},{1,129},{129,1},{2,130},{130,2},{3,131},{131,3},{4... | collective-permute-start | bytes 786440 | tf_op jit(solution)/shard_map/ppermute | solution.py:214
  83.8 1.0 %broadcast_in_dim.50 = f32[1,1,2,256,4096]{4,3,2,1,0:T(8,128)S(1)} broadcast(f32[]{:T(128)} %constant.108.clone.1), dimensions={} | broadcast | bytes 8388612 | tf_op jit(solution)/shard_map/broadcast_in_dim | solution.py:280
  86.6 3.0 %collective-permute-done.18 = bf16[512,256]{1,0:T(8,128)(2,1)S(1)} collective-permute-done((bf16[512,256]{1,0:T(8,128)(2,1)S(1)}, bf16[512,256]{1,0:T(8,128)(2,1)S(1)}, u32[]{:S(2)}, u32[]{:S(2)}) %collective-permute-start.18) | collective-permute-done | bytes 262176 | tf_op jit(solution)/shard_map/ppermute | solution.py:214
  90.0 0.8 convert_dynamic-update-slice_fusion
  (61 shorter events, 12.1 us)
Async XLA Ops:
  1.3 6.2 %collective-permute-start = (f32[2,16,128]{2,1,0:T(8,128)S(1)}, f32[2,16,128]{2,1,0:T(8,128)S(1)}, u32[]{:S(2)}, u32[]{:S(2)}) collective-permute-start(f32[2,16,128]{2,1,0:T(8,128)S(1)} %get-tuple-element.27), channel_id=1, source_target_pairs={{0,1},{1,0},{2,3},{3,2},{4,5},{5,4},{6,7},{7,6},{8,9},{9,8},{10,11... | collective-permute-start | bytes 49160 | tf_op jit(solution)/shard_map/ppermute | solution.py:69
  1.4 6.1 %collective-permute-start.1 = (f32[2,16,128]{2,1,0:T(8,128)S(1)}, f32[2,16,128]{2,1,0:T(8,128)S(1)}, u32[]{:S(2)}, u32[]{:S(2)}) collective-permute-start(f32[2,16,128]{2,1,0:T(8,128)S(1)} %get-tuple-element.26), channel_id=1, source_target_pairs={{0,2},{1,3},{2,0},{3,1},{4,6},{5,7},{6,4},{7,5},{8,10},{9,11},{10,... | collective-permute-start | bytes 49160 | tf_op jit(solution)/shard_map/ppermute | solution.py:69
  2.9 4.7 %collective-permute-start.2 = (f32[2,16,128]{2,1,0:T(8,128)S(1)}, f32[2,16,128]{2,1,0:T(8,128)S(1)}, u32[]{:S(2)}, u32[]{:S(2)}) collective-permute-start(f32[2,16,128]{2,1,0:T(8,128)S(1)} %get-tuple-element.25), channel_id=1, source_target_pairs={{0,3},{1,2},{2,1},{3,0},{4,7},{5,6},{6,5},{7,4},{8,11},{9,10},{10,... | collective-permute-start | bytes 49160 | tf_op jit(solution)/shard_map/ppermute | solution.py:69
  25.0 18.1 %collective-permute-start.4 = (bf16[256,1024]{1,0:T(8,128)(2,1)S(1)}, bf16[256,1024]{1,0:T(8,128)(2,1)S(1)}, u32[]{:S(2)}, u32[]{:S(2)}) collective-permute-start(bf16[256,1024]{1,0:T(8,128)(2,1)S(1)} %bitcast.51), channel_id=1, source_target_pairs={{0,16},{16,32},{32,48},{48,64},{64,80},{80,96},{96,112},{112,0},{1... | collective-permute-start | bytes 1572872 | tf_op jit(solution)/shard_map/ppermute | solution.py:217
  26.9 16.1 %collective-permute-start.10 = (bf16[256,1024]{1,0:T(8,128)(2,1)S(1)}, bf16[256,1024]{1,0:T(8,128)(2,1)S(1)}, u32[]{:S(2)}, u32[]{:S(2)}) collective-permute-start(bf16[256,1024]{1,0:T(8,128)(2,1)S(1)} %bitcast.52), channel_id=1, source_target_pairs={{0,112},{16,0},{32,16},{48,32},{64,48},{80,64},{96,80},{112,96},{1... | collective-permute-start | bytes 1572872 | tf_op jit(solution)/shard_map/ppermute | solution.py:217
  30.9 16.4 %collective-permute-start.3 = (bf16[256,1024]{1,0:T(8,128)(2,1)S(1)}, bf16[256,1024]{1,0:T(8,128)(2,1)S(1)}, u32[]{:S(2)}, u32[]{:S(2)}) collective-permute-start(bf16[256,1024]{1,0:T(8,128)(2,1)S(1)} %bitcast.53), channel_id=1, source_target_pairs={{0,128},{128,0},{1,129},{129,1},{2,130},{130,2},{3,131},{131,3},{4... | collective-permute-start | bytes 1572872 | tf_op jit(solution)/shard_map/ppermute | solution.py:214
  43.1 14.6 %collective-permute-start.5 = (bf16[256,1024]{1,0:T(8,128)(2,1)S(1)}, bf16[256,1024]{1,0:T(8,128)(2,1)S(1)}, u32[]{:S(2)}, u32[]{:S(2)}) collective-permute-start(bf16[256,1024]{1,0:T(8,128)(2,1)S(1)} %collective-permute-done.4), channel_id=1, source_target_pairs={{0,16},{16,32},{32,48},{48,64},{64,80},{80,96},{96,112},{112,0},{1... | collective-permute-start | bytes 1572872 | tf_op jit(solution)/shard_map/ppermute | solution.py:217
  43.1 16.5 %collective-permute-start.11 = (bf16[256,1024]{1,0:T(8,128)(2,1)S(1)}, bf16[256,1024]{1,0:T(8,128)(2,1)S(1)}, u32[]{:S(2)}, u32[]{:S(2)}) collective-permute-start(bf16[256,1024]{1,0:T(8,128)(2,1)S(1)} %collective-permute-done.10), channel_id=1, source_target_pairs={{0,112},{16,0},{32,16},{48,32},{64,48},{80,64},{96,80},{112,96},{1... | collective-permute-start | bytes 1572872 | tf_op jit(solution)/shard_map/ppermute | solution.py:217
  47.8 10.9 %collective-permute-start.7 = (bf16[512,256]{1,0:T(8,128)(2,1)S(1)}, bf16[512,256]{1,0:T(8,128)(2,1)S(1)}, u32[]{:S(2)}, u32[]{:S(2)}) collective-permute-start(bf16[512,256]{1,0:T(8,128)(2,1)S(1)} %fusion.2), channel_id=1, source_target_pairs={{0,128},{128,0},{1,129},{129,1},{2,130},{130,2},{3,131},{131,3},{4... | collective-permute-start | bytes 786440 | tf_op jit(solution)/shard_map/ppermute | solution.py:214
  49.7 13.6 %collective-permute-start.15 = (bf16[512,256]{1,0:T(8,128)(2,1)S(1)}, bf16[512,256]{1,0:T(8,128)(2,1)S(1)}, u32[]{:S(2)}, u32[]{:S(2)}) collective-permute-start(bf16[512,256]{1,0:T(8,128)(2,1)S(1)} %fusion.3), channel_id=1, source_target_pairs={{0,128},{128,0},{1,129},{129,1},{2,130},{130,2},{3,131},{131,3},{4... | collective-permute-start | bytes 786440 | tf_op jit(solution)/shard_map/ppermute | solution.py:214
  57.7 13.7 %collective-permute-start.6 = (bf16[256,1024]{1,0:T(8,128)(2,1)S(1)}, bf16[256,1024]{1,0:T(8,128)(2,1)S(1)}, u32[]{:S(2)}, u32[]{:S(2)}) collective-permute-start(bf16[256,1024]{1,0:T(8,128)(2,1)S(1)} %collective-permute-done.5), channel_id=1, source_target_pairs={{0,16},{16,32},{32,48},{48,64},{64,80},{80,96},{96,112},{112,0},{1... | collective-permute-start | bytes 1572872 | tf_op jit(solution)/shard_map/ppermute | solution.py:217
  58.7 13.2 %collective-permute-start.8 = (bf16[512,256]{1,0:T(8,128)(2,1)S(1)}, bf16[512,256]{1,0:T(8,128)(2,1)S(1)}, u32[]{:S(2)}, u32[]{:S(2)}) collective-permute-start(bf16[512,256]{1,0:T(8,128)(2,1)S(1)} %fusion.1), channel_id=1, source_target_pairs={{0,128},{128,0},{1,129},{129,1},{2,130},{130,2},{3,131},{131,3},{4... | collective-permute-start | bytes 786440 | tf_op jit(solution)/shard_map/ppermute | solution.py:214
  59.6 13.8 %collective-permute-start.12 = (bf16[256,1024]{1,0:T(8,128)(2,1)S(1)}, bf16[256,1024]{1,0:T(8,128)(2,1)S(1)}, u32[]{:S(2)}, u32[]{:S(2)}) collective-permute-start(bf16[256,1024]{1,0:T(8,128)(2,1)S(1)} %collective-permute-done.11), channel_id=1, source_target_pairs={{0,112},{16,0},{32,16},{48,32},{64,48},{80,64},{96,80},{112,96},{1... | collective-permute-start | bytes 1572872 | tf_op jit(solution)/shard_map/ppermute | solution.py:217
  63.3 13.9 %collective-permute-start.16 = (bf16[512,256]{1,0:T(8,128)(2,1)S(1)}, bf16[512,256]{1,0:T(8,128)(2,1)S(1)}, u32[]{:S(2)}, u32[]{:S(2)}) collective-permute-start(bf16[512,256]{1,0:T(8,128)(2,1)S(1)} %fusion.4), channel_id=1, source_target_pairs={{0,128},{128,0},{1,129},{129,1},{2,130},{130,2},{3,131},{131,3},{4... | collective-permute-start | bytes 786440 | tf_op jit(solution)/shard_map/ppermute | solution.py:214
  71.9 7.9 %collective-permute-start.9 = (bf16[512,256]{1,0:T(8,128)(2,1)S(1)}, bf16[512,256]{1,0:T(8,128)(2,1)S(1)}, u32[]{:S(2)}, u32[]{:S(2)}) collective-permute-start(bf16[512,256]{1,0:T(8,128)(2,1)S(1)} %fusion), channel_id=1, source_target_pairs={{0,128},{128,0},{1,129},{129,1},{2,130},{130,2},{3,131},{131,3},{4... | collective-permute-start | bytes 786440 | tf_op jit(solution)/shard_map/ppermute | solution.py:214
  73.3 7.7 %collective-permute-start.13 = (bf16[128,1024]{1,0:T(8,128)(2,1)S(1)}, bf16[128,1024]{1,0:T(8,128)(2,1)S(1)}, u32[]{:S(2)}, u32[]{:S(2)}) collective-permute-start(bf16[128,1024]{1,0:T(8,128)(2,1)S(1)} %slice.28), channel_id=1, source_target_pairs={{0,16},{16,32},{32,48},{48,64},{64,80},{80,96},{96,112},{112,0},{1... | collective-permute-start | bytes 786440 | tf_op jit(solution)/shard_map/ppermute | solution.py:217
  73.5 8.0 %collective-permute-start.14 = (bf16[128,1024]{1,0:T(8,128)(2,1)S(1)}, bf16[128,1024]{1,0:T(8,128)(2,1)S(1)}, u32[]{:S(2)}, u32[]{:S(2)}) collective-permute-start(bf16[128,1024]{1,0:T(8,128)(2,1)S(1)} %slice.29), channel_id=1, source_target_pairs={{0,112},{16,0},{32,16},{48,32},{64,48},{80,64},{96,80},{112,96},{1... | collective-permute-start | bytes 786440 | tf_op jit(solution)/shard_map/ppermute | solution.py:217
  77.3 9.3 %collective-permute-start.17 = (bf16[512,256]{1,0:T(8,128)(2,1)S(1)}, bf16[512,256]{1,0:T(8,128)(2,1)S(1)}, u32[]{:S(2)}, u32[]{:S(2)}) collective-permute-start(bf16[512,256]{1,0:T(8,128)(2,1)S(1)} %fusion.5), channel_id=1, source_target_pairs={{0,128},{128,0},{1,129},{129,1},{2,130},{130,2},{3,131},{131,3},{4... | collective-permute-start | bytes 786440 | tf_op jit(solution)/shard_map/ppermute | solution.py:214
  82.5 7.1 %collective-permute-start.18 = (bf16[512,256]{1,0:T(8,128)(2,1)S(1)}, bf16[512,256]{1,0:T(8,128)(2,1)S(1)}, u32[]{:S(2)}, u32[]{:S(2)}) collective-permute-start(bf16[512,256]{1,0:T(8,128)(2,1)S(1)} %fusion.6), channel_id=1, source_target_pairs={{0,128},{128,0},{1,129},{129,1},{2,130},{130,2},{3,131},{131,3},{4... | collective-permute-start | bytes 786440 | tf_op jit(solution)/shard_map/ppermute | solution.py:214
  86.6 3.4 %copy-start = (f32[1,1,2,256,4096]{4,3,2,1,0:T(8,128)}, f32[1,1,2,256,4096]{4,3,2,1,0:T(8,128)S(1)}, u32[]{:S(2)}) copy-start(f32[1,1,2,256,4096]{4,3,2,1,0:T(8,128)S(1)} %convert_dynamic-update-slice_fusion.1) | copy-start | bytes 25165828

commit v5 on v4

--- a/solution.py
+++ b/solution.py
@@ -256,7 +256,7 @@
     own(ahead[2], -2)
     move(3)
     own(behind[2], 2)
-    given_a3, given_b3 = swap(ahead[3], given_a2), swap(behind[3], given_b2)
+    given_a3, given_b3 = swap(after(ahead[3], given_a2)), swap(after(behind[3], given_b2))
     own(ahead[3], -3, given_a3)
     own(behind[3], 3, given_a3)
     opposite = [
@@ -264,8 +264,9 @@
         onward(behind[3][half:], -1),
     ]
     opposite = jnp.concatenate(opposite, axis=0)
-    given_4 = swap(opposite, given_a3)
-    own(opposite, 4)
+    made = product(other_left, opposite).astype(jnp.bfloat16)
+    given_4 = across(after(made, given_a3))
+    own(opposite, 4, made)
     visibility = jnp.zeros((2, height, height * z_size * 2), jnp.float32)
     blocks[0] = (after(blocks[0][0], given_a3), *blocks[0][1:])
     for values, x, by in blocks:

time: 91 us -> 90.9 us (level)
    ppermute x8, waiting for transfers between devices: 25.1 us -> 22 us  [onward(): return lax.ppermute(piece, 'z', ring_pairs(z_size, by))]
    ppermute x8, waiting for transfers between devices: 5.05 us -> 7.89 us  [across(): return lax.ppermute(piece, 'xl', ring_pairs(2, 1))]
  transfers between devices with their start and end apart: 19 -> 19, of which waited for: 7 -> 8; matrix products, arithmetic and copies ran while one was open for 11% -> 11% of each run, Pallas kernels for 3% -> 3%
where the time goes in v5:
time: 90.9 us; the launch traced here: 90.8 us
  waiting for transfers between devices  29.9 us (33%)
  starting transfers between devices  28.1 us (31%)
  blocking collectives  17 us (19%)
  matrix products  7.61 us (8%)
  local copies, waits for them, and re-layouts  3.28 us (4%)
  Pallas kernels  3.22 us (4%)
  other arithmetic  1.23 us (1%)
    ppermute x8, waiting for transfers between devices, onward(): return lax.ppermute(piece, 'z', ring_pairs(z_size, by))  22 us
    all_to_all x1, blocking collectives, local(): block = lax.all_to_all(formed, ('y', 'xh', 'c'), 0, 0, tiled=True)  17 us
    ppermute x8, starting transfers between devices, onward(): return lax.ppermute(piece, 'z', ring_pairs(z_size, by))  15.8 us
    ppermute x8, starting transfers between devices, across(): return lax.ppermute(piece, 'xl', ring_pairs(2, 1))  8.9 us
    ppermute x8, waiting for transfers between devices, across(): return lax.ppermute(piece, 'xl', ring_pairs(2, 1))  7.89 us
    dot_general x16, matrix products, product(): jnp.einsum('rk,pk->rp', lhs, columns, preferred_element_type=jnp.float32)  7.61 us
    ppermute x3, starting transfers between devices, exchange(): lax.ppermute(pieces[by], axis, xor_pairs(count, by))  3.46 us
    pallas_call x1, Pallas kernels, spectra(): pl.pallas_call(spectra_kernel, in_specs=[ANY, ANY, ANY], out_shape=pltpu....  2.75 us
  transfers between devices with their start and end apart: 19, of which 8 were waited for; matrix products, arithmetic and copies ran while one was open for 11% of the time, Pallas kernels for 3%

profile of v5, /device:TPU:6, one launch (start us, length us, event | category | flops | bytes accessed | tf_op | source)
XLA Modules:
  0.0 90.8 jit_solution(9463881152290937160)
XLA Ops:
  0.0 1.1 %copy.9 = f32[2,64,4,32]{3,2,1,0:T(4,128)S(1)} copy(f32[2,64,4,32]{1,3,2,0:T(8,128)} %param.5) | data formatting | bytes 131072 | tf_op args[1]
  1.4 1.5 %collective-permute-start.1 = (f32[2,16,128]{2,1,0:T(8,128)S(1)}, f32[2,16,128]{2,1,0:T(8,128)S(1)}, u32[]{:S(2)}, u32[]{:S(2)}) collective-permute-start(f32[2,16,128]{2,1,0:T(8,128)S(1)} %get-tuple-element.28), channel_id=1, source_target_pairs={{0,2},{1,3},{2,0},{3,1},{4,6},{5,7},{6,4},{7,5},{8,10},{9,11},{10,... | collective-permute-start | bytes 49160 | tf_op jit(solution)/shard_map/ppermute | solution.py:69
  2.9 1.9 %collective-permute-start.2 = (f32[2,16,128]{2,1,0:T(8,128)S(1)}, f32[2,16,128]{2,1,0:T(8,128)S(1)}, u32[]{:S(2)}, u32[]{:S(2)}) collective-permute-start(f32[2,16,128]{2,1,0:T(8,128)S(1)} %get-tuple-element.27), channel_id=1, source_target_pairs={{0,3},{1,2},{2,1},{3,0},{4,7},{5,6},{6,5},{7,4},{8,11},{9,10},{10,... | collective-permute-start | bytes 49160 | tf_op jit(solution)/shard_map/ppermute | solution.py:69
  4.7 2.7 %spectra.1.spectra_ref = f32[256,1024]{1,0:T(8,128)S(1)} custom-call(bf16[16,11776]{1,0:T(8,128)(2,1)} %samples_any.1, f32[8,512]{1,0:T(8,128)} %constant.126.clone.window_any, bf16[1024,1024]{1,0:T(8,128)(2,1)} %constant.125.clone.table_any), custom_call_target="tpu_custom_call" | custom-call | tf_op jit(solution)/shard_map/spectra/pallas_call | solution.py:112
  8.0 17.0 %all_to_all.5 = bf16[16,16,1024]{2,1,0:T(8,128)(2,1)S(1)} all-to-all(bf16[16,16,1024]{2,1,0:T(8,128)(2,1)S(1)} %bitcast.50), channel_id=1, replica_groups=mesh['xl'=2,'z'=8,'y'=4,'xh'=2,'c'=2] {'y','xh','c'}, dimensions={0} | all-to-all | bytes 1048576 | tf_op jit(solution)/shard_map/all_to_all | solution.py:207
  25.0 1.9 %collective-permute-start.4 = (bf16[256,1024]{1,0:T(8,128)(2,1)S(1)}, bf16[256,1024]{1,0:T(8,128)(2,1)S(1)}, u32[]{:S(2)}, u32[]{:S(2)}) collective-permute-start(bf16[256,1024]{1,0:T(8,128)(2,1)S(1)} %bitcast.51), channel_id=1, source_target_pairs={{0,16},{16,32},{32,48},{48,64},{64,80},{80,96},{96,112},{112,0},{1... | collective-permute-start | bytes 1572872 | tf_op jit(solution)/shard_map/ppermute | solution.py:217
  26.9 3.9 %collective-permute-start.10 = (bf16[256,1024]{1,0:T(8,128)(2,1)S(1)}, bf16[256,1024]{1,0:T(8,128)(2,1)S(1)}, u32[]{:S(2)}, u32[]{:S(2)}) collective-permute-start(bf16[256,1024]{1,0:T(8,128)(2,1)S(1)} %bitcast.52), channel_id=1, source_target_pairs={{0,112},{16,0},{32,16},{48,32},{64,48},{80,64},{96,80},{112,96},{1... | collective-permute-start | bytes 1572872 | tf_op jit(solution)/shard_map/ppermute | solution.py:217
  32.2 10.9 %collective-permute-done.4 = bf16[256,1024]{1,0:T(8,128)(2,1)S(1)} collective-permute-done((bf16[256,1024]{1,0:T(8,128)(2,1)S(1)}, bf16[256,1024]{1,0:T(8,128)(2,1)S(1)}, u32[]{:S(2)}, u32[]{:S(2)}) %collective-permute-start.4) | collective-permute-done | bytes 524320 | tf_op jit(solution)/shard_map/ppermute | solution.py:217
  43.1 3.2 %collective-permute-start.11 = (bf16[256,1024]{1,0:T(8,128)(2,1)S(1)}, bf16[256,1024]{1,0:T(8,128)(2,1)S(1)}, u32[]{:S(2)}, u32[]{:S(2)}) collective-permute-start(bf16[256,1024]{1,0:T(8,128)(2,1)S(1)} %collective-permute-done.10), channel_id=1, source_target_pairs={{0,112},{16,0},{32,16},{48,32},{64,48},{80,64},{96,80},{112,96},{1... | collective-permute-start | bytes 1572872 | tf_op jit(solution)/shard_map/ppermute | solution.py:217
  47.8 0.9 %collective-permute-start.7 = (bf16[512,256]{1,0:T(8,128)(2,1)S(1)}, bf16[512,256]{1,0:T(8,128)(2,1)S(1)}, u32[]{:S(2)}, u32[]{:S(2)}) collective-permute-start(bf16[512,256]{1,0:T(8,128)(2,1)S(1)} %fusion.1), channel_id=1, source_target_pairs={{0,128},{128,0},{1,129},{129,1},{2,130},{130,2},{3,131},{131,3},{4... | collective-permute-start | bytes 786440 | tf_op jit(solution)/shard_map/ppermute | solution.py:214
  49.7 1.3 %collective-permute-start.15 = (bf16[512,256]{1,0:T(8,128)(2,1)S(1)}, bf16[512,256]{1,0:T(8,128)(2,1)S(1)}, u32[]{:S(2)}, u32[]{:S(2)}) collective-permute-start(bf16[512,256]{1,0:T(8,128)(2,1)S(1)} %fusion.4), channel_id=1, source_target_pairs={{0,128},{128,0},{1,129},{129,1},{2,130},{130,2},{3,131},{131,3},{4... | collective-permute-start | bytes 786440 | tf_op jit(solution)/shard_map/ppermute | solution.py:214
  51.0 6.7 %collective-permute-done.5 = bf16[256,1024]{1,0:T(8,128)(2,1)S(1)} collective-permute-done((bf16[256,1024]{1,0:T(8,128)(2,1)S(1)}, bf16[256,1024]{1,0:T(8,128)(2,1)S(1)}, u32[]{:S(2)}, u32[]{:S(2)}) %collective-permute-start.5) | collective-permute-done | bytes 524320 | tf_op jit(solution)/shard_map/ppermute | solution.py:217
  58.2 1.1 %collective-permute-start.8 = (bf16[512,256]{1,0:T(8,128)(2,1)S(1)}, bf16[512,256]{1,0:T(8,128)(2,1)S(1)}, u32[]{:S(2)}, u32[]{:S(2)}) collective-permute-start(bf16[512,256]{1,0:T(8,128)(2,1)S(1)} %fusion), channel_id=1, source_target_pairs={{0,128},{128,0},{1,129},{129,1},{2,130},{130,2},{3,131},{131,3},{4... | collective-permute-start | bytes 786440 | tf_op jit(solution)/shard_map/ppermute | solution.py:214
  59.8 3.3 %collective-permute-start.12 = (bf16[256,1024]{1,0:T(8,128)(2,1)S(1)}, bf16[256,1024]{1,0:T(8,128)(2,1)S(1)}, u32[]{:S(2)}, u32[]{:S(2)}) collective-permute-start(bf16[256,1024]{1,0:T(8,128)(2,1)S(1)} %collective-permute-done.11), channel_id=1, source_target_pairs={{0,112},{16,0},{32,16},{48,32},{64,48},{80,64},{96,80},{112,96},{1... | collective-permute-start | bytes 1572872 | tf_op jit(solution)/shard_map/ppermute | solution.py:217
  63.6 1.3 %collective-permute-start.16 = (bf16[512,256]{1,0:T(8,128)(2,1)S(1)}, bf16[512,256]{1,0:T(8,128)(2,1)S(1)}, u32[]{:S(2)}, u32[]{:S(2)}) collective-permute-start(bf16[512,256]{1,0:T(8,128)(2,1)S(1)} %fusion.5), channel_id=1, source_target_pairs={{0,128},{128,0},{1,129},{129,1},{2,130},{130,2},{3,131},{131,3},{4... | collective-permute-start | bytes 786440 | tf_op jit(solution)/shard_map/ppermute | solution.py:214
  64.9 2.8 %collective-permute-done.8 = bf16[512,256]{1,0:T(8,128)(2,1)S(1)} collective-permute-done((bf16[512,256]{1,0:T(8,128)(2,1)S(1)}, bf16[512,256]{1,0:T(8,128)(2,1)S(1)}, u32[]{:S(2)}, u32[]{:S(2)}) %collective-permute-start.8) | collective-permute-done | bytes 262176 | tf_op jit(solution)/shard_map/ppermute | solution.py:214
  67.7 3.7 %collective-permute-done.6 = bf16[256,1024]{1,0:T(8,128)(2,1)S(1)} collective-permute-done((bf16[256,1024]{1,0:T(8,128)(2,1)S(1)}, bf16[256,1024]{1,0:T(8,128)(2,1)S(1)}, u32[]{:S(2)}, u32[]{:S(2)}) %collective-permute-start.6) | collective-permute-done | bytes 524320 | tf_op jit(solution)/shard_map/ppermute | solution.py:217
  71.9 0.9 %collective-permute-start.9 = (bf16[512,256]{1,0:T(8,128)(2,1)S(1)}, bf16[512,256]{1,0:T(8,128)(2,1)S(1)}, u32[]{:S(2)}, u32[]{:S(2)}) collective-permute-start(bf16[512,256]{1,0:T(8,128)(2,1)S(1)} %fusion.2), channel_id=1, source_target_pairs={{0,128},{128,0},{1,129},{129,1},{2,130},{130,2},{3,131},{131,3},{4... | collective-permute-start | bytes 786440 | tf_op jit(solution)/shard_map/ppermute | solution.py:214
  73.5 3.3 %collective-permute-start.14 = (bf16[128,1024]{1,0:T(8,128)(2,1)S(1)}, bf16[128,1024]{1,0:T(8,128)(2,1)S(1)}, u32[]{:S(2)}, u32[]{:S(2)}) collective-permute-start(bf16[128,1024]{1,0:T(8,128)(2,1)S(1)} %slice.29), channel_id=1, source_target_pairs={{0,112},{16,0},{32,16},{48,32},{64,48},{80,64},{96,80},{112,96},{1... | collective-permute-start | bytes 786440 | tf_op jit(solution)/shard_map/ppermute | solution.py:217
  77.2 1.3 %collective-permute-start.17 = (bf16[512,256]{1,0:T(8,128)(2,1)S(1)}, bf16[512,256]{1,0:T(8,128)(2,1)S(1)}, u32[]{:S(2)}, u32[]{:S(2)}) collective-permute-start(bf16[512,256]{1,0:T(8,128)(2,1)S(1)} %fusion.6), channel_id=1, source_target_pairs={{0,128},{128,0},{1,129},{129,1},{2,130},{130,2},{3,131},{131,3},{4... | collective-permute-start | bytes 786440 | tf_op jit(solution)/shard_map/ppermute | solution.py:214
  78.5 1.3 %collective-permute-done.9 = bf16[512,256]{1,0:T(8,128)(2,1)S(1)} collective-permute-done((bf16[512,256]{1,0:T(8,128)(2,1)S(1)}, bf16[512,256]{1,0:T(8,128)(2,1)S(1)}, u32[]{:S(2)}, u32[]{:S(2)}) %collective-permute-start.9) | collective-permute-done | bytes 262176 | tf_op jit(solution)/shard_map/ppermute | solution.py:214
  82.5 1.3 %collective-permute-start.18 = (bf16[512,256]{1,0:T(8,128)(2,1)S(1)}, bf16[512,256]{1,0:T(8,128)(2,1)S(1)}, u32[]{:S(2)}, u32[]{:S(2)}) collective-permute-start(bf16[512,256]{1,0:T(8,128)(2,1)S(1)} %fusion.3), channel_id=1, source_target_pairs={{0,128},{128,0},{1,129},{129,1},{2,130},{130,2},{3,131},{131,3},{4... | collective-permute-start | bytes 786440 | tf_op jit(solution)/shard_map/ppermute | solution.py:214
  83.8 1.0 %broadcast_in_dim.50 = f32[1,1,2,256,4096]{4,3,2,1,0:T(8,128)S(1)} broadcast(f32[]{:T(128)} %constant.108.clone.1), dimensions={} | broadcast | bytes 8388612 | tf_op jit(solution)/shard_map/broadcast_in_dim | solution.py:281
  86.6 3.0 %collective-permute-done.18 = bf16[512,256]{1,0:T(8,128)(2,1)S(1)} collective-permute-done((bf16[512,256]{1,0:T(8,128)(2,1)S(1)}, bf16[512,256]{1,0:T(8,128)(2,1)S(1)}, u32[]{:S(2)}, u32[]{:S(2)}) %collective-permute-start.18) | collective-permute-done | bytes 262176 | tf_op jit(solution)/shard_map/ppermute | solution.py:214
  (61 shorter events, 12.9 us)
Async XLA Ops:
  1.3 6.2 %collective-permute-start = (f32[2,16,128]{2,1,0:T(8,128)S(1)}, f32[2,16,128]{2,1,0:T(8,128)S(1)}, u32[]{:S(2)}, u32[]{:S(2)}) collective-permute-start(f32[2,16,128]{2,1,0:T(8,128)S(1)} %get-tuple-element.29), channel_id=1, source_target_pairs={{0,1},{1,0},{2,3},{3,2},{4,5},{5,4},{6,7},{7,6},{8,9},{9,8},{10,11... | collective-permute-start | bytes 49160 | tf_op jit(solution)/shard_map/ppermute | solution.py:69
  1.4 6.1 %collective-permute-start.1 = (f32[2,16,128]{2,1,0:T(8,128)S(1)}, f32[2,16,128]{2,1,0:T(8,128)S(1)}, u32[]{:S(2)}, u32[]{:S(2)}) collective-permute-start(f32[2,16,128]{2,1,0:T(8,128)S(1)} %get-tuple-element.28), channel_id=1, source_target_pairs={{0,2},{1,3},{2,0},{3,1},{4,6},{5,7},{6,4},{7,5},{8,10},{9,11},{10,... | collective-permute-start | bytes 49160 | tf_op jit(solution)/shard_map/ppermute | solution.py:69
  2.9 4.7 %collective-permute-start.2 = (f32[2,16,128]{2,1,0:T(8,128)S(1)}, f32[2,16,128]{2,1,0:T(8,128)S(1)}, u32[]{:S(2)}, u32[]{:S(2)}) collective-permute-start(f32[2,16,128]{2,1,0:T(8,128)S(1)} %get-tuple-element.27), channel_id=1, source_target_pairs={{0,3},{1,2},{2,1},{3,0},{4,7},{5,6},{6,5},{7,4},{8,11},{9,10},{10,... | collective-permute-start | bytes 49160 | tf_op jit(solution)/shard_map/ppermute | solution.py:69
  25.0 18.1 %collective-permute-start.4 = (bf16[256,1024]{1,0:T(8,128)(2,1)S(1)}, bf16[256,1024]{1,0:T(8,128)(2,1)S(1)}, u32[]{:S(2)}, u32[]{:S(2)}) collective-permute-start(bf16[256,1024]{1,0:T(8,128)(2,1)S(1)} %bitcast.51), channel_id=1, source_target_pairs={{0,16},{16,32},{32,48},{48,64},{64,80},{80,96},{96,112},{112,0},{1... | collective-permute-start | bytes 1572872 | tf_op jit(solution)/shard_map/ppermute | solution.py:217
  26.9 16.1 %collective-permute-start.10 = (bf16[256,1024]{1,0:T(8,128)(2,1)S(1)}, bf16[256,1024]{1,0:T(8,128)(2,1)S(1)}, u32[]{:S(2)}, u32[]{:S(2)}) collective-permute-start(bf16[256,1024]{1,0:T(8,128)(2,1)S(1)} %bitcast.52), channel_id=1, source_target_pairs={{0,112},{16,0},{32,16},{48,32},{64,48},{80,64},{96,80},{112,96},{1... | collective-permute-start | bytes 1572872 | tf_op jit(solution)/shard_map/ppermute | solution.py:217
  30.9 16.4 %collective-permute-start.3 = (bf16[256,1024]{1,0:T(8,128)(2,1)S(1)}, bf16[256,1024]{1,0:T(8,128)(2,1)S(1)}, u32[]{:S(2)}, u32[]{:S(2)}) collective-permute-start(bf16[256,1024]{1,0:T(8,128)(2,1)S(1)} %bitcast.53), channel_id=1, source_target_pairs={{0,128},{128,0},{1,129},{129,1},{2,130},{130,2},{3,131},{131,3},{4... | collective-permute-start | bytes 1572872 | tf_op jit(solution)/shard_map/ppermute | solution.py:214
  43.1 14.6 %collective-permute-start.5 = (bf16[256,1024]{1,0:T(8,128)(2,1)S(1)}, bf16[256,1024]{1,0:T(8,128)(2,1)S(1)}, u32[]{:S(2)}, u32[]{:S(2)}) collective-permute-start(bf16[256,1024]{1,0:T(8,128)(2,1)S(1)} %collective-permute-done.4), channel_id=1, source_target_pairs={{0,16},{16,32},{32,48},{48,64},{64,80},{80,96},{96,112},{112,0},{1... | collective-permute-start | bytes 1572872 | tf_op jit(solution)/shard_map/ppermute | solution.py:217
  43.1 16.7 %collective-permute-start.11 = (bf16[256,1024]{1,0:T(8,128)(2,1)S(1)}, bf16[256,1024]{1,0:T(8,128)(2,1)S(1)}, u32[]{:S(2)}, u32[]{:S(2)}) collective-permute-start(bf16[256,1024]{1,0:T(8,128)(2,1)S(1)} %collective-permute-done.10), channel_id=1, source_target_pairs={{0,112},{16,0},{32,16},{48,32},{64,48},{80,64},{96,80},{112,96},{1... | collective-permute-start | bytes 1572872 | tf_op jit(solution)/shard_map/ppermute | solution.py:217
  47.8 10.4 %collective-permute-start.7 = (bf16[512,256]{1,0:T(8,128)(2,1)S(1)}, bf16[512,256]{1,0:T(8,128)(2,1)S(1)}, u32[]{:S(2)}, u32[]{:S(2)}) collective-permute-start(bf16[512,256]{1,0:T(8,128)(2,1)S(1)} %fusion.1), channel_id=1, source_target_pairs={{0,128},{128,0},{1,129},{129,1},{2,130},{130,2},{3,131},{131,3},{4... | collective-permute-start | bytes 786440 | tf_op jit(solution)/shard_map/ppermute | solution.py:214
  49.7 13.9 %collective-permute-start.15 = (bf16[512,256]{1,0:T(8,128)(2,1)S(1)}, bf16[512,256]{1,0:T(8,128)(2,1)S(1)}, u32[]{:S(2)}, u32[]{:S(2)}) collective-permute-start(bf16[512,256]{1,0:T(8,128)(2,1)S(1)} %fusion.4), channel_id=1, source_target_pairs={{0,128},{128,0},{1,129},{129,1},{2,130},{130,2},{3,131},{131,3},{4... | collective-permute-start | bytes 786440 | tf_op jit(solution)/shard_map/ppermute | solution.py:214
  57.7 13.7 %collective-permute-start.6 = (bf16[256,1024]{1,0:T(8,128)(2,1)S(1)}, bf16[256,1024]{1,0:T(8,128)(2,1)S(1)}, u32[]{:S(2)}, u32[]{:S(2)}) collective-permute-start(bf16[256,1024]{1,0:T(8,128)(2,1)S(1)} %collective-permute-done.5), channel_id=1, source_target_pairs={{0,16},{16,32},{32,48},{48,64},{64,80},{80,96},{96,112},{112,0},{1... | collective-permute-start | bytes 1572872 | tf_op jit(solution)/shard_map/ppermute | solution.py:217
  58.2 9.5 %collective-permute-start.8 = (bf16[512,256]{1,0:T(8,128)(2,1)S(1)}, bf16[512,256]{1,0:T(8,128)(2,1)S(1)}, u32[]{:S(2)}, u32[]{:S(2)}) collective-permute-start(bf16[512,256]{1,0:T(8,128)(2,1)S(1)} %fusion), channel_id=1, source_target_pairs={{0,128},{128,0},{1,129},{129,1},{2,130},{130,2},{3,131},{131,3},{4... | collective-permute-start | bytes 786440 | tf_op jit(solution)/shard_map/ppermute | solution.py:214
  59.8 13.7 %collective-permute-start.12 = (bf16[256,1024]{1,0:T(8,128)(2,1)S(1)}, bf16[256,1024]{1,0:T(8,128)(2,1)S(1)}, u32[]{:S(2)}, u32[]{:S(2)}) collective-permute-start(bf16[256,1024]{1,0:T(8,128)(2,1)S(1)} %collective-permute-done.11), channel_id=1, source_target_pairs={{0,112},{16,0},{32,16},{48,32},{64,48},{80,64},{96,80},{112,96},{1... | collective-permute-start | bytes 1572872 | tf_op jit(solution)/shard_map/ppermute | solution.py:217
  63.6 13.2 %collective-permute-start.16 = (bf16[512,256]{1,0:T(8,128)(2,1)S(1)}, bf16[512,256]{1,0:T(8,128)(2,1)S(1)}, u32[]{:S(2)}, u32[]{:S(2)}) collective-permute-start(bf16[512,256]{1,0:T(8,128)(2,1)S(1)} %fusion.5), channel_id=1, source_target_pairs={{0,128},{128,0},{1,129},{129,1},{2,130},{130,2},{3,131},{131,3},{4... | collective-permute-start | bytes 786440 | tf_op jit(solution)/shard_map/ppermute | solution.py:214
  71.9 7.9 %collective-permute-start.9 = (bf16[512,256]{1,0:T(8,128)(2,1)S(1)}, bf16[512,256]{1,0:T(8,128)(2,1)S(1)}, u32[]{:S(2)}, u32[]{:S(2)}) collective-permute-start(bf16[512,256]{1,0:T(8,128)(2,1)S(1)} %fusion.2), channel_id=1, source_target_pairs={{0,128},{128,0},{1,129},{129,1},{2,130},{130,2},{3,131},{131,3},{4... | collective-permute-start | bytes 786440 | tf_op jit(solution)/shard_map/ppermute | solution.py:214
  73.3 7.7 %collective-permute-start.13 = (bf16[128,1024]{1,0:T(8,128)(2,1)S(1)}, bf16[128,1024]{1,0:T(8,128)(2,1)S(1)}, u32[]{:S(2)}, u32[]{:S(2)}) collective-permute-start(bf16[128,1024]{1,0:T(8,128)(2,1)S(1)} %slice.28), channel_id=1, source_target_pairs={{0,16},{16,32},{32,48},{48,64},{64,80},{80,96},{96,112},{112,0},{1... | collective-permute-start | bytes 786440 | tf_op jit(solution)/shard_map/ppermute | solution.py:217
  73.5 8.0 %collective-permute-start.14 = (bf16[128,1024]{1,0:T(8,128)(2,1)S(1)}, bf16[128,1024]{1,0:T(8,128)(2,1)S(1)}, u32[]{:S(2)}, u32[]{:S(2)}) collective-permute-start(bf16[128,1024]{1,0:T(8,128)(2,1)S(1)} %slice.29), channel_id=1, source_target_pairs={{0,112},{16,0},{32,16},{48,32},{64,48},{80,64},{96,80},{112,96},{1... | collective-permute-start | bytes 786440 | tf_op jit(solution)/shard_map/ppermute | solution.py:217
  77.2 9.3 %collective-permute-start.17 = (bf16[512,256]{1,0:T(8,128)(2,1)S(1)}, bf16[512,256]{1,0:T(8,128)(2,1)S(1)}, u32[]{:S(2)}, u32[]{:S(2)}) collective-permute-start(bf16[512,256]{1,0:T(8,128)(2,1)S(1)} %fusion.6), channel_id=1, source_target_pairs={{0,128},{128,0},{1,129},{129,1},{2,130},{130,2},{3,131},{131,3},{4... | collective-permute-start | bytes 786440 | tf_op jit(solution)/shard_map/ppermute | solution.py:214
  82.5 7.1 %collective-permute-start.18 = (bf16[512,256]{1,0:T(8,128)(2,1)S(1)}, bf16[512,256]{1,0:T(8,128)(2,1)S(1)}, u32[]{:S(2)}, u32[]{:S(2)}) collective-permute-start(bf16[512,256]{1,0:T(8,128)(2,1)S(1)} %fusion.3), channel_id=1, source_target_pairs={{0,128},{128,0},{1,129},{129,1},{2,130},{130,2},{3,131},{131,3},{4... | collective-permute-start | bytes 786440 | tf_op jit(solution)/shard_map/ppermute | solution.py:214
  86.6 3.4 %copy-start = (f32[1,1,2,256,4096]{4,3,2,1,0:T(8,128)}, f32[1,1,2,256,4096]{4,3,2,1,0:T(8,128)S(1)}, u32[]{:S(2)}) copy-start(f32[1,1,2,256,4096]{4,3,2,1,0:T(8,128)S(1)} %convert_dynamic-update-slice_fusion.1) | copy-start | bytes 25165828
